TPU v7x, 256 devices: a whole 4x4x8 slice. The times are simulated.
256 devices in a mesh: ctx: 32 (over z, y_lo, core), tp: 8 (over y_hi, x).
Axes of the slice: x: 4, y: 4 (y_hi: 2, y_lo: 2; y = y_hi * 2 + y_lo), z: 8, core: 2. Of those that a mesh axis runs over, the one named last changes fastest.
Arguments:
- hidden: bfloat16 [8192, 8192], P('ctx', 'tp'), may hold values from -6 to 6
- query_weight: bfloat16 [8192, 4096], P('ctx', 'tp')
- keys: bfloat16 [8192, 4096], P('ctx', 'tp'), may hold values from -6 to 6
- values: bfloat16 [8192, 4096], P('ctx', 'tp'), may hold values from -6 to 6
- d_attended: bfloat16 [8192, 4096], P('ctx', 'tp'), may hold values from -6 to 6
Outputs:
- attended: bfloat16 [8192, 4096], P('ctx', 'tp')
- d_hidden: bfloat16 [8192, 8192], P('ctx', 'tp')
- d_query_weight: bfloat16 [8192, 4096], P('ctx', 'tp')
- d_keys: bfloat16 [8192, 4096], P('ctx', 'tp')
- d_values: bfloat16 [8192, 4096], P('ctx', 'tp')
All inputs are finite; a program needn't handle non-finite values.
Results may differ from a plain program's by a relative error of at most 0.03.
Values may be sent and summed in bfloat16 or wider, within the bound.
No kernel may reach another device: no remote copies, remote signals or barrier semaphores. Data moves between devices by JAX's collectives and lax.ppermute only.
A program may use at most 128 MiB of HBM per device.

v0:
```python
import jax
import jax.numpy as jnp
from jax import lax
from jax.experimental import pallas as pl
from jax.experimental.pallas import tpu as pltpu
from jax.sharding import Mesh, PartitionSpec as P

DH = 128
W = 512
SEQ_Z = 4
AXES = ("z", "yl", "co", "yh", "x")
SIZES = (8, 2, 2, 2, 4)
NZ, NX = 8, 4
T = 256
SCALE = 1.0 / DH**0.5
LOG2E = 1.4426950408889634
BF = jnp.bfloat16
F32 = jnp.float32
VMEM = 56 * 1024 * 1024


def route(target):
    pairs = []
    for i in range(256):
        rest, place = i, []
        for size in SIZES[::-1]:
            place.append(rest % size)
            rest //= size
        there = target(*place[::-1])
        j = 0
        for size, c in zip(SIZES, there):
            j = j * size + c % size
        pairs.append((i, j))
    return pairs


def move(block, dz=0, yl=0, co=0, yh=0, dx=0):
    pairs = route(lambda z, a, b, c, x: (z + dz, a ^ yl, b ^ co, c ^ yh, x + dx))
    return lax.ppermute(block, AXES, pairs)


def params():
    return pltpu.CompilerParams(vmem_limit_bytes=VMEM)


def cost(flops, bytes_accessed, exps=0):
    return pl.CostEstimate(flops=flops, bytes_accessed=bytes_accessed, transcendentals=exps)


def mm(a, b, dims):
    return lax.dot_general(a, b, (dims, ((), ())), preferred_element_type=F32)


def feature_block(tokens, i, dl):
    return tokens[i // 2][i % 2, dl]


def query_kernel(place_ref, *refs):
    own, other, w_ref, outs = refs[:4], refs[4:8], refs[8], refs[9:13]
    w = jnp.concatenate([w_ref[place_ref[i]] for i in range(8)], axis=0)
    for dc, tokens in enumerate((own, other)):
        for dl in range(2):
            h = jnp.concatenate([feature_block(tokens, i, dl) for i in range(8)], axis=1)
            part = mm(h, w, ((1,), (0,))).astype(BF)
            row = pl.multiple_of(place_ref[8 + dc * 2 + dl] * T, T)
            for k in range(4):
                outs[k][pl.ds(row, T), :] = part[:, k * DH : (k + 1) * DH]


def in_vmem(kernel, name, work, outs, *args):
    vm = pl.BlockSpec(memory_space=pltpu.VMEM)
    return pl.pallas_call(
        kernel,
        in_specs=[pl.BlockSpec(memory_space=pltpu.SMEM)] + [vm] * (len(args) - 1),
        out_specs=[vm] * len(outs),
        out_shape=[jax.ShapeDtypeStruct(shape, kind) for shape, kind in outs],
        compiler_params=params(),
        cost_estimate=work,
        name=name,
    )(*args)


def query_part(place, own, other, weights):
    work = cost(2 * 1024 * 2048 * 512, 7 << 20)
    outs = [((4 * T, DH), BF)] * 4
    return in_vmem(query_kernel, "query_part", work, outs, place, *own, *other, weights)


def d_hidden_block(place_ref, refs, dl, i):
    row = pl.multiple_of(place_ref[8 + dl] * T, T)
    dq = jnp.concatenate([refs[k][pl.ds(row, T), :] for k in range(4)], axis=1)
    return mm(dq, refs[4][place_ref[i]], ((1,), (1,)))


def d_hidden_away_kernel(place_ref, *refs):
    for dl in range(2):
        for i in range(8):
            refs[5][i, dl] = d_hidden_block(place_ref, refs, dl, i).astype(BF)


def d_hidden_near_kernel(place_ref, *refs):
    for dl in range(2):
        for i in range(8):
            part = d_hidden_block(place_ref, refs, dl, i)
            refs[6 + i // 2][i % 2, dl] = (part + refs[5][i, dl].astype(F32)).astype(BF)


def d_hidden_away(place, dq, weights):
    work = cost(1024 * 2048 * 512, 5 << 20)
    outs = [((8, 2, T, T), BF)]
    return in_vmem(d_hidden_away_kernel, "d_hidden_away", work, outs, place, *dq, weights)[0]


def d_hidden_near(place, dq, weights, away):
    work = cost(1024 * 2048 * 512, 7 << 20)
    outs = [((2, 2, T, T), BF)] * 4
    return in_vmem(d_hidden_near_kernel, "d_hidden_near", work, outs, place, *dq, weights, away)


def d_weight_kernel(place_ref, *refs):
    own, other, dqs, out_ref = refs[:4], refs[4:8], refs[8:12], refs[12]
    dq = jnp.concatenate(
        [
            jnp.concatenate(
                [
                    ref[pl.ds(pl.multiple_of(place_ref[8 + j] * T, T), T), :]
                    for ref in dqs
                ],
                axis=1,
            )
            for j in range(4)
        ],
        axis=0,
    )
    for i in range(8):
        h = jnp.concatenate(
            [feature_block(tokens, i, dl) for tokens in (own, other) for dl in range(2)], axis=0
        )
        out_ref[place_ref[i]] = mm(h, dq, ((0,), (0,))).astype(BF)


def d_weight_part(place, own, other, dq):
    work = cost(2 * 1024 * 2048 * 512, 7 << 20)
    outs = [((NZ, T, 4 * DH), BF)]
    return in_vmem(d_weight_kernel, "d_weight_part", work, outs, place, *own, *other, *dq)[0]


def attended_kernel(place_ref, own_ref, core_ref, y_ref, *outs):
    for k, ref in enumerate((own_ref, core_ref.at[0], y_ref.at[0], core_ref.at[1])):
        at = pl.multiple_of(place_ref[12 + k] * DH, DH)
        for j in range(3):
            outs[j][:, pl.ds(at, DH)] = ref[j]


def last_kernel(place_ref, *refs):
    for k in range(4):
        at = place_ref[16 + k]
        for co in range(2):
            first = pl.multiple_of((at + co * 2) * DH, DH)
            refs[8][:, pl.ds(first, DH)] = refs[k][:, co * DH : (co + 1) * DH]
    for dy in range(2):
        row = pl.multiple_of(place_ref[20 + dy] * DH, DH)
        for dc in range(2):
            for dl in range(2):
                at = pl.multiple_of(place_ref[12 + dl * 2 + dc] * DH, DH)
                refs[9][pl.ds(row, DH), pl.ds(at, DH)] = refs[4 + dy * 2 + dc][
                    :, dl * DH : (dl + 1) * DH
                ]


def attend_kernel(
    place_ref, q0_ref, q1_ref, q2_ref, q3_ref, p0_ref, p1_ref, p2_ref, prev_ref,
    out_ref, dq_ref, dkv_ref, dprev_ref, k_ref, v_ref, g_ref, o_ref, dk_ref, dv_ref,
):
    tokens = [pl.multiple_of(place_ref[12 + k] * T, T) for k in range(4)]
    for half in range(2):
        k_ref[half * T : (half + 1) * T] = prev_ref[half, 0]
        v_ref[half * T : (half + 1) * T] = prev_ref[half, 1]
    for row, ref in zip(tokens, (p0_ref, p1_ref.at[0], p2_ref.at[0], p2_ref.at[1])):
        k_ref[pl.ds(W + row, T), :] = ref[0]
        v_ref[pl.ds(W + row, T), :] = ref[1]
        g_ref[pl.ds(row, T), :] = ref[2]
    dk_ref[...] = jnp.zeros_like(dk_ref)
    dv_ref[...] = jnp.zeros_like(dv_ref)
    inside = place_ref[22] == 0
    rows = lax.broadcasted_iota(jnp.int32, (T, T), 0)
    cols = lax.broadcasted_iota(jnp.int32, (T, T), 1)
    old = cols > rows
    for i in range(4):
        at = slice(i * T, (i + 1) * T)
        window = slice(i * T, i * T + W + T)
        q = (
            q0_ref[at].astype(F32) + q1_ref[at].astype(F32)
            + q2_ref[at].astype(F32) + q3_ref[at].astype(F32)
        ).astype(BF)
        g = g_ref[at]
        k = k_ref[window]
        v = v_ref[window]
        s = mm(q, k, ((1,), (1,)))
        sa, sb, sc = s[:, :T], s[:, T : 2 * T], s[:, 2 * T :]
        if i < 2:
            sa = jnp.where(inside, sa, -1e30)
        if i < 1:
            sb = jnp.where(inside, sb, -1e30)
        sm = jnp.where(old, sa, sc)
        top = jnp.max(jnp.maximum(sm, sb), axis=1, keepdims=True)
        em = jnp.exp2((sm - top) * (SCALE * LOG2E))
        eb = jnp.exp2((sb - top) * (SCALE * LOG2E))
        inv = 1.0 / jnp.sum(em + eb, axis=1, keepdims=True)
        pm = em * inv
        pb = eb * inv
        prob = jnp.concatenate(
            [
                jnp.where(old, pm, 0.0).astype(BF),
                pb.astype(BF),
                jnp.where(old, 0.0, pm).astype(BF),
            ],
            axis=1,
        )
        o_ref[at] = mm(prob, v, ((1,), (0,))).astype(BF)
        dp = mm(g, v, ((1,), (1,)))
        dpm = jnp.where(old, dp[:, :T], dp[:, 2 * T :])
        dpb = dp[:, T : 2 * T]
        delta = jnp.sum(pm * dpm + pb * dpb, axis=1, keepdims=True)
        dsm = pm * (dpm - delta) * SCALE
        dsb = pb * (dpb - delta) * SCALE
        ds = jnp.concatenate(
            [
                jnp.where(old, dsm, 0.0).astype(BF),
                dsb.astype(BF),
                jnp.where(old, 0.0, dsm).astype(BF),
            ],
            axis=1,
        )
        dq_ref[at] = mm(ds, k, ((1,), (0,))).astype(BF)
        dk_ref[window] += mm(ds, q, ((0,), (0,)))
        dv_ref[window] += mm(prob, g, ((0,), (0,)))
    for half in range(2):
        dprev_ref[half, 0] = dk_ref[half * T : (half + 1) * T].astype(BF)
        dprev_ref[half, 1] = dv_ref[half * T : (half + 1) * T].astype(BF)
    for k, row in enumerate(tokens):
        out_ref[k] = o_ref[pl.ds(row, T), :]
        dkv_ref[k, 0] = dk_ref[pl.ds(W + row, T), :]
        dkv_ref[k, 1] = dv_ref[pl.ds(W + row, T), :]


def attend(place, parts, pieces, prev):
    vm = pl.BlockSpec(memory_space=pltpu.VMEM)
    n = 4 * T
    return pl.pallas_call(
        attend_kernel,
        in_specs=[pl.BlockSpec(memory_space=pltpu.SMEM)] + [vm] * 8,
        out_specs=[vm] * 4,
        out_shape=[
            jax.ShapeDtypeStruct((4, T, DH), BF),
            jax.ShapeDtypeStruct((n, DH), BF),
            jax.ShapeDtypeStruct((4, 2, T, DH), F32),
            jax.ShapeDtypeStruct((2, 2, T, DH), BF),
        ],
        scratch_shapes=[
            pltpu.VMEM((W + n, DH), BF),
            pltpu.VMEM((W + n, DH), BF),
            pltpu.VMEM((n, DH), BF),
            pltpu.VMEM((n, DH), BF),
            pltpu.VMEM((W + n, DH), F32),
            pltpu.VMEM((W + n, DH), F32),
        ],
        compiler_params=params(),
        cost_estimate=cost(12 * n * 768 * DH, 5 << 20, n * W),
        name="attend",
    )(place, *parts, *pieces, prev)


def tie(*groups):
    flat = iter(lax.optimization_barrier([a for group in groups for a in group]))
    return [[next(flat) for _ in group] for group in groups]


def per_device(hidden, weight, keys, values, d_attended):
    z, yl, co, yh, x = (lax.axis_index(a) for a in AXES)
    quad = [(a, b) for a in range(2) for b in range(2)]
    blocks = [(yh ^ dy) * NX + (x - dx) % NX for dx in range(NX) for dy in range(2)]
    rows = [(yl ^ dl) * 2 + (co ^ dc) for dc, dl in quad]
    heads = [(yl ^ dl) * 2 + (co ^ dc) for dl, dc in quad]
    lanes = [(yl ^ dl) * 4 + (yh ^ dy) for dy, dl in quad]
    tail = heads + lanes + [yh, 1 - yh, (z % SEQ_Z == 0).astype(jnp.int32)]
    place = jnp.stack(blocks + rows + tail).astype(jnp.int32)
    place_other = jnp.stack(blocks + rows[2:] + rows[:2] + tail).astype(jnp.int32)

    def weight_piece(dc, dy):
        half = lax.dynamic_slice_in_dim(weight, (yh ^ dy) * DH, DH, 0)
        return jnp.concatenate(
            [
                lax.dynamic_slice_in_dim(half, ((yl ^ dl) * 2 + (co ^ dc)) * DH, DH, 1)
                for dl in range(2)
            ],
            axis=1,
        )

    kvd = [
        jnp.stack(
            [lax.dynamic_slice_in_dim(a, heads[k] * DH, DH, 1) for a in (keys, values, d_attended)]
        )
        for k in range(4)
    ]

    sent = [weight_piece(dc, dy) for dc, dy in quad]
    got = [sent[0], move(sent[1], yh=1), move(sent[2], co=1), move(sent[3], co=1, yh=1)]
    mine = jnp.concatenate(got[:2], axis=1)
    theirs = jnp.concatenate(got[2:], axis=1)
    shard = jnp.concatenate(
        [jnp.where(co == 0, mine, theirs), jnp.where(co == 0, theirs, mine)], axis=0
    )

    def hidden_piece(dy, dl):
        part = lax.dynamic_slice_in_dim(hidden, (yl ^ dl) * 2 * T, 2 * T, 1)
        part = part.reshape(T, 2, 2, DH)
        return lax.dynamic_index_in_dim(part, yh ^ dy, 2, keepdims=False).reshape(T, T)

    mixed = [hidden_piece(dy, dl) for dy, dl in quad]
    mixed = [mixed[0]] + [move(mixed[k], yh=quad[k][0], yl=quad[k][1]) for k in (1, 2, 3)]
    mixed = jnp.stack(mixed).reshape(2, 2, T, T)

    own = [move(mixed, dx=dx) if dx else mixed for dx in range(NX)]
    own, kvd = tie(own, kvd)
    other = [move(block, co=1) for block in own]
    swapped = move(jnp.stack([kvd[1], kvd[3]]), co=1)
    pieces = [kvd[0], swapped, move(jnp.stack([kvd[2], swapped[1]]), yl=1)]
    weights = lax.all_gather(shard, "z", axis=0, tiled=False)
    own, other, (weights,) = tie(own, other, (weights,))

    parts = query_part(place, own, other, weights)
    parts, pieces = tie(parts, pieces)
    low = jnp.where(yl == 1, jnp.stack([pieces[0][:2], pieces[1][0, :2]]), pieces[2][:, :2])
    prev = move(jnp.where(co == 0, low, low[::-1]), dz=1)

    parts = [parts[0]] + [move(parts[k], yh=k // 2, yl=k % 2) for k in range(1, 4)]
    attended, dq, dkv, dprev = attend(place, parts, pieces, prev)
    dq = [dq] + [move(dq, yh=k // 2, yl=k % 2) for k in range(1, 4)]

    late = move(dprev, dz=-1)
    dq, (late,) = tie(dq, (late,))
    sums = d_weight_part(place, own, other, dq)
    shard = lax.psum_scatter(sums.reshape(NZ * T, 4 * DH), "z", scatter_dimension=0, tiled=True)
    away = move(d_hidden_away(place_other, dq, weights), co=1)
    near = d_hidden_near(place, dq, weights, away)

    outs = []
    for k, (dl, dc) in enumerate(quad):
        half = lax.dynamic_index_in_dim(late, co ^ dc, 0, keepdims=False).astype(F32)
        grads = dkv[k] + jnp.where((yl ^ dl) == 1, half, 0.0)
        outs.append(jnp.concatenate([attended[k][None], grads.astype(BF)], axis=0))

    crossed = move(jnp.stack(outs[2:]), yl=1)
    outs = [outs[0], move(jnp.stack([outs[1], crossed[1]]), co=1), crossed]
    result = in_vmem(
        attended_kernel, "attended_last", cost(0, 1 << 20), [((T, 4 * DH), BF)] * 3, place, *outs
    )

    line = [near[0]] + [move(near[dx], dx=-dx) for dx in range(1, NX)]
    line, result = tie(line, result)
    line = sum(block.astype(F32) for block in line).astype(BF)
    back = [line[dy, dl] for dy, dl in quad]
    back = [back[0]] + [move(back[k], yh=quad[k][0], yl=quad[k][1]) for k in (1, 2, 3)]
    def weight_back(dc, dy):
        block = lax.dynamic_slice_in_dim(shard, (co ^ dc) * DH, DH, 0)
        block = block[:, dy * T : (dy + 1) * T]
        return move(block, co=dc, yh=dy) if dc or dy else block

    back += [weight_back(dc, dy) for dy, dc in quad]
    d_hidden, d_weight = in_vmem(
        last_kernel, "last", cost(0, 1 << 20), [((T, 8 * DH), BF), ((T, 4 * DH), BF)], place, *back
    )

    return result[0], d_hidden, d_weight, result[1], result[2]


def solution(mesh):
    grid = Mesh(mesh.devices.reshape(SIZES), AXES)
    spec = P(("z", "yl", "co"), ("yh", "x"))
    return jax.shard_map(
        per_device, mesh=grid, in_specs=(spec,) * 5, out_specs=(spec,) * 5, check_vma=False
    )
```

profile of v0, /device:TPU:1, one launch (start us, length us, event | category | flops | bytes accessed | tf_op | source)
XLA Modules:
  0.0 189.5 jit_solution(17164286986793704857)
XLA Ops:
  7.3 1.3 fusion.14
  8.6 4.5 %collective-permute-start.12 = (bf16[128,256]{1,0:T(8,128)(2,1)S(1)}, bf16[128,256]{1,0:T(8,128)(2,1)S(1)}, u32[]{:S(2)}, u32[]{:S(2)}) collective-permute-start(bf16[128,256]{1,0:T(8,128)(2,1)S(1)} %pad_maximum_fusion.14), channel_id=1, source_target_pairs={{0,12},{1,13},{2,14},{3,15},{4,8},{5,9},{6,10},{7,11},{8,4},{9,5},... | collective-permute-start | bytes 196616 | tf_op jit(solution)/shard_map/ppermute | solution.py:39
  13.2 1.8 collective-permute-start.10
  15.0 2.8 %collective-permute-done.10 = bf16[128,256]{1,0:T(8,128)(2,1)S(1)} collective-permute-done((bf16[128,256]{1,0:T(8,128)(2,1)S(1)}, bf16[128,256]{1,0:T(8,128)(2,1)S(1)}, u32[]{:S(2)}, u32[]{:S(2)}) %collective-permute-start.10) | collective-permute-done | bytes 65568 | tf_op jit(solution)/shard_map/ppermute | solution.py:39
  19.2 1.1 collective-permute-start.2
  20.7 2.4 %collective-permute-start.1 = (bf16[256,256]{0,1:T(8,128)(2,1)S(1)}, bf16[256,256]{0,1:T(8,128)(2,1)S(1)}, u32[]{:S(2)}, u32[]{:S(2)}) collective-permute-start(bf16[256,256]{0,1:T(8,128)(2,1)S(1)} %bitcast.98), channel_id=1, source_target_pairs={{0,4},{1,5},{2,6},{3,7},{4,0},{5,1},{6,2},{7,3},{8,12},{9,13},{10,... | collective-permute-start | bytes 393224 | tf_op jit(solution)/shard_map/ppermute | solution.py:39
  23.2 1.1 collective-permute-done.2
  24.3 3.0 %collective-permute-done.1 = bf16[256,256]{0,1:T(8,128)(2,1)S(1)} collective-permute-done((bf16[256,256]{0,1:T(8,128)(2,1)S(1)}, bf16[256,256]{0,1:T(8,128)(2,1)S(1)}, u32[]{:S(2)}, u32[]{:S(2)}) %collective-permute-start.1) | collective-permute-done | bytes 131104 | tf_op jit(solution)/shard_map/ppermute | solution.py:39
  27.6 2.6 %collective-permute-start.5 = (bf16[2,2,256,256]{3,2,1,0:T(8,128)(2,1)S(1)}, bf16[2,2,256,256]{3,2,1,0:T(8,128)(2,1)S(1)}, u32[]{:S(2)}, u32[]{:S(2)}) collective-permute-start(bf16[2,2,256,256]{3,2,1,0:T(8,128)(2,1)S(1)} %bitcast.91), channel_id=1, source_target_pairs={{0,3},{1,0},{2,1},{3,2},{4,7},{5,4},{6,5},{7,6},{8,11},{9,8},{10,9... | collective-permute-start | bytes 1572872 | tf_op jit(solution)/shard_map/ppermute | solution.py:39
  31.5 7.6 %collective-permute-done.5.refs_3_ = bf16[2,2,256,256]{3,2,1,0:T(8,128)(2,1)S(1)} collective-permute-done((bf16[2,2,256,256]{3,2,1,0:T(8,128)(2,1)S(1)}, bf16[2,2,256,256]{3,2,1,0:T(8,128)(2,1)S(1)}, u32[]{:S(2)}, u32[]{:S(2)}) %collective-permute-start.5) | collective-permute-done | bytes 524320 | tf_op jit(solution)/shard_map/ppermute | solution.py:39
  39.0 2.7 %collective-permute-done.4.refs_2_ = bf16[2,2,256,256]{3,2,1,0:T(8,128)(2,1)S(1)} collective-permute-done((bf16[2,2,256,256]{3,2,1,0:T(8,128)(2,1)S(1)}, bf16[2,2,256,256]{3,2,1,0:T(8,128)(2,1)S(1)}, u32[]{:S(2)}, u32[]{:S(2)}) %collective-permute-start.4) | collective-permute-done | bytes 524320 | tf_op jit(solution)/shard_map/ppermute | solution.py:39
  41.8 15.1 %collective-permute-done.3.refs_1_ = bf16[2,2,256,256]{3,2,1,0:T(8,128)(2,1)S(1)} collective-permute-done((bf16[2,2,256,256]{3,2,1,0:T(8,128)(2,1)S(1)}, bf16[2,2,256,256]{3,2,1,0:T(8,128)(2,1)S(1)}, u32[]{:S(2)}, u32[]{:S(2)}) %collective-permute-start.3) | collective-permute-done | bytes 524320 | tf_op jit(solution)/shard_map/ppermute | solution.py:39
  58.8 1.5 collective-permute-start.14
  61.9 6.2 %query_part.1 = (bf16[1024,128]{1,0:T(8,128)(2,1)}, bf16[1024,128]{1,0:T(8,128)(2,1)}, bf16[1024,128]{1,0:T(8,128)(2,1)}, bf16[1024,128]{1,0:T(8,128)(2,1)}) custom-call(s32[23]{0:T(128)} %stack.209.place_ref, bf16[2,2,256,256]{3,2,1,0:T(8,128)(2,1)} %bitcast.95, bf16[2,2,256,256]{3,2,1,0:T(8,128)(2,1)} %copy-done.26, bf16[2,2,256,256]{3,2,1,0:T(8,128)(2,1)} %copy-done.25, ...), custom_call_target="tpu_custom_call" | custom-call | flops 2147483648 | bytes 7340032 | tf_op jit(solution)/shard_map/query_part/pallas_call | solution.py:72
  68.1 1.1 collective-permute-done.14.p2_ref
  69.4 1.9 collective-permute-start.18
  71.3 1.5 collective-permute-start.15
  72.7 0.9 collective-permute-start.16
  73.6 1.5 collective-permute-start.17
  75.1 5.5 %collective-permute-done.18.prev_ref = bf16[2,2,256,128]{3,2,1,0:T(8,128)(2,1)S(1)} collective-permute-done((bf16[2,2,256,128]{3,2,1,0:T(8,128)(2,1)S(1)}, bf16[2,2,256,128]{3,2,1,0:T(8,128)(2,1)S(1)}, u32[]{:S(2)}, u32[]{:S(2)}) %collective-permute-start.18) | collective-permute-done | bytes 262176 | tf_op jit(solution)/shard_map/ppermute | solution.py:39
  80.6 3.7 %collective-permute-done.16.q2_ref = bf16[1024,128]{1,0:T(8,128)(2,1)S(1)} collective-permute-done((bf16[1024,128]{1,0:T(8,128)(2,1)}, bf16[1024,128]{1,0:T(8,128)(2,1)S(1)}, u32[]{:S(2)}, u32[]{:S(2)}) %collective-permute-start.16) | collective-permute-done | bytes 262176 | tf_op jit(solution)/shard_map/ppermute | solution.py:39
  84.4 2.9 %collective-permute-done.17.q3_ref = bf16[1024,128]{1,0:T(8,128)(2,1)S(1)} collective-permute-done((bf16[1024,128]{1,0:T(8,128)(2,1)}, bf16[1024,128]{1,0:T(8,128)(2,1)S(1)}, u32[]{:S(2)}, u32[]{:S(2)}) %collective-permute-start.17) | collective-permute-done | bytes 262176 | tf_op jit(solution)/shard_map/ppermute | solution.py:39
  87.9 7.3 %attend.1 = (bf16[4,256,128]{2,1,0:T(8,128)(2,1)}, bf16[1024,128]{1,0:T(8,128)(2,1)}, f32[4,2,256,128]{3,2,1,0:T(8,128)}, bf16[2,2,256,128]{3,2,1,0:T(8,128)(2,1)}) custom-call(s32[23]{0:T(128)} %stack.209.place_ref, bf16[1024,128]{1,0:T(8,128)(2,1)} %get-tuple-element.79.q0_ref, bf16[1024,128]{1,0:T(8,128)(2,1)} %copy-done.28, ...), custom_call_target="tpu_custom_call" | custom-call | flops 1207959552 | bytes 5242880 | tf_op jit(solution)/shard_map/attend/pallas_call | solution.py:250
  95.3 4.0 %collective-permute-start.22 = (bf16[2,2,256,128]{3,2,1,0:T(8,128)(2,1)}, bf16[2,2,256,128]{3,2,1,0:T(8,128)(2,1)S(1)}, u32[]{:S(2)}, u32[]{:S(2)}) collective-permute-start(bf16[2,2,256,128]{3,2,1,0:T(8,128)(2,1)} %get-tuple-element.87), channel_id=1, source_target_pairs={{0,224},{1,225},{2,226},{3,227},{4,228},{5,229},{6,230},{7,231},{8... | collective-permute-start | bytes 786440 | tf_op jit(solution)/shard_map/ppermute | solution.py:39
  99.3 1.7 collective-permute-start.21
  101.0 1.6 collective-permute-start.19
  103.0 8.0 %collective-permute-done.21.refs_3_.refs_11_ = bf16[1024,128]{1,0:T(8,128)(2,1)S(1)} collective-permute-done((bf16[1024,128]{1,0:T(8,128)(2,1)}, bf16[1024,128]{1,0:T(8,128)(2,1)S(1)}, u32[]{:S(2)}, u32[]{:S(2)}) %collective-permute-start.21) | collective-permute-done | bytes 262176 | tf_op jit(solution)/shard_map/ppermute | solution.py:39
  111.0 1.1 collective-permute-done.19.refs_1_.refs_9_
  112.8 6.2 %d_weight_part.1 = bf16[8,256,512]{2,1,0:T(8,128)(2,1)} custom-call(s32[23]{0:T(128)} %stack.209.place_ref, bf16[2,2,256,256]{3,2,1,0:T(8,128)(2,1)} %bitcast.96, bf16[2,2,256,256]{3,2,1,0:T(8,128)(2,1)} %copy-done.26, bf16[2,2,256,256]{3,2,1,0:T(8,128)(2,1)} %copy-done.25, bf16[2,2,256,256]{3,2,1,0:T(8,128)(2,1)} %copy-done.24, ...), custom_call_target="tpu_custom_call" | custom-call | flops 2147483648 | bytes 7340032 | tf_op jit(solution)/shard_map/d_weight_part/pallas_call | solution.py:72
  119.6 4.7 %d_hidden_away.1 = bf16[8,2,256,256]{3,2,1,0:T(8,128)(2,1)} custom-call(s32[23]{0:T(128)} %stack.237.place_ref, bf16[1024,128]{1,0:T(8,128)(2,1)} %get-tuple-element.88.refs_0_.refs_8_, bf16[1024,128]{1,0:T(8,128)(2,1)} %copy-done.4, bf16[1024,128]{1,0:T(8,128)(2,1)} %copy-done.3, bf16[1024,128]{1,0:T(8,128)(2,1)} %copy-done.2, bf16[8,256,512]{2,1,0:T(8,128)(2,1)} %bitcast.83), custom_call_target="tpu_custom_call" | custom-call | flops 1073741824 | bytes 5242880 | tf_op jit(solution)/shard_map/d_hidden_away/pallas_call | solution.py:72
  124.3 3.8 %collective-permute-start.23 = (bf16[8,2,256,256]{3,2,1,0:T(8,128)(2,1)}, bf16[8,2,256,256]{3,2,1,0:T(8,128)(2,1)S(1)}, u32[]{:S(2)}, u32[]{:S(2)}) collective-permute-start(bf16[8,2,256,256]{3,2,1,0:T(8,128)(2,1)} %d_hidden_away.1), channel_id=1, source_target_pairs={{0,8},{1,9},{2,10},{3,11},{4,12},{5,13},{6,14},{7,15},{8,0},{9,1},... | collective-permute-start | bytes 6291464 | tf_op jit(solution)/shard_map/ppermute | solution.py:39
  128.1 1.1 fusion.9
  129.4 2.6 %collective-permute-done.23.refs_5_ = bf16[8,2,256,256]{3,2,1,0:T(8,128)(2,1)S(1)} collective-permute-done((bf16[8,2,256,256]{3,2,1,0:T(8,128)(2,1)}, bf16[8,2,256,256]{3,2,1,0:T(8,128)(2,1)S(1)}, u32[]{:S(2)}, u32[]{:S(2)}) %collective-permute-start.23) | collective-permute-done | bytes 2097184 | tf_op jit(solution)/shard_map/ppermute | solution.py:39
  132.1 1.3 copy-done
  133.4 4.9 %d_hidden_near.1 = (bf16[2,2,256,256]{3,2,1,0:T(8,128)(2,1)}, bf16[2,2,256,256]{3,2,1,0:T(8,128)(2,1)}, bf16[2,2,256,256]{3,2,1,0:T(8,128)(2,1)}, bf16[2,2,256,256]{3,2,1,0:T(8,128)(2,1)}) custom-call(s32[23]{0:T(128)} %stack.209.place_ref, bf16[1024,128]{1,0:T(8,128)(2,1)} %get-tuple-element.88.refs_0_.refs_8_, bf16[1024,128]{1,0:T(8,128)(2,1)} %copy-done.4, ...), custom_call_target="tpu_custom_call" | custom-call | flops 1073741824 | bytes 7340032 | tf_op jit(solution)/shard_map/d_hidden_near/pallas_call | solution.py:72
  140.3 0.8 collective-permute-start.28
  142.5 0.8 copy-done.10
  143.3 2.2 %attended_last.1 = (bf16[256,512]{1,0:T(8,128)(2,1)}, bf16[256,512]{1,0:T(8,128)(2,1)}, bf16[256,512]{1,0:T(8,128)(2,1)}) custom-call(s32[23]{0:T(128)} %stack.209.place_ref, bf16[3,256,128]{2,1,0:T(8,128)(2,1)} %pad_maximum_fusion.10.own_ref, bf16[2,3,256,128]{3,2,1,0:T(8,128)(2,1)} %copy-done.10, bf16[2,3,256,128]{3,2,1,0:T(8,128)(2,1)} %copy-done.5), custom_call_target="tpu_custom_call" | custom-call | bytes 1048576 | tf_op jit(solution)/shard_map/attended_last/pallas_call | solution.py:72
  145.5 6.4 %collective-permute-done.24 = bf16[2,2,256,256]{3,2,1,0:T(8,128)(2,1)S(1)} collective-permute-done((bf16[2,2,256,256]{3,2,1,0:T(8,128)(2,1)}, bf16[2,2,256,256]{3,2,1,0:T(8,128)(2,1)S(1)}, u32[]{:S(2)}, u32[]{:S(2)}) %collective-permute-start.24) | collective-permute-done | bytes 524320 | tf_op jit(solution)/shard_map/ppermute | solution.py:39
  151.8 1.4 collective-permute-done.25
  153.2 12.2 %collective-permute-done.26 = bf16[2,2,256,256]{3,2,1,0:T(8,128)(2,1)S(1)} collective-permute-done((bf16[2,2,256,256]{3,2,1,0:T(8,128)(2,1)}, bf16[2,2,256,256]{3,2,1,0:T(8,128)(2,1)S(1)}, u32[]{:S(2)}, u32[]{:S(2)}) %collective-permute-start.26) | collective-permute-done | bytes 524320 | tf_op jit(solution)/shard_map/ppermute | solution.py:39
  166.4 1.7 collective-permute-start.31
  168.1 1.6 collective-permute-start.29
  169.7 1.6 fusion.12
  171.3 2.3 %collective-permute-start.34 = (bf16[128,256]{1,0:T(8,128)(2,1)S(1)}, bf16[128,256]{1,0:T(8,128)(2,1)S(1)}, u32[]{:S(2)}, u32[]{:S(2)}) collective-permute-start(bf16[128,256]{1,0:T(8,128)(2,1)S(1)} %get-tuple-element.121), channel_id=1, source_target_pairs={{0,12},{1,13},{2,14},{3,15},{4,8},{5,9},{6,10},{7,11},{8,4},{9,5},... | collective-permute-start | bytes 196616 | tf_op jit(solution)/shard_map/ppermute | solution.py:39
  173.6 2.0 %collective-permute-start.33 = (bf16[128,256]{1,0:T(8,128)(2,1)S(1)}, bf16[128,256]{1,0:T(8,128)(2,1)S(1)}, u32[]{:S(2)}, u32[]{:S(2)}) collective-permute-start(bf16[128,256]{1,0:T(8,128)(2,1)S(1)} %get-tuple-element.124), channel_id=1, source_target_pairs={{0,4},{1,5},{2,6},{3,7},{4,0},{5,1},{6,2},{7,3},{8,12},{9,13},{10,... | collective-permute-start | bytes 196616 | tf_op jit(solution)/shard_map/ppermute | solution.py:39
  175.6 4.2 %collective-permute-done.34.refs_7_ = bf16[128,256]{1,0:T(8,128)(2,1)S(1)} collective-permute-done((bf16[128,256]{1,0:T(8,128)(2,1)S(1)}, bf16[128,256]{1,0:T(8,128)(2,1)S(1)}, u32[]{:S(2)}, u32[]{:S(2)}) %collective-permute-start.34) | collective-permute-done | bytes 65568 | tf_op jit(solution)/shard_map/ppermute | solution.py:39
  180.4 2.2 %last.1 = (bf16[256,1024]{1,0:T(8,128)(2,1)}, bf16[256,512]{1,0:T(8,128)(2,1)}) custom-call(s32[23]{0:T(128)} %stack.209.place_ref, bf16[256,256]{1,0:T(8,128)(2,1)} %get-tuple-element.118.refs_0_, bf16[256,256]{1,0:T(8,128)(2,1)} %copy-done.20, bf16[256,256]{1,0:T(8,128)(2,1)} %copy-done.19, bf16[256,256]{1,0:T(8,128)(2,1)} %copy-done.18, ...), custom_call_target="tpu_custom_call" | custom-call | bytes 1048576 | tf_op jit(solution)/shard_map/last/pallas_call | solution.py:72
  (138 shorter events, 14.6 us)
Async XLA Ops:
  7.2 11.6 %copy-start.8 = (bf16[256,1024]{1,0:T(8,128)(2,1)S(1)}, bf16[256,1024]{1,0:T(8,128)(2,1)}, u32[]{:S(2)}) copy-start(bf16[256,1024]{1,0:T(8,128)(2,1)} %param.5) | copy-start | bytes 1572868
  7.2 54.7 %all-gather.3.cloned.1.call-start = ((), (), s32[]{:S(2)}) async-start(), calls=%async_computation.2 | async-start | bytes 2359296 | tf_op jit(solution)/shard_map/all_gather | solution.py:329
  8.6 6.4 %collective-permute-start.12 = (bf16[128,256]{1,0:T(8,128)(2,1)S(1)}, bf16[128,256]{1,0:T(8,128)(2,1)S(1)}, u32[]{:S(2)}, u32[]{:S(2)}) collective-permute-start(bf16[128,256]{1,0:T(8,128)(2,1)S(1)} %pad_maximum_fusion.14), channel_id=1, source_target_pairs={{0,12},{1,13},{2,14},{3,15},{4,8},{5,9},{6,10},{7,11},{8,4},{9,5},... | collective-permute-start | bytes 196616 | tf_op jit(solution)/shard_map/ppermute | solution.py:39
  13.1 1.9 %collective-permute-start.11 = (bf16[128,256]{1,0:T(8,128)(2,1)S(1)}, bf16[128,256]{1,0:T(8,128)(2,1)S(1)}, u32[]{:S(2)}, u32[]{:S(2)}) collective-permute-start(bf16[128,256]{1,0:T(8,128)(2,1)S(1)} %pad_maximum_fusion.13), channel_id=1, source_target_pairs={{0,8},{1,9},{2,10},{3,11},{4,12},{5,13},{6,14},{7,15},{8,0},{9,1},... | collective-permute-start | bytes 196616 | tf_op jit(solution)/shard_map/ppermute | solution.py:39
  13.2 4.7 %collective-permute-start.10 = (bf16[128,256]{1,0:T(8,128)(2,1)S(1)}, bf16[128,256]{1,0:T(8,128)(2,1)S(1)}, u32[]{:S(2)}, u32[]{:S(2)}) collective-permute-start(bf16[128,256]{1,0:T(8,128)(2,1)S(1)} %pad_maximum_fusion.12), channel_id=1, source_target_pairs={{0,4},{1,5},{2,6},{3,7},{4,0},{5,1},{6,2},{7,3},{8,12},{9,13},{10,... | collective-permute-start | bytes 196616 | tf_op jit(solution)/shard_map/ppermute | solution.py:39
  18.7 151.0 %reduce-scatter.2.cloned.1.call-start = ((), (), s32[]{:S(2)}) async-start(), calls=%async_computation.1 | async-start | bytes 2359296 | tf_op jit(solution)/shard_map/reduce_scatter | solution.py:344
  19.1 12.2 %copy-start.12 = (bf16[256,512]{1,0:T(8,128)(2,1)S(1)}, bf16[256,512]{1,0:T(8,128)(2,1)}, u32[]{:S(2)}) copy-start(bf16[256,512]{1,0:T(8,128)(2,1)} %param.7) | copy-start | bytes 786436
  19.2 5.1 %collective-permute-start.2 = (bf16[256,256]{0,1:T(8,128)(2,1)S(1)}, bf16[256,256]{0,1:T(8,128)(2,1)S(1)}, u32[]{:S(2)}, u32[]{:S(2)}) collective-permute-start(bf16[256,256]{0,1:T(8,128)(2,1)S(1)} %bitcast.100), channel_id=1, source_target_pairs={{0,20},{1,21},{2,22},{3,23},{4,16},{5,17},{6,18},{7,19},{8,28},{9,... | collective-permute-start | bytes 393224 | tf_op jit(solution)/shard_map/ppermute | solution.py:39
  20.3 4.0 %collective-permute-start = (bf16[256,256]{0,1:T(8,128)(2,1)S(1)}, bf16[256,256]{0,1:T(8,128)(2,1)S(1)}, u32[]{:S(2)}, u32[]{:S(2)}) collective-permute-start(bf16[256,256]{0,1:T(8,128)(2,1)S(1)} %bitcast.99), channel_id=1, source_target_pairs={{0,16},{1,17},{2,18},{3,19},{4,20},{5,21},{6,22},{7,23},{8,24},{9,... | collective-permute-start | bytes 393224 | tf_op jit(solution)/shard_map/ppermute | solution.py:39
  20.7 6.6 %collective-permute-start.1 = (bf16[256,256]{0,1:T(8,128)(2,1)S(1)}, bf16[256,256]{0,1:T(8,128)(2,1)S(1)}, u32[]{:S(2)}, u32[]{:S(2)}) collective-permute-start(bf16[256,256]{0,1:T(8,128)(2,1)S(1)} %bitcast.98), channel_id=1, source_target_pairs={{0,4},{1,5},{2,6},{3,7},{4,0},{5,1},{6,2},{7,3},{8,12},{9,13},{10,... | collective-permute-start | bytes 393224 | tf_op jit(solution)/shard_map/ppermute | solution.py:39
  27.6 32.7 %copy-start.9 = (bf16[4,256,256]{2,1,0:T(8,128)(2,1)}, bf16[4,256,256]{2,1,0:T(8,128)(2,1)S(1)}, u32[]{:S(2)}) copy-start(bf16[4,256,256]{2,1,0:T(8,128)(2,1)S(1)} %copy.14) | copy-start | bytes 1572868
  27.6 11.4 %collective-permute-start.5 = (bf16[2,2,256,256]{3,2,1,0:T(8,128)(2,1)S(1)}, bf16[2,2,256,256]{3,2,1,0:T(8,128)(2,1)S(1)}, u32[]{:S(2)}, u32[]{:S(2)}) collective-permute-start(bf16[2,2,256,256]{3,2,1,0:T(8,128)(2,1)S(1)} %bitcast.91), channel_id=1, source_target_pairs={{0,3},{1,0},{2,1},{3,2},{4,7},{5,4},{6,5},{7,6},{8,11},{9,8},{10,9... | collective-permute-start | bytes 1572872 | tf_op jit(solution)/shard_map/ppermute | solution.py:39
  30.2 11.6 %collective-permute-start.4 = (bf16[2,2,256,256]{3,2,1,0:T(8,128)(2,1)S(1)}, bf16[2,2,256,256]{3,2,1,0:T(8,128)(2,1)S(1)}, u32[]{:S(2)}, u32[]{:S(2)}) collective-permute-start(bf16[2,2,256,256]{3,2,1,0:T(8,128)(2,1)S(1)} %bitcast.92), channel_id=1, source_target_pairs={{0,2},{1,3},{2,0},{3,1},{4,6},{5,7},{6,4},{7,5},{8,10},{9,11},{10,... | collective-permute-start | bytes 1572872 | tf_op jit(solution)/shard_map/ppermute | solution.py:39
  30.7 26.2 %collective-permute-start.3 = (bf16[2,2,256,256]{3,2,1,0:T(8,128)(2,1)S(1)}, bf16[2,2,256,256]{3,2,1,0:T(8,128)(2,1)S(1)}, u32[]{:S(2)}, u32[]{:S(2)}) collective-permute-start(bf16[2,2,256,256]{3,2,1,0:T(8,128)(2,1)S(1)} %bitcast.93), channel_id=1, source_target_pairs={{0,1},{1,2},{2,3},{3,0},{4,5},{5,6},{6,7},{7,4},{8,9},{9,10},{10,1... | collective-permute-start | bytes 1572872 | tf_op jit(solution)/shard_map/ppermute | solution.py:39
  31.4 37.8 %copy-start.6 = (bf16[3,256,128]{2,1,0:T(8,128)(2,1)}, bf16[3,256,128]{2,1,0:T(8,128)(2,1)S(1)}, u32[]{:S(2)}) copy-start(bf16[3,256,128]{2,1,0:T(8,128)(2,1)S(1)} %pad_maximum_fusion.6.p0_ref) | copy-start | bytes 589828
  39.0 22.8 %copy-start.24 = (bf16[2,2,256,256]{3,2,1,0:T(8,128)(2,1)}, bf16[2,2,256,256]{3,2,1,0:T(8,128)(2,1)S(1)}, u32[]{:S(2)}) copy-start(bf16[2,2,256,256]{3,2,1,0:T(8,128)(2,1)S(1)} %collective-permute-done.5.refs_3_) | copy-start | bytes 1572868
  41.8 20.1 %copy-start.25 = (bf16[2,2,256,256]{3,2,1,0:T(8,128)(2,1)}, bf16[2,2,256,256]{3,2,1,0:T(8,128)(2,1)S(1)}, u32[]{:S(2)}) copy-start(bf16[2,2,256,256]{3,2,1,0:T(8,128)(2,1)S(1)} %collective-permute-done.4.refs_2_) | copy-start | bytes 1572868
  56.9 1.8 collective-permute-start.13
  57.4 3.6 %collective-permute-start.6 = (bf16[2,2,256,256]{3,2,1,0:T(8,128)(2,1)S(1)}, bf16[2,2,256,256]{3,2,1,0:T(8,128)(2,1)}, u32[]{:S(2)}, u32[]{:S(2)}) collective-permute-start(bf16[2,2,256,256]{3,2,1,0:T(8,128)(2,1)S(1)} %bitcast.94), channel_id=1, source_target_pairs={{0,8},{1,9},{2,10},{3,11},{4,12},{5,13},{6,14},{7,15},{8,0},{9,1},... | collective-permute-start | bytes 1572872 | tf_op jit(solution)/shard_map/ppermute | solution.py:39
  57.5 3.5 %collective-permute-start.7 = (bf16[2,2,256,256]{3,2,1,0:T(8,128)(2,1)S(1)}, bf16[2,2,256,256]{3,2,1,0:T(8,128)(2,1)}, u32[]{:S(2)}, u32[]{:S(2)}) collective-permute-start(bf16[2,2,256,256]{3,2,1,0:T(8,128)(2,1)S(1)} %collective-permute-done.3.refs_1_), channel_id=1, source_target_pairs={{0,8},{1,9},{2,10},{3,11},{4,12},{5,13},{6,14},{7,15},{8,0},{9,1},... | collective-permute-start | bytes 1572872 | tf_op jit(solution)/shard_map/ppermute | solution.py:39
  57.9 3.2 %collective-permute-start.8 = (bf16[2,2,256,256]{3,2,1,0:T(8,128)(2,1)S(1)}, bf16[2,2,256,256]{3,2,1,0:T(8,128)(2,1)}, u32[]{:S(2)}, u32[]{:S(2)}) collective-permute-start(bf16[2,2,256,256]{3,2,1,0:T(8,128)(2,1)S(1)} %collective-permute-done.4.refs_2_), channel_id=1, source_target_pairs={{0,8},{1,9},{2,10},{3,11},{4,12},{5,13},{6,14},{7,15},{8,0},{9,1},... | collective-permute-start | bytes 1572872 | tf_op jit(solution)/shard_map/ppermute | solution.py:39
  58.0 3.8 %collective-permute-start.9 = (bf16[2,2,256,256]{3,2,1,0:T(8,128)(2,1)S(1)}, bf16[2,2,256,256]{3,2,1,0:T(8,128)(2,1)}, u32[]{:S(2)}, u32[]{:S(2)}) collective-permute-start(bf16[2,2,256,256]{3,2,1,0:T(8,128)(2,1)S(1)} %collective-permute-done.5.refs_3_), channel_id=1, source_target_pairs={{0,8},{1,9},{2,10},{3,11},{4,12},{5,13},{6,14},{7,15},{8,0},{9,1},... | collective-permute-start | bytes 1572872 | tf_op jit(solution)/shard_map/ppermute | solution.py:39
  58.7 10.5 %copy-start.11 = (bf16[2,3,256,128]{3,2,1,0:T(8,128)(2,1)}, bf16[2,3,256,128]{3,2,1,0:T(8,128)(2,1)S(1)}, u32[]{:S(2)}) copy-start(bf16[2,3,256,128]{3,2,1,0:T(8,128)(2,1)S(1)} %collective-permute-done.13.p1_ref) | copy-start | bytes 1179652
  58.8 10.4 %collective-permute-start.14 = (bf16[2,3,256,128]{3,2,1,0:T(8,128)(2,1)S(1)}, bf16[2,3,256,128]{3,2,1,0:T(8,128)(2,1)S(1)}, u32[]{:S(2)}, u32[]{:S(2)}) collective-permute-start(bf16[2,3,256,128]{3,2,1,0:T(8,128)(2,1)S(1)} %pad_maximum_fusion.2), channel_id=1, source_target_pairs={{0,16},{1,17},{2,18},{3,19},{4,20},{5,21},{6,22},{7,23},{8,24},{9,... | collective-permute-start | bytes 1179656 | tf_op jit(solution)/shard_map/ppermute | solution.py:39
  69.2 18.0 %copy-start.17 = (bf16[2,3,256,128]{3,2,1,0:T(8,128)(2,1)}, bf16[2,3,256,128]{3,2,1,0:T(8,128)(2,1)S(1)}, u32[]{:S(2)}) copy-start(bf16[2,3,256,128]{3,2,1,0:T(8,128)(2,1)S(1)} %collective-permute-done.14.p2_ref) | copy-start | bytes 1179652
  69.4 11.3 %collective-permute-start.18 = (bf16[2,2,256,128]{3,2,1,0:T(8,128)(2,1)S(1)}, bf16[2,2,256,128]{3,2,1,0:T(8,128)(2,1)S(1)}, u32[]{:S(2)}, u32[]{:S(2)}) collective-permute-start(bf16[2,2,256,128]{3,2,1,0:T(8,128)(2,1)S(1)} %reverse_select_fusion), channel_id=1, source_target_pairs={{0,32},{1,33},{2,34},{3,35},{4,36},{5,37},{6,38},{7,39},{8,40},{9,... | collective-permute-start | bytes 786440 | tf_op jit(solution)/shard_map/ppermute | solution.py:39
  71.3 9.4 %collective-permute-start.15 = (bf16[1024,128]{1,0:T(8,128)(2,1)}, bf16[1024,128]{1,0:T(8,128)(2,1)S(1)}, u32[]{:S(2)}, u32[]{:S(2)}) collective-permute-start(bf16[1024,128]{1,0:T(8,128)(2,1)} %get-tuple-element.80), channel_id=1, source_target_pairs={{0,16},{1,17},{2,18},{3,19},{4,20},{5,21},{6,22},{7,23},{8,24},{9,... | collective-permute-start | bytes 786440 | tf_op jit(solution)/shard_map/ppermute | solution.py:39
  72.7 11.6 %collective-permute-start.16 = (bf16[1024,128]{1,0:T(8,128)(2,1)}, bf16[1024,128]{1,0:T(8,128)(2,1)S(1)}, u32[]{:S(2)}, u32[]{:S(2)}) collective-permute-start(bf16[1024,128]{1,0:T(8,128)(2,1)} %get-tuple-element.81), channel_id=1, source_target_pairs={{0,4},{1,5},{2,6},{3,7},{4,0},{5,1},{6,2},{7,3},{8,12},{9,13},{10,... | collective-permute-start | bytes 786440 | tf_op jit(solution)/shard_map/ppermute | solution.py:39
  73.6 13.6 %collective-permute-start.17 = (bf16[1024,128]{1,0:T(8,128)(2,1)}, bf16[1024,128]{1,0:T(8,128)(2,1)S(1)}, u32[]{:S(2)}, u32[]{:S(2)}) collective-permute-start(bf16[1024,128]{1,0:T(8,128)(2,1)} %get-tuple-element.82), channel_id=1, source_target_pairs={{0,20},{1,21},{2,22},{3,23},{4,16},{5,17},{6,18},{7,19},{8,28},{9,... | collective-permute-start | bytes 786440 | tf_op jit(solution)/shard_map/ppermute | solution.py:39
  95.3 7.7 %collective-permute-start.22 = (bf16[2,2,256,128]{3,2,1,0:T(8,128)(2,1)}, bf16[2,2,256,128]{3,2,1,0:T(8,128)(2,1)S(1)}, u32[]{:S(2)}, u32[]{:S(2)}) collective-permute-start(bf16[2,2,256,128]{3,2,1,0:T(8,128)(2,1)} %get-tuple-element.87), channel_id=1, source_target_pairs={{0,224},{1,225},{2,226},{3,227},{4,228},{5,229},{6,230},{7,231},{8... | collective-permute-start | bytes 786440 | tf_op jit(solution)/shard_map/ppermute | solution.py:39
  99.3 11.6 %collective-permute-start.21 = (bf16[1024,128]{1,0:T(8,128)(2,1)}, bf16[1024,128]{1,0:T(8,128)(2,1)S(1)}, u32[]{:S(2)}, u32[]{:S(2)}) collective-permute-start(bf16[1024,128]{1,0:T(8,128)(2,1)} %get-tuple-element.88.refs_0_.refs_8_), channel_id=1, source_target_pairs={{0,20},{1,21},{2,22},{3,23},{4,16},{5,17},{6,18},{7,19},{8,28},{9,... | collective-permute-start | bytes 786440 | tf_op jit(solution)/shard_map/ppermute | solution.py:39
  101.0 10.0 %collective-permute-start.20 = (bf16[1024,128]{1,0:T(8,128)(2,1)}, bf16[1024,128]{1,0:T(8,128)(2,1)S(1)}, u32[]{:S(2)}, u32[]{:S(2)}) collective-permute-start(bf16[1024,128]{1,0:T(8,128)(2,1)} %get-tuple-element.88.refs_0_.refs_8_), channel_id=1, source_target_pairs={{0,4},{1,5},{2,6},{3,7},{4,0},{5,1},{6,2},{7,3},{8,12},{9,13},{10,... | collective-permute-start | bytes 786440 | tf_op jit(solution)/shard_map/ppermute | solution.py:39
  101.0 11.1 %collective-permute-start.19 = (bf16[1024,128]{1,0:T(8,128)(2,1)}, bf16[1024,128]{1,0:T(8,128)(2,1)S(1)}, u32[]{:S(2)}, u32[]{:S(2)}) collective-permute-start(bf16[1024,128]{1,0:T(8,128)(2,1)} %get-tuple-element.88.refs_0_.refs_8_), channel_id=1, source_target_pairs={{0,16},{1,17},{2,18},{3,19},{4,20},{5,21},{6,22},{7,23},{8,24},{9,... | collective-permute-start | bytes 786440 | tf_op jit(solution)/shard_map/ppermute | solution.py:39
  119.6 8.4 %copy-start.13 = (bf16[4,256,128]{2,1,0:T(8,128)(2,1)S(1)}, bf16[4,256,128]{2,1,0:T(8,128)(2,1)}, u32[]{:S(2)}) copy-start(bf16[4,256,128]{2,1,0:T(8,128)(2,1)} %get-tuple-element.96) | copy-start | bytes 786436
  119.6 8.5 %copy-start.1 = (f32[4,2,256,128]{3,2,1,0:T(8,128)S(1)}, f32[4,2,256,128]{3,2,1,0:T(8,128)}, u32[]{:S(2)}) copy-start(f32[4,2,256,128]{3,2,1,0:T(8,128)} %get-tuple-element.97) | copy-start | bytes 3145732
  124.3 7.8 %collective-permute-start.23 = (bf16[8,2,256,256]{3,2,1,0:T(8,128)(2,1)}, bf16[8,2,256,256]{3,2,1,0:T(8,128)(2,1)S(1)}, u32[]{:S(2)}, u32[]{:S(2)}) collective-permute-start(bf16[8,2,256,256]{3,2,1,0:T(8,128)(2,1)} %d_hidden_away.1), channel_id=1, source_target_pairs={{0,8},{1,9},{2,10},{3,11},{4,12},{5,13},{6,14},{7,15},{8,0},{9,1},... | collective-permute-start | bytes 6291464 | tf_op jit(solution)/shard_map/ppermute | solution.py:39
  129.3 10.9 %collective-permute-start.27 = (bf16[2,3,256,128]{3,2,1,0:T(8,128)(2,1)S(1)}, bf16[2,3,256,128]{3,2,1,0:T(8,128)(2,1)S(1)}, u32[]{:S(2)}, u32[]{:S(2)}) collective-permute-start(bf16[2,3,256,128]{3,2,1,0:T(8,128)(2,1)S(1)} %pad_maximum_fusion.3), channel_id=1, source_target_pairs={{0,16},{1,17},{2,18},{3,19},{4,20},{5,21},{6,22},{7,23},{8,24},{9,... | collective-permute-start | bytes 1179656 | tf_op jit(solution)/shard_map/ppermute | solution.py:39
  138.4 27.1 %copy-start.7 = (bf16[2,2,256,256]{3,2,1,0:T(8,128)(2,1)S(1)}, bf16[2,2,256,256]{3,2,1,0:T(8,128)(2,1)}, u32[]{:S(2)}) copy-start(bf16[2,2,256,256]{3,2,1,0:T(8,128)(2,1)} %get-tuple-element.103) | copy-start | bytes 1572868
  138.4 13.5 %collective-permute-start.24 = (bf16[2,2,256,256]{3,2,1,0:T(8,128)(2,1)}, bf16[2,2,256,256]{3,2,1,0:T(8,128)(2,1)S(1)}, u32[]{:S(2)}, u32[]{:S(2)}) collective-permute-start(bf16[2,2,256,256]{3,2,1,0:T(8,128)(2,1)} %get-tuple-element.93), channel_id=1, source_target_pairs={{0,3},{1,0},{2,1},{3,2},{4,7},{5,4},{6,5},{7,6},{8,11},{9,8},{10,9... | collective-permute-start | bytes 1572872 | tf_op jit(solution)/shard_map/ppermute | solution.py:39
  138.7 14.6 %collective-permute-start.25 = (bf16[2,2,256,256]{3,2,1,0:T(8,128)(2,1)}, bf16[2,2,256,256]{3,2,1,0:T(8,128)(2,1)S(1)}, u32[]{:S(2)}, u32[]{:S(2)}) collective-permute-start(bf16[2,2,256,256]{3,2,1,0:T(8,128)(2,1)} %get-tuple-element.94), channel_id=1, source_target_pairs={{0,2},{1,3},{2,0},{3,1},{4,6},{5,7},{6,4},{7,5},{8,10},{9,11},{10,... | collective-permute-start | bytes 1572872 | tf_op jit(solution)/shard_map/ppermute | solution.py:39
  139.2 26.3 %collective-permute-start.26 = (bf16[2,2,256,256]{3,2,1,0:T(8,128)(2,1)}, bf16[2,2,256,256]{3,2,1,0:T(8,128)(2,1)S(1)}, u32[]{:S(2)}, u32[]{:S(2)}) collective-permute-start(bf16[2,2,256,256]{3,2,1,0:T(8,128)(2,1)} %get-tuple-element.95), channel_id=1, source_target_pairs={{0,1},{1,2},{2,3},{3,0},{4,5},{5,6},{6,7},{7,4},{8,9},{9,10},{10,1... | collective-permute-start | bytes 1572872 | tf_op jit(solution)/shard_map/ppermute | solution.py:39
  140.3 2.2 %collective-permute-start.28 = (bf16[2,3,256,128]{3,2,1,0:T(8,128)(2,1)S(1)}, bf16[2,3,256,128]{3,2,1,0:T(8,128)(2,1)S(1)}, u32[]{:S(2)}, u32[]{:S(2)}) collective-permute-start(bf16[2,3,256,128]{3,2,1,0:T(8,128)(2,1)S(1)} %pad_maximum_fusion.4), channel_id=1, source_target_pairs={{0,8},{1,9},{2,10},{3,11},{4,12},{5,13},{6,14},{7,15},{8,0},{9,1},... | collective-permute-start | bytes 1179656 | tf_op jit(solution)/shard_map/ppermute | solution.py:39
  166.4 7.2 %collective-permute-start.31 = (bf16[256,256]{1,0:T(8,128)(2,1)S(1)}, bf16[256,256]{1,0:T(8,128)(2,1)S(1)}, u32[]{:S(2)}, u32[]{:S(2)}) collective-permute-start(bf16[256,256]{1,0:T(8,128)(2,1)S(1)} %get-tuple-element.115), channel_id=1, source_target_pairs={{0,20},{1,21},{2,22},{3,23},{4,16},{5,17},{6,18},{7,19},{8,28},{9,... | collective-permute-start | bytes 393224 | tf_op jit(solution)/shard_map/ppermute | solution.py:39
  168.1 7.5 %collective-permute-start.30 = (bf16[256,256]{1,0:T(8,128)(2,1)S(1)}, bf16[256,256]{1,0:T(8,128)(2,1)S(1)}, u32[]{:S(2)}, u32[]{:S(2)}) collective-permute-start(bf16[256,256]{1,0:T(8,128)(2,1)S(1)} %get-tuple-element.116), channel_id=1, source_target_pairs={{0,4},{1,5},{2,6},{3,7},{4,0},{5,1},{6,2},{7,3},{8,12},{9,13},{10,... | collective-permute-start | bytes 393224 | tf_op jit(solution)/shard_map/ppermute | solution.py:39
  168.1 7.5 %collective-permute-start.29 = (bf16[256,256]{1,0:T(8,128)(2,1)S(1)}, bf16[256,256]{1,0:T(8,128)(2,1)S(1)}, u32[]{:S(2)}, u32[]{:S(2)}) collective-permute-start(bf16[256,256]{1,0:T(8,128)(2,1)S(1)} %get-tuple-element.117), channel_id=1, source_target_pairs={{0,16},{1,17},{2,18},{3,19},{4,20},{5,21},{6,22},{7,23},{8,24},{9,... | collective-permute-start | bytes 393224 | tf_op jit(solution)/shard_map/ppermute | solution.py:39
  171.3 8.5 %collective-permute-start.34 = (bf16[128,256]{1,0:T(8,128)(2,1)S(1)}, bf16[128,256]{1,0:T(8,128)(2,1)S(1)}, u32[]{:S(2)}, u32[]{:S(2)}) collective-permute-start(bf16[128,256]{1,0:T(8,128)(2,1)S(1)} %get-tuple-element.121), channel_id=1, source_target_pairs={{0,12},{1,13},{2,14},{3,15},{4,8},{5,9},{6,10},{7,11},{8,4},{9,5},... | collective-permute-start | bytes 196616 | tf_op jit(solution)/shard_map/ppermute | solution.py:39
  173.6 6.2 %collective-permute-start.32 = (bf16[128,256]{1,0:T(8,128)(2,1)S(1)}, bf16[128,256]{1,0:T(8,128)(2,1)S(1)}, u32[]{:S(2)}, u32[]{:S(2)}) collective-permute-start(bf16[128,256]{1,0:T(8,128)(2,1)S(1)} %get-tuple-element.122), channel_id=1, source_target_pairs={{0,8},{1,9},{2,10},{3,11},{4,12},{5,13},{6,14},{7,15},{8,0},{9,1},... | collective-permute-start | bytes 196616 | tf_op jit(solution)/shard_map/ppermute | solution.py:39
  173.6 6.2 %collective-permute-start.33 = (bf16[128,256]{1,0:T(8,128)(2,1)S(1)}, bf16[128,256]{1,0:T(8,128)(2,1)S(1)}, u32[]{:S(2)}, u32[]{:S(2)}) collective-permute-start(bf16[128,256]{1,0:T(8,128)(2,1)S(1)} %get-tuple-element.124), channel_id=1, source_target_pairs={{0,4},{1,5},{2,6},{3,7},{4,0},{5,1},{6,2},{7,3},{8,12},{9,13},{10,... | collective-permute-start | bytes 196616 | tf_op jit(solution)/shard_map/ppermute | solution.py:39
  (20 other events, 64.2 us)
Sparse Core Ops, SparseCore 0:
  18.8 39.3 all-gather.2
  119.1 36.6 reduce-scatter.1
where the time goes:
time: 190 us
  waiting for transfers between devices  84.1 us (44%)
  starting transfers between devices  43.8 us (23%)
  Pallas kernels  33.8 us (18%)
  between operations  14.6 us (8%)
  local copies, waits for them, and re-layouts  9.85 us (5%)
  other arithmetic  3.34 us (2%)
    ppermute x35, waiting for transfers between devices, move(): return lax.ppermute(block, AXES, pairs)  84.1 us
    ppermute x35, starting transfers between devices, move(): return lax.ppermute(block, AXES, pairs)  43.8 us
    pallas_call x6, Pallas kernels, in_vmem(): pl.pallas_call(kernel, in_specs=[pl.BlockSpec(memory_space=pltpu.SMEM)] +...  26.4 us
    pallas_call x1, Pallas kernels, attend(): pl.pallas_call(attend_kernel, in_specs=[pl.BlockSpec(memory_space=pltpu.S...  7.34 us
    unnamed x65, local copies, waits for them, and re-layouts  4.51 us
  transfers between devices with their start and end apart: 37, of which 23 were waited for; matrix products, arithmetic and copies ran while one was open for 4% of the time, Pallas kernels for 10%

commit v1 on v0

--- a/solution.py
+++ b/solution.py
@@ -16,7 +16,6 @@
 LOG2E = 1.4426950408889634
 BF = jnp.bfloat16
 F32 = jnp.float32
-VMEM = 56 * 1024 * 1024
 
 
 def route(target):
@@ -39,8 +38,8 @@
     return lax.ppermute(block, AXES, pairs)
 
 
-def params():
-    return pltpu.CompilerParams(vmem_limit_bytes=VMEM)
+def params(mebibytes=20):
+    return pltpu.CompilerParams(vmem_limit_bytes=mebibytes * 1024 * 1024)
 
 
 def cost(flops, bytes_accessed, exps=0):
@@ -67,14 +66,14 @@
                 outs[k][pl.ds(row, T), :] = part[:, k * DH : (k + 1) * DH]
 
 
-def in_vmem(kernel, name, work, outs, *args):
+def in_vmem(kernel, name, work, outs, *args, room=20):
     vm = pl.BlockSpec(memory_space=pltpu.VMEM)
     return pl.pallas_call(
         kernel,
         in_specs=[pl.BlockSpec(memory_space=pltpu.SMEM)] + [vm] * (len(args) - 1),
         out_specs=[vm] * len(outs),
         out_shape=[jax.ShapeDtypeStruct(shape, kind) for shape, kind in outs],
-        compiler_params=params(),
+        compiler_params=params(room),
         cost_estimate=work,
         name=name,
     )(*args)
@@ -83,7 +82,7 @@
 def query_part(place, own, other, weights):
     work = cost(2 * 1024 * 2048 * 512, 7 << 20)
     outs = [((4 * T, DH), BF)] * 4
-    return in_vmem(query_kernel, "query_part", work, outs, place, *own, *other, weights)
+    return in_vmem(query_kernel, "query_part", work, outs, place, *own, *other, weights, room=56)
 
 
 def d_hidden_block(place_ref, refs, dl, i):
@@ -108,7 +107,7 @@
 def d_hidden_away(place, dq, weights):
     work = cost(1024 * 2048 * 512, 5 << 20)
     outs = [((8, 2, T, T), BF)]
-    return in_vmem(d_hidden_away_kernel, "d_hidden_away", work, outs, place, *dq, weights)[0]
+    return in_vmem(d_hidden_away_kernel, "d_hidden_away", work, outs, place, *dq, weights, room=56)[0]
 
 
 def d_hidden_near(place, dq, weights, away):
@@ -169,13 +168,13 @@
 
 
 def attend_kernel(
-    place_ref, q0_ref, q1_ref, q2_ref, q3_ref, p0_ref, p1_ref, p2_ref, prev_ref,
+    place_ref, q0_ref, q1_ref, q2_ref, q3_ref, p0_ref, p1_ref, p2_ref, prev0_ref, prev1_ref,
     out_ref, dq_ref, dkv_ref, dprev_ref, k_ref, v_ref, g_ref, o_ref, dk_ref, dv_ref,
 ):
     tokens = [pl.multiple_of(place_ref[12 + k] * T, T) for k in range(4)]
-    for half in range(2):
-        k_ref[half * T : (half + 1) * T] = prev_ref[half, 0]
-        v_ref[half * T : (half + 1) * T] = prev_ref[half, 1]
+    for half, ref in enumerate((prev0_ref, prev1_ref)):
+        k_ref[half * T : (half + 1) * T] = ref[0]
+        v_ref[half * T : (half + 1) * T] = ref[1]
     for row, ref in zip(tokens, (p0_ref, p1_ref.at[0], p2_ref.at[0], p2_ref.at[1])):
         k_ref[pl.ds(W + row, T), :] = ref[0]
         v_ref[pl.ds(W + row, T), :] = ref[1]
@@ -249,7 +248,7 @@
     n = 4 * T
     return pl.pallas_call(
         attend_kernel,
-        in_specs=[pl.BlockSpec(memory_space=pltpu.SMEM)] + [vm] * 8,
+        in_specs=[pl.BlockSpec(memory_space=pltpu.SMEM)] + [vm] * 9,
         out_specs=[vm] * 4,
         out_shape=[
             jax.ShapeDtypeStruct((4, T, DH), BF),
@@ -265,15 +264,19 @@
             pltpu.VMEM((W + n, DH), F32),
             pltpu.VMEM((W + n, DH), F32),
         ],
-        compiler_params=params(),
+        compiler_params=params(56),
         cost_estimate=cost(12 * n * 768 * DH, 5 << 20, n * W),
         name="attend",
-    )(place, *parts, *pieces, prev)
+    )(place, *parts, *pieces, *prev)
 
 
 def tie(*groups):
     flat = iter(lax.optimization_barrier([a for group in groups for a in group]))
     return [[next(flat) for _ in group] for group in groups]
+
+
+def after(group, *others):
+    return tie(group, others)[0]
 
 
 def per_device(hidden, weight, keys, values, d_attended):
@@ -322,28 +325,30 @@
     mixed = jnp.stack(mixed).reshape(2, 2, T, T)
 
     own = [move(mixed, dx=dx) if dx else mixed for dx in range(NX)]
-    own, kvd = tie(own, kvd)
     other = [move(block, co=1) for block in own]
+    kvd = after(kvd, mixed)
     swapped = move(jnp.stack([kvd[1], kvd[3]]), co=1)
     pieces = [kvd[0], swapped, move(jnp.stack([kvd[2], swapped[1]]), yl=1)]
     weights = lax.all_gather(shard, "z", axis=0, tiled=False)
     own, other, (weights,) = tie(own, other, (weights,))
 
     parts = query_part(place, own, other, weights)
-    parts, pieces = tie(parts, pieces)
+    pieces = after(pieces, *parts)
     low = jnp.where(yl == 1, jnp.stack([pieces[0][:2], pieces[1][0, :2]]), pieces[2][:, :2])
-    prev = move(jnp.where(co == 0, low, low[::-1]), dz=1)
-
-    parts = [parts[0]] + [move(parts[k], yh=k // 2, yl=k % 2) for k in range(1, 4)]
+    prev = [move(lax.dynamic_index_in_dim(low, co ^ k, 0, keepdims=False), dz=1) for k in range(2)]
+    parts = [parts[0]] + [move(parts[k], yh=k // 2, yl=k % 2) for k in (3, 2, 1)]
     attended, dq, dkv, dprev = attend(place, parts, pieces, prev)
     dq = [dq] + [move(dq, yh=k // 2, yl=k % 2) for k in range(1, 4)]
 
-    late = move(dprev, dz=-1)
-    dq, (late,) = tie(dq, (late,))
+    late = [move(dprev[half], dz=-1) for half in range(2)]
+    dq, late = tie(dq, late)
+    late = jnp.stack(late)
+
     sums = d_weight_part(place, own, other, dq)
     shard = lax.psum_scatter(sums.reshape(NZ * T, 4 * DH), "z", scatter_dimension=0, tiled=True)
     away = move(d_hidden_away(place_other, dq, weights), co=1)
     near = d_hidden_near(place, dq, weights, away)
+    line = [near[0]] + [move(near[dx], dx=-dx) for dx in range(1, NX)]
 
     outs = []
     for k, (dl, dc) in enumerate(quad):
@@ -357,17 +362,17 @@
         attended_kernel, "attended_last", cost(0, 1 << 20), [((T, 4 * DH), BF)] * 3, place, *outs
     )
 
-    line = [near[0]] + [move(near[dx], dx=-dx) for dx in range(1, NX)]
-    line, result = tie(line, result)
+    def weight_back(dc, dy):
+        block = lax.dynamic_slice_in_dim(shard, (co ^ dc) * DH, DH, 0)
+        return block[:, dy * T : (dy + 1) * T]
+
+    ends = [weight_back(dc, dy) for dy, dc in quad]
+    line = after(line, *ends)
+    ends = [move(ends[k], yh=quad[k][0], co=quad[k][1]) if k else ends[0] for k in range(4)]
     line = sum(block.astype(F32) for block in line).astype(BF)
     back = [line[dy, dl] for dy, dl in quad]
     back = [back[0]] + [move(back[k], yh=quad[k][0], yl=quad[k][1]) for k in (1, 2, 3)]
-    def weight_back(dc, dy):
-        block = lax.dynamic_slice_in_dim(shard, (co ^ dc) * DH, DH, 0)
-        block = block[:, dy * T : (dy + 1) * T]
-        return move(block, co=dc, yh=dy) if dc or dy else block
-
-    back += [weight_back(dc, dy) for dy, dc in quad]
+    back += ends
     d_hidden, d_weight = in_vmem(
         last_kernel, "last", cost(0, 1 << 20), [((T, 8 * DH), BF), ((T, 4 * DH), BF)], place, *back
     )

time: 190 us -> 179 us (0.942)
  waiting for transfers between devices: 84.1 us -> 48.6 us
  starting transfers between devices: 43.8 us -> 66.1 us
  other arithmetic: 3.34 us -> 7.23 us
  Pallas kernels: 33.8 us -> 30.2 us
  local copies, waits for them, and re-layouts: 9.85 us -> 12 us
    ppermute x35 -> x37, waiting for transfers between devices: 84.1 us -> 35.5 us  [move(): return lax.ppermute(block, AXES, pairs)]
    ppermute x35 -> x37, starting transfers between devices: 43.8 us -> 66.1 us  [move(): return lax.ppermute(block, AXES, pairs)]
    reduce_scatter x1, waiting for transfers between devices: 0.01 us -> 13 us  [per_device(): lax.psum_scatter(sums.reshape(NZ * T, 4 * DH), 'z', scatter_dimension=0,...]
    pallas_call x6, Pallas kernels: 26.4 us -> 22.9 us  [in_vmem(): pl.pallas_call(kernel, in_specs=[pl.BlockSpec(memory_space=pltpu.SMEM)] +...]
    unnamed x65 -> x83, local copies, waits for them, and re-layouts: 4.51 us -> 5.36 us
  transfers between devices with their start and end apart: 37 -> 39, of which waited for: 23 -> 14; matrix products, arithmetic and copies ran while one was open for 4% -> 7% of each run, Pallas kernels for 10% -> 9%
where the time goes in v1:
time: 179 us
  starting transfers between devices  66.1 us (37%)
  waiting for transfers between devices  48.6 us (27%)
  Pallas kernels  30.2 us (17%)
  between operations  14.7 us (8%)
  local copies, waits for them, and re-layouts  12 us (7%)
  other arithmetic  7.23 us (4%)
    ppermute x37, starting transfers between devices, move(): return lax.ppermute(block, AXES, pairs)  66.1 us
    ppermute x37, waiting for transfers between devices, move(): return lax.ppermute(block, AXES, pairs)  35.5 us
    pallas_call x6, Pallas kernels, in_vmem(): pl.pallas_call(kernel, in_specs=[pl.BlockSpec(memory_space=pltpu.SMEM)] +...  22.9 us
    reduce_scatter x1, waiting for transfers between devices, per_device(): lax.psum_scatter(sums.reshape(NZ * T, 4 * DH), 'z', scatter_dimension=0,...  13 us
    pallas_call x1, Pallas kernels, attend(): pl.pallas_call(attend_kernel, in_specs=[pl.BlockSpec(memory_space=pltpu.S...  7.31 us
    unnamed x83, local copies, waits for them, and re-layouts  5.36 us
  transfers between devices with their start and end apart: 39, of which 14 were waited for; matrix products, arithmetic and copies ran while one was open for 7% of the time, Pallas kernels for 9%

profile of v1, /device:TPU:1, one launch (start us, length us, event | category | flops | bytes accessed | tf_op | source)
XLA Modules:
  0.0 178.8 jit_solution(2483207960496388973)
XLA Ops:
  7.3 1.3 fusion.16
  8.6 4.5 %collective-permute-start.12 = (bf16[128,256]{1,0:T(8,128)(2,1)S(1)}, bf16[128,256]{1,0:T(8,128)(2,1)S(1)}, u32[]{:S(2)}, u32[]{:S(2)}) collective-permute-start(bf16[128,256]{1,0:T(8,128)(2,1)S(1)} %pad_maximum_fusion.14), channel_id=1, source_target_pairs={{0,12},{1,13},{2,14},{3,15},{4,8},{5,9},{6,10},{7,11},{8,4},{9,5},... | collective-permute-start | bytes 196616 | tf_op jit(solution)/shard_map/ppermute | solution.py:38
  13.2 1.8 %collective-permute-start.10 = (bf16[128,256]{1,0:T(8,128)(2,1)S(1)}, bf16[128,256]{1,0:T(8,128)(2,1)S(1)}, u32[]{:S(2)}, u32[]{:S(2)}) collective-permute-start(bf16[128,256]{1,0:T(8,128)(2,1)S(1)} %pad_maximum_fusion.12), channel_id=1, source_target_pairs={{0,4},{1,5},{2,6},{3,7},{4,0},{5,1},{6,2},{7,3},{8,12},{9,13},{10,... | collective-permute-start | bytes 196616 | tf_op jit(solution)/shard_map/ppermute | solution.py:38
  15.0 2.8 %collective-permute-done.10 = bf16[128,256]{1,0:T(8,128)(2,1)S(1)} collective-permute-done((bf16[128,256]{1,0:T(8,128)(2,1)S(1)}, bf16[128,256]{1,0:T(8,128)(2,1)S(1)}, u32[]{:S(2)}, u32[]{:S(2)}) %collective-permute-start.10) | collective-permute-done | bytes 65568 | tf_op jit(solution)/shard_map/ppermute | solution.py:38
  19.2 1.1 collective-permute-start.2
  20.7 2.4 %collective-permute-start.1 = (bf16[256,256]{0,1:T(8,128)(2,1)S(1)}, bf16[256,256]{0,1:T(8,128)(2,1)S(1)}, u32[]{:S(2)}, u32[]{:S(2)}) collective-permute-start(bf16[256,256]{0,1:T(8,128)(2,1)S(1)} %bitcast.109), channel_id=1, source_target_pairs={{0,4},{1,5},{2,6},{3,7},{4,0},{5,1},{6,2},{7,3},{8,12},{9,13},{10,... | collective-permute-start | bytes 393224 | tf_op jit(solution)/shard_map/ppermute | solution.py:38
  23.4 0.9 collective-permute-done.2
  24.3 3.0 %collective-permute-done.1 = bf16[256,256]{0,1:T(8,128)(2,1)S(1)} collective-permute-done((bf16[256,256]{0,1:T(8,128)(2,1)S(1)}, bf16[256,256]{0,1:T(8,128)(2,1)S(1)}, u32[]{:S(2)}, u32[]{:S(2)}) %collective-permute-start.1) | collective-permute-done | bytes 131104 | tf_op jit(solution)/shard_map/ppermute | solution.py:38
  27.6 2.6 %collective-permute-start.5 = (bf16[2,2,256,256]{3,2,1,0:T(8,128)(2,1)S(1)}, bf16[2,2,256,256]{3,2,1,0:T(8,128)(2,1)S(1)}, u32[]{:S(2)}, u32[]{:S(2)}) collective-permute-start(bf16[2,2,256,256]{3,2,1,0:T(8,128)(2,1)S(1)} %bitcast.95), channel_id=1, source_target_pairs={{0,3},{1,0},{2,1},{3,2},{4,7},{5,4},{6,5},{7,6},{8,11},{9,8},{10,9... | collective-permute-start | bytes 1572872 | tf_op jit(solution)/shard_map/ppermute | solution.py:38
  31.4 4.1 %collective-permute-start.16 = (bf16[2,3,256,128]{3,2,1,0:T(8,128)(2,1)S(1)}, bf16[2,3,256,128]{3,2,1,0:T(8,128)(2,1)S(1)}, u32[]{:S(2)}, u32[]{:S(2)}) collective-permute-start(bf16[2,3,256,128]{3,2,1,0:T(8,128)(2,1)S(1)} %pad_maximum_fusion.1), channel_id=1, source_target_pairs={{0,8},{1,9},{2,10},{3,11},{4,12},{5,13},{6,14},{7,15},{8,0},{9,1},... | collective-permute-start | bytes 1179656 | tf_op jit(solution)/shard_map/ppermute | solution.py:38
  35.5 3.5 %collective-permute-done.5.refs_3_ = bf16[2,2,256,256]{3,2,1,0:T(8,128)(2,1)S(1)} collective-permute-done((bf16[2,2,256,256]{3,2,1,0:T(8,128)(2,1)S(1)}, bf16[2,2,256,256]{3,2,1,0:T(8,128)(2,1)S(1)}, u32[]{:S(2)}, u32[]{:S(2)}) %collective-permute-start.5) | collective-permute-done | bytes 524320 | tf_op jit(solution)/shard_map/ppermute | solution.py:38
  39.0 14.5 %collective-permute-start.9 = (bf16[2,2,256,256]{3,2,1,0:T(8,128)(2,1)S(1)}, bf16[2,2,256,256]{3,2,1,0:T(8,128)(2,1)S(1)}, u32[]{:S(2)}, u32[]{:S(2)}) collective-permute-start(bf16[2,2,256,256]{3,2,1,0:T(8,128)(2,1)S(1)} %collective-permute-done.5.refs_3_), channel_id=1, source_target_pairs={{0,8},{1,9},{2,10},{3,11},{4,12},{5,13},{6,14},{7,15},{8,0},{9,1},... | collective-permute-start | bytes 1572872 | tf_op jit(solution)/shard_map/ppermute | solution.py:38
  53.6 3.2 %collective-permute-done.3.refs_1_ = bf16[2,2,256,256]{3,2,1,0:T(8,128)(2,1)S(1)} collective-permute-done((bf16[2,2,256,256]{3,2,1,0:T(8,128)(2,1)S(1)}, bf16[2,2,256,256]{3,2,1,0:T(8,128)(2,1)S(1)}, u32[]{:S(2)}, u32[]{:S(2)}) %collective-permute-start.3) | collective-permute-done | bytes 524320 | tf_op jit(solution)/shard_map/ppermute | solution.py:38
  58.8 1.5 collective-permute-start.17
  61.9 6.2 %query_part.1 = (bf16[1024,128]{1,0:T(8,128)(2,1)}, bf16[1024,128]{1,0:T(8,128)(2,1)}, bf16[1024,128]{1,0:T(8,128)(2,1)}, bf16[1024,128]{1,0:T(8,128)(2,1)}) custom-call(s32[23]{0:T(128)} %stack.218.place_ref, bf16[2,2,256,256]{3,2,1,0:T(8,128)(2,1)} %bitcast.99, bf16[2,2,256,256]{3,2,1,0:T(8,128)(2,1)} %copy-done.18, bf16[2,2,256,256]{3,2,1,0:T(8,128)(2,1)} %copy-done.16, ...), custom_call_target="tpu_custom_call" | custom-call | flops 2147483648 | bytes 7340032 | tf_op jit(solution)/shard_map/query_part/pallas_call | solution.py:71
  68.8 1.0 collective-permute-start.14
  69.9 1.5 collective-permute-start.15
  72.3 1.0 maximum_select_fusion
  73.3 1.7 collective-permute-start.19
  75.0 1.7 collective-permute-start.18
  76.8 4.8 %collective-permute-done.19.prev1_ref = bf16[2,256,128]{2,1,0:T(8,128)(2,1)S(1)} collective-permute-done((bf16[2,256,128]{2,1,0:T(8,128)(2,1)S(1)}, bf16[2,256,128]{2,1,0:T(8,128)(2,1)S(1)}, u32[]{:S(2)}, u32[]{:S(2)}) %collective-permute-start.19) | collective-permute-done | bytes 131104 | tf_op jit(solution)/shard_map/ppermute | solution.py:38
  81.6 2.8 %collective-permute-done.18.prev0_ref = bf16[2,256,128]{2,1,0:T(8,128)(2,1)S(1)} collective-permute-done((bf16[2,256,128]{2,1,0:T(8,128)(2,1)S(1)}, bf16[2,256,128]{2,1,0:T(8,128)(2,1)S(1)}, u32[]{:S(2)}, u32[]{:S(2)}) %collective-permute-start.18) | collective-permute-done | bytes 131104 | tf_op jit(solution)/shard_map/ppermute | solution.py:38
  85.9 7.3 %attend.1 = (bf16[4,256,128]{2,1,0:T(8,128)(2,1)}, bf16[1024,128]{1,0:T(8,128)(2,1)}, f32[4,2,256,128]{3,2,1,0:T(8,128)}, bf16[2,2,256,128]{3,2,1,0:T(8,128)(2,1)}) custom-call(s32[23]{0:T(128)} %stack.218.place_ref, bf16[1024,128]{1,0:T(8,128)(2,1)} %get-tuple-element.57.q0_ref, bf16[1024,128]{1,0:T(8,128)(2,1)} %copy-done.35, ...), custom_call_target="tpu_custom_call" | custom-call | flops 1207959552 | bytes 5242880 | tf_op jit(solution)/shard_map/attend/pallas_call | solution.py:249
  94.9 1.6 collective-permute-start.20
  96.5 1.0 slice_bitcast_fusion.4
  97.5 3.9 %collective-permute-start.24 = (bf16[2,256,128]{2,1,0:T(8,128)(2,1)S(1)}, bf16[2,256,128]{2,1,0:T(8,128)(2,1)S(1)}, u32[]{:S(2)}, u32[]{:S(2)}) collective-permute-start(bf16[2,256,128]{2,1,0:T(8,128)(2,1)S(1)} %get-tuple-element.109), channel_id=1, source_target_pairs={{0,224},{1,225},{2,226},{3,227},{4,228},{5,229},{6,230},{7,231},{8... | collective-permute-start | bytes 393224 | tf_op jit(solution)/shard_map/ppermute | solution.py:38
  102.1 1.2 collective-permute-done.24
  103.3 2.9 %collective-permute-done.23 = bf16[2,256,128]{2,1,0:T(8,128)(2,1)S(1)} collective-permute-done((bf16[2,256,128]{2,1,0:T(8,128)(2,1)S(1)}, bf16[2,256,128]{2,1,0:T(8,128)(2,1)S(1)}, u32[]{:S(2)}, u32[]{:S(2)}) %collective-permute-start.23) | collective-permute-done | bytes 131104 | tf_op jit(solution)/shard_map/ppermute | solution.py:38
  106.2 1.2 collective-permute-done.22.refs_3_.refs_11_
  107.5 1.0 copy-done.1
  108.5 5.0 %d_weight_part.1 = bf16[8,256,512]{2,1,0:T(8,128)(2,1)} custom-call(s32[23]{0:T(128)S(1)} %copy-done.13, bf16[2,2,256,256]{3,2,1,0:T(8,128)(2,1)S(1)} %bitcast.100, bf16[2,2,256,256]{3,2,1,0:T(8,128)(2,1)S(1)} %copy-done.19, bf16[2,2,256,256]{3,2,1,0:T(8,128)(2,1)S(1)} %copy-done.17, bf16[2,2,256,256]{3,2,1,0:T(8,128)(2,1)S(1)} %copy-done.15, ...), custom_call_target="tpu_custom_call" | custom-call | flops 2147483648 | bytes 7340032 | tf_op jit(solution)/shard_map/d_weight_part/pallas_call | solution.py:71
  114.2 4.7 %d_hidden_away.1 = bf16[8,2,256,256]{3,2,1,0:T(8,128)(2,1)} custom-call(s32[23]{0:T(128)} %stack.254.place_ref, bf16[1024,128]{1,0:T(8,128)(2,1)} %get-tuple-element.75.refs_0_.refs_8_, bf16[1024,128]{1,0:T(8,128)(2,1)} %copy-done.7, bf16[1024,128]{1,0:T(8,128)(2,1)} %copy-done.5, bf16[1024,128]{1,0:T(8,128)(2,1)} %copy-done.3, bf16[8,256,512]{2,1,0:T(8,128)(2,1)} %bitcast.93), custom_call_target="tpu_custom_call" | custom-call | flops 1073741824 | bytes 5242880 | tf_op jit(solution)/shard_map/d_hidden_away/pallas_call | solution.py:71
  118.9 2.2 %collective-permute-start.27 = (bf16[8,2,256,256]{3,2,1,0:T(8,128)(2,1)}, bf16[8,2,256,256]{3,2,1,0:T(8,128)(2,1)}, u32[]{:S(2)}, u32[]{:S(2)}) collective-permute-start(bf16[8,2,256,256]{3,2,1,0:T(8,128)(2,1)} %d_hidden_away.1), channel_id=1, source_target_pairs={{0,8},{1,9},{2,10},{3,11},{4,12},{5,13},{6,14},{7,15},{8,0},{9,1},... | collective-permute-start | bytes 6291464 | tf_op jit(solution)/shard_map/ppermute | solution.py:38
  121.7 2.3 %fusion.9 = (bf16[2,256,128]{2,1,0:T(8,128)(2,1)}, bf16[2,256,128]{2,1,0:T(8,128)(2,1)S(1)}, bf16[2,256,128]{2,1,0:T(8,128)(2,1)S(1)}, bf16[2,256,128]{2,1,0:T(8,128)(2,1)}) fusion(f32[4,2,256,128]{3,2,1,0:T(8,128)} %get-tuple-element.69, pred[]{:T(512)S(6)} %eq.28, s32[]{:T(128)S(6)} %select_n.188, bf16[1,2,256,128]{3,2,1,0:T(8,128)(2,1)} %bitcast.107, ...), kind=kLoop, calls=%fused_computation.33 | loop fusion | flops 1310720 | bytes 1835018 | tf_op jit(solution)/shard_map/convert_element_type | solution.py:357
  125.2 3.8 %d_hidden_near.1 = (bf16[2,2,256,256]{3,2,1,0:T(8,128)(2,1)S(1)}, bf16[2,2,256,256]{3,2,1,0:T(8,128)(2,1)}, bf16[2,2,256,256]{3,2,1,0:T(8,128)(2,1)}, bf16[2,2,256,256]{3,2,1,0:T(8,128)(2,1)}) custom-call(s32[23]{0:T(128)S(1)} %copy-done.13, bf16[1024,128]{1,0:T(8,128)(2,1)S(1)} %copy-done.2, bf16[1024,128]{1,0:T(8,128)(2,1)S(1)} %copy-done.8, ...), custom_call_target="tpu_custom_call" | custom-call | flops 1073741824 | bytes 7340032 | tf_op jit(solution)/shard_map/d_hidden_near/pallas_call | solution.py:71
  131.3 0.9 maximum_bitcast_fusion
  132.3 3.5 %collective-permute-done.25.y_ref = bf16[2,3,256,128]{3,2,1,0:T(8,128)(2,1)S(1)} collective-permute-done((bf16[2,3,256,128]{3,2,1,0:T(8,128)(2,1)}, bf16[2,3,256,128]{3,2,1,0:T(8,128)(2,1)S(1)}, u32[]{:S(2)}, u32[]{:S(2)}) %collective-permute-start.25) | collective-permute-done | bytes 393248 | tf_op jit(solution)/shard_map/ppermute | solution.py:38
  135.8 1.0 collective-permute-start.26
  136.8 13.0 %reduce-scatter.2.cloned.1.call-done = bf16[256,512]{1,0:T(8,128)(2,1)} async-done(((bf16[2048,512]{1,0:T(8,128)(2,1)}), bf16[256,512]{1,0:T(8,128)(2,1)}) %reduce-scatter.2.cloned.1.call-update) | async-done | bytes 262160 | tf_op jit(solution)/shard_map/reduce_scatter | solution.py:348
  149.8 1.0 fusion.14
  150.8 7.5 %collective-permute-start.36 = (bf16[128,256]{1,0:T(8,128)(2,1)S(1)}, bf16[128,256]{1,0:T(8,128)(2,1)S(1)}, u32[]{:S(2)}, u32[]{:S(2)}) collective-permute-start(bf16[128,256]{1,0:T(8,128)(2,1)S(1)} %get-tuple-element.101), channel_id=1, source_target_pairs={{0,12},{1,13},{2,14},{3,15},{4,8},{5,9},{6,10},{7,11},{8,4},{9,5},... | collective-permute-start | bytes 196616 | tf_op jit(solution)/shard_map/ppermute | solution.py:38
  158.6 0.9 collective-permute-start.33
  159.5 1.1 collective-permute-start.32
  160.7 1.3 collective-permute-start.31
  162.1 1.3 collective-permute-start.35
  163.4 1.6 attended_last.1
  165.0 5.4 %collective-permute-done.35.refs_6_ = bf16[128,256]{1,0:T(8,128)(2,1)S(1)} collective-permute-done((bf16[128,256]{1,0:T(8,128)(2,1)S(1)}, bf16[128,256]{1,0:T(8,128)(2,1)S(1)}, u32[]{:S(2)}, u32[]{:S(2)}) %collective-permute-start.35) | collective-permute-done | bytes 65568 | tf_op jit(solution)/shard_map/ppermute | solution.py:38
  170.3 1.6 last.1
  (161 shorter events, 18.2 us)
Async XLA Ops:
  7.2 53.8 %all-gather.3.cloned.1.call-start = ((), (), s32[]{:S(2)}) async-start(), calls=%async_computation.2 | async-start | bytes 2359296 | tf_op jit(solution)/shard_map/all_gather | solution.py:332
  8.6 6.4 %collective-permute-start.12 = (bf16[128,256]{1,0:T(8,128)(2,1)S(1)}, bf16[128,256]{1,0:T(8,128)(2,1)S(1)}, u32[]{:S(2)}, u32[]{:S(2)}) collective-permute-start(bf16[128,256]{1,0:T(8,128)(2,1)S(1)} %pad_maximum_fusion.14), channel_id=1, source_target_pairs={{0,12},{1,13},{2,14},{3,15},{4,8},{5,9},{6,10},{7,11},{8,4},{9,5},... | collective-permute-start | bytes 196616 | tf_op jit(solution)/shard_map/ppermute | solution.py:38
  13.1 1.9 %collective-permute-start.11 = (bf16[128,256]{1,0:T(8,128)(2,1)S(1)}, bf16[128,256]{1,0:T(8,128)(2,1)S(1)}, u32[]{:S(2)}, u32[]{:S(2)}) collective-permute-start(bf16[128,256]{1,0:T(8,128)(2,1)S(1)} %pad_maximum_fusion.13), channel_id=1, source_target_pairs={{0,8},{1,9},{2,10},{3,11},{4,12},{5,13},{6,14},{7,15},{8,0},{9,1},... | collective-permute-start | bytes 196616 | tf_op jit(solution)/shard_map/ppermute | solution.py:38
  13.2 4.7 %collective-permute-start.10 = (bf16[128,256]{1,0:T(8,128)(2,1)S(1)}, bf16[128,256]{1,0:T(8,128)(2,1)S(1)}, u32[]{:S(2)}, u32[]{:S(2)}) collective-permute-start(bf16[128,256]{1,0:T(8,128)(2,1)S(1)} %pad_maximum_fusion.12), channel_id=1, source_target_pairs={{0,4},{1,5},{2,6},{3,7},{4,0},{5,1},{6,2},{7,3},{8,12},{9,13},{10,... | collective-permute-start | bytes 196616 | tf_op jit(solution)/shard_map/ppermute | solution.py:38
  18.7 131.1 %reduce-scatter.2.cloned.1.call-start = ((), (), s32[]{:S(2)}) async-start(), calls=%async_computation.1 | async-start | bytes 2359296 | tf_op jit(solution)/shard_map/reduce_scatter | solution.py:348
  19.2 5.1 %collective-permute-start.2 = (bf16[256,256]{0,1:T(8,128)(2,1)S(1)}, bf16[256,256]{0,1:T(8,128)(2,1)S(1)}, u32[]{:S(2)}, u32[]{:S(2)}) collective-permute-start(bf16[256,256]{0,1:T(8,128)(2,1)S(1)} %bitcast.111), channel_id=1, source_target_pairs={{0,20},{1,21},{2,22},{3,23},{4,16},{5,17},{6,18},{7,19},{8,28},{9,... | collective-permute-start | bytes 393224 | tf_op jit(solution)/shard_map/ppermute | solution.py:38
  20.3 4.0 %collective-permute-start = (bf16[256,256]{0,1:T(8,128)(2,1)S(1)}, bf16[256,256]{0,1:T(8,128)(2,1)S(1)}, u32[]{:S(2)}, u32[]{:S(2)}) collective-permute-start(bf16[256,256]{0,1:T(8,128)(2,1)S(1)} %bitcast.110), channel_id=1, source_target_pairs={{0,16},{1,17},{2,18},{3,19},{4,20},{5,21},{6,22},{7,23},{8,24},{9,... | collective-permute-start | bytes 393224 | tf_op jit(solution)/shard_map/ppermute | solution.py:38
  20.7 6.6 %collective-permute-start.1 = (bf16[256,256]{0,1:T(8,128)(2,1)S(1)}, bf16[256,256]{0,1:T(8,128)(2,1)S(1)}, u32[]{:S(2)}, u32[]{:S(2)}) collective-permute-start(bf16[256,256]{0,1:T(8,128)(2,1)S(1)} %bitcast.109), channel_id=1, source_target_pairs={{0,4},{1,5},{2,6},{3,7},{4,0},{5,1},{6,2},{7,3},{8,12},{9,13},{10,... | collective-permute-start | bytes 393224 | tf_op jit(solution)/shard_map/ppermute | solution.py:38
  27.6 33.4 %copy-start.11 = (bf16[4,256,256]{2,1,0:T(8,128)(2,1)}, bf16[4,256,256]{2,1,0:T(8,128)(2,1)S(1)}, u32[]{:S(2)}) copy-start(bf16[4,256,256]{2,1,0:T(8,128)(2,1)S(1)} %copy.14) | copy-start | bytes 1572868
  27.6 11.4 %collective-permute-start.5 = (bf16[2,2,256,256]{3,2,1,0:T(8,128)(2,1)S(1)}, bf16[2,2,256,256]{3,2,1,0:T(8,128)(2,1)S(1)}, u32[]{:S(2)}, u32[]{:S(2)}) collective-permute-start(bf16[2,2,256,256]{3,2,1,0:T(8,128)(2,1)S(1)} %bitcast.95), channel_id=1, source_target_pairs={{0,3},{1,0},{2,1},{3,2},{4,7},{5,4},{6,5},{7,6},{8,11},{9,8},{10,9... | collective-permute-start | bytes 1572872 | tf_op jit(solution)/shard_map/ppermute | solution.py:38
  30.1 23.4 %collective-permute-start.4 = (bf16[2,2,256,256]{3,2,1,0:T(8,128)(2,1)S(1)}, bf16[2,2,256,256]{3,2,1,0:T(8,128)(2,1)S(1)}, u32[]{:S(2)}, u32[]{:S(2)}) collective-permute-start(bf16[2,2,256,256]{3,2,1,0:T(8,128)(2,1)S(1)} %bitcast.96), channel_id=1, source_target_pairs={{0,2},{1,3},{2,0},{3,1},{4,6},{5,7},{6,4},{7,5},{8,10},{9,11},{10,... | collective-permute-start | bytes 1572872 | tf_op jit(solution)/shard_map/ppermute | solution.py:38
  30.7 26.2 %collective-permute-start.3 = (bf16[2,2,256,256]{3,2,1,0:T(8,128)(2,1)S(1)}, bf16[2,2,256,256]{3,2,1,0:T(8,128)(2,1)S(1)}, u32[]{:S(2)}, u32[]{:S(2)}) collective-permute-start(bf16[2,2,256,256]{3,2,1,0:T(8,128)(2,1)S(1)} %bitcast.97), channel_id=1, source_target_pairs={{0,1},{1,2},{2,3},{3,0},{4,5},{5,6},{6,7},{7,4},{8,9},{9,10},{10,1... | collective-permute-start | bytes 1572872 | tf_op jit(solution)/shard_map/ppermute | solution.py:38
  31.3 40.0 %copy-start.24 = (bf16[3,256,128]{2,1,0:T(8,128)(2,1)}, bf16[3,256,128]{2,1,0:T(8,128)(2,1)S(1)}, u32[]{:S(2)}) copy-start(bf16[3,256,128]{2,1,0:T(8,128)(2,1)S(1)} %pad_maximum_fusion.6.p0_ref) | copy-start | bytes 589828
  31.4 25.8 %collective-permute-start.16 = (bf16[2,3,256,128]{3,2,1,0:T(8,128)(2,1)S(1)}, bf16[2,3,256,128]{3,2,1,0:T(8,128)(2,1)S(1)}, u32[]{:S(2)}, u32[]{:S(2)}) collective-permute-start(bf16[2,3,256,128]{3,2,1,0:T(8,128)(2,1)S(1)} %pad_maximum_fusion.1), channel_id=1, source_target_pairs={{0,8},{1,9},{2,10},{3,11},{4,12},{5,13},{6,14},{7,15},{8,0},{9,1},... | collective-permute-start | bytes 1179656 | tf_op jit(solution)/shard_map/ppermute | solution.py:38
  35.4 25.4 %collective-permute-start.6 = (bf16[2,2,256,256]{3,2,1,0:T(8,128)(2,1)S(1)}, bf16[2,2,256,256]{3,2,1,0:T(8,128)(2,1)S(1)}, u32[]{:S(2)}, u32[]{:S(2)}) collective-permute-start(bf16[2,2,256,256]{3,2,1,0:T(8,128)(2,1)S(1)} %bitcast.98), channel_id=1, source_target_pairs={{0,8},{1,9},{2,10},{3,11},{4,12},{5,13},{6,14},{7,15},{8,0},{9,1},... | collective-permute-start | bytes 1572872 | tf_op jit(solution)/shard_map/ppermute | solution.py:38
  39.0 21.9 %collective-permute-start.9 = (bf16[2,2,256,256]{3,2,1,0:T(8,128)(2,1)S(1)}, bf16[2,2,256,256]{3,2,1,0:T(8,128)(2,1)S(1)}, u32[]{:S(2)}, u32[]{:S(2)}) collective-permute-start(bf16[2,2,256,256]{3,2,1,0:T(8,128)(2,1)S(1)} %collective-permute-done.5.refs_3_), channel_id=1, source_target_pairs={{0,8},{1,9},{2,10},{3,11},{4,12},{5,13},{6,14},{7,15},{8,0},{9,1},... | collective-permute-start | bytes 1572872 | tf_op jit(solution)/shard_map/ppermute | solution.py:38
  53.6 7.4 %collective-permute-start.8 = (bf16[2,2,256,256]{3,2,1,0:T(8,128)(2,1)S(1)}, bf16[2,2,256,256]{3,2,1,0:T(8,128)(2,1)}, u32[]{:S(2)}, u32[]{:S(2)}) collective-permute-start(bf16[2,2,256,256]{3,2,1,0:T(8,128)(2,1)S(1)} %collective-permute-done.4.refs_2_), channel_id=1, source_target_pairs={{0,8},{1,9},{2,10},{3,11},{4,12},{5,13},{6,14},{7,15},{8,0},{9,1},... | collective-permute-start | bytes 1572872 | tf_op jit(solution)/shard_map/ppermute | solution.py:38
  56.8 4.1 %collective-permute-start.7 = (bf16[2,2,256,256]{3,2,1,0:T(8,128)(2,1)S(1)}, bf16[2,2,256,256]{3,2,1,0:T(8,128)(2,1)}, u32[]{:S(2)}, u32[]{:S(2)}) collective-permute-start(bf16[2,2,256,256]{3,2,1,0:T(8,128)(2,1)S(1)} %collective-permute-done.3.refs_1_), channel_id=1, source_target_pairs={{0,8},{1,9},{2,10},{3,11},{4,12},{5,13},{6,14},{7,15},{8,0},{9,1},... | collective-permute-start | bytes 1572872 | tf_op jit(solution)/shard_map/ppermute | solution.py:38
  58.8 12.5 %collective-permute-start.17 = (bf16[2,3,256,128]{3,2,1,0:T(8,128)(2,1)}, bf16[2,3,256,128]{3,2,1,0:T(8,128)(2,1)}, u32[]{:S(2)}, u32[]{:S(2)}) collective-permute-start(bf16[2,3,256,128]{3,2,1,0:T(8,128)(2,1)} %pad_maximum_fusion.2), channel_id=1, source_target_pairs={{0,16},{1,17},{2,18},{3,19},{4,20},{5,21},{6,22},{7,23},{8,24},{9,... | collective-permute-start | bytes 1179656 | tf_op jit(solution)/shard_map/ppermute | solution.py:38
  68.1 16.3 %collective-permute-start.13 = (bf16[1024,128]{1,0:T(8,128)(2,1)}, bf16[1024,128]{1,0:T(8,128)(2,1)S(1)}, u32[]{:S(2)}, u32[]{:S(2)}) collective-permute-start(bf16[1024,128]{1,0:T(8,128)(2,1)} %get-tuple-element.58), channel_id=1, source_target_pairs={{0,20},{1,21},{2,22},{3,23},{4,16},{5,17},{6,18},{7,19},{8,28},{9,... | collective-permute-start | bytes 786440 | tf_op jit(solution)/shard_map/ppermute | solution.py:38
  68.8 15.6 %collective-permute-start.14 = (bf16[1024,128]{1,0:T(8,128)(2,1)}, bf16[1024,128]{1,0:T(8,128)(2,1)S(1)}, u32[]{:S(2)}, u32[]{:S(2)}) collective-permute-start(bf16[1024,128]{1,0:T(8,128)(2,1)} %get-tuple-element.59), channel_id=1, source_target_pairs={{0,4},{1,5},{2,6},{3,7},{4,0},{5,1},{6,2},{7,3},{8,12},{9,13},{10,... | collective-permute-start | bytes 786440 | tf_op jit(solution)/shard_map/ppermute | solution.py:38
  69.9 14.6 %collective-permute-start.15 = (bf16[1024,128]{1,0:T(8,128)(2,1)}, bf16[1024,128]{1,0:T(8,128)(2,1)S(1)}, u32[]{:S(2)}, u32[]{:S(2)}) collective-permute-start(bf16[1024,128]{1,0:T(8,128)(2,1)} %get-tuple-element.60), channel_id=1, source_target_pairs={{0,16},{1,17},{2,18},{3,19},{4,20},{5,21},{6,22},{7,23},{8,24},{9,... | collective-permute-start | bytes 786440 | tf_op jit(solution)/shard_map/ppermute | solution.py:38
  73.3 8.3 %collective-permute-start.19 = (bf16[2,256,128]{2,1,0:T(8,128)(2,1)S(1)}, bf16[2,256,128]{2,1,0:T(8,128)(2,1)S(1)}, u32[]{:S(2)}, u32[]{:S(2)}) collective-permute-start(bf16[2,256,128]{2,1,0:T(8,128)(2,1)S(1)} %get-tuple-element.111), channel_id=1, source_target_pairs={{0,32},{1,33},{2,34},{3,35},{4,36},{5,37},{6,38},{7,39},{8,40},{9,... | collective-permute-start | bytes 393224 | tf_op jit(solution)/shard_map/ppermute | solution.py:38
  75.0 32.4 %copy-start.12 = (bf16[4,256,256]{2,1,0:T(8,128)(2,1)S(1)}, bf16[4,256,256]{2,1,0:T(8,128)(2,1)}, u32[]{:S(2)}) copy-start(bf16[4,256,256]{2,1,0:T(8,128)(2,1)} %copy-done.11) | copy-start | bytes 1572868
  75.0 32.4 %copy-start.13 = (s32[23]{0:T(128)S(1)}, s32[23]{0:T(128)}, u32[]{:S(2)}) copy-start(s32[23]{0:T(128)} %stack.218.place_ref) | copy-start | bytes 280
  75.0 32.4 %copy-start.15 = (bf16[2,2,256,256]{3,2,1,0:T(8,128)(2,1)S(1)}, bf16[2,2,256,256]{3,2,1,0:T(8,128)(2,1)}, u32[]{:S(2)}) copy-start(bf16[2,2,256,256]{3,2,1,0:T(8,128)(2,1)} %copy-done.14) | copy-start | bytes 1572868
  75.0 32.4 %copy-start.17 = (bf16[2,2,256,256]{3,2,1,0:T(8,128)(2,1)S(1)}, bf16[2,2,256,256]{3,2,1,0:T(8,128)(2,1)}, u32[]{:S(2)}) copy-start(bf16[2,2,256,256]{3,2,1,0:T(8,128)(2,1)} %copy-done.16) | copy-start | bytes 1572868
  75.0 32.4 %copy-start.19 = (bf16[2,2,256,256]{3,2,1,0:T(8,128)(2,1)S(1)}, bf16[2,2,256,256]{3,2,1,0:T(8,128)(2,1)}, u32[]{:S(2)}) copy-start(bf16[2,2,256,256]{3,2,1,0:T(8,128)(2,1)} %copy-done.18) | copy-start | bytes 1572868
  75.0 32.4 %copy-start.21 = (bf16[2,2,256,256]{3,2,1,0:T(8,128)(2,1)S(1)}, bf16[2,2,256,256]{3,2,1,0:T(8,128)(2,1)}, u32[]{:S(2)}) copy-start(bf16[2,2,256,256]{3,2,1,0:T(8,128)(2,1)} %copy-done.20) | copy-start | bytes 1572868
  75.0 32.4 %copy-start.23 = (bf16[2,2,256,256]{3,2,1,0:T(8,128)(2,1)S(1)}, bf16[2,2,256,256]{3,2,1,0:T(8,128)(2,1)}, u32[]{:S(2)}) copy-start(bf16[2,2,256,256]{3,2,1,0:T(8,128)(2,1)} %copy-done.22) | copy-start | bytes 1572868
  75.0 9.4 %collective-permute-start.18 = (bf16[2,256,128]{2,1,0:T(8,128)(2,1)S(1)}, bf16[2,256,128]{2,1,0:T(8,128)(2,1)S(1)}, u32[]{:S(2)}, u32[]{:S(2)}) collective-permute-start(bf16[2,256,128]{2,1,0:T(8,128)(2,1)S(1)} %get-tuple-element.112), channel_id=1, source_target_pairs={{0,32},{1,33},{2,34},{3,35},{4,36},{5,37},{6,38},{7,39},{8,40},{9,... | collective-permute-start | bytes 393224 | tf_op jit(solution)/shard_map/ppermute | solution.py:38
  93.2 14.1 %collective-permute-start.22 = (bf16[1024,128]{1,0:T(8,128)(2,1)}, bf16[1024,128]{1,0:T(8,128)(2,1)S(1)}, u32[]{:S(2)}, u32[]{:S(2)}) collective-permute-start(bf16[1024,128]{1,0:T(8,128)(2,1)} %get-tuple-element.75.refs_0_.refs_8_), channel_id=1, source_target_pairs={{0,20},{1,21},{2,22},{3,23},{4,16},{5,17},{6,18},{7,19},{8,28},{9,... | collective-permute-start | bytes 786440 | tf_op jit(solution)/shard_map/ppermute | solution.py:38
  94.0 13.3 %collective-permute-start.21 = (bf16[1024,128]{1,0:T(8,128)(2,1)}, bf16[1024,128]{1,0:T(8,128)(2,1)S(1)}, u32[]{:S(2)}, u32[]{:S(2)}) collective-permute-start(bf16[1024,128]{1,0:T(8,128)(2,1)} %get-tuple-element.75.refs_0_.refs_8_), channel_id=1, source_target_pairs={{0,4},{1,5},{2,6},{3,7},{4,0},{5,1},{6,2},{7,3},{8,12},{9,13},{10,... | collective-permute-start | bytes 786440 | tf_op jit(solution)/shard_map/ppermute | solution.py:38
  94.9 12.5 %collective-permute-start.20 = (bf16[1024,128]{1,0:T(8,128)(2,1)}, bf16[1024,128]{1,0:T(8,128)(2,1)S(1)}, u32[]{:S(2)}, u32[]{:S(2)}) collective-permute-start(bf16[1024,128]{1,0:T(8,128)(2,1)} %get-tuple-element.75.refs_0_.refs_8_), channel_id=1, source_target_pairs={{0,16},{1,17},{2,18},{3,19},{4,20},{5,21},{6,22},{7,23},{8,24},{9,... | collective-permute-start | bytes 786440 | tf_op jit(solution)/shard_map/ppermute | solution.py:38
  97.5 5.8 %collective-permute-start.24 = (bf16[2,256,128]{2,1,0:T(8,128)(2,1)S(1)}, bf16[2,256,128]{2,1,0:T(8,128)(2,1)S(1)}, u32[]{:S(2)}, u32[]{:S(2)}) collective-permute-start(bf16[2,256,128]{2,1,0:T(8,128)(2,1)S(1)} %get-tuple-element.109), channel_id=1, source_target_pairs={{0,224},{1,225},{2,226},{3,227},{4,228},{5,229},{6,230},{7,231},{8... | collective-permute-start | bytes 393224 | tf_op jit(solution)/shard_map/ppermute | solution.py:38
  101.4 4.8 %collective-permute-start.23 = (bf16[2,256,128]{2,1,0:T(8,128)(2,1)S(1)}, bf16[2,256,128]{2,1,0:T(8,128)(2,1)S(1)}, u32[]{:S(2)}, u32[]{:S(2)}) collective-permute-start(bf16[2,256,128]{2,1,0:T(8,128)(2,1)S(1)} %get-tuple-element.110), channel_id=1, source_target_pairs={{0,224},{1,225},{2,226},{3,227},{4,228},{5,229},{6,230},{7,231},{8... | collective-permute-start | bytes 393224 | tf_op jit(solution)/shard_map/ppermute | solution.py:38
  118.9 6.3 %collective-permute-start.27 = (bf16[8,2,256,256]{3,2,1,0:T(8,128)(2,1)}, bf16[8,2,256,256]{3,2,1,0:T(8,128)(2,1)}, u32[]{:S(2)}, u32[]{:S(2)}) collective-permute-start(bf16[8,2,256,256]{3,2,1,0:T(8,128)(2,1)} %d_hidden_away.1), channel_id=1, source_target_pairs={{0,8},{1,9},{2,10},{3,11},{4,12},{5,13},{6,14},{7,15},{8,0},{9,1},... | collective-permute-start | bytes 6291464 | tf_op jit(solution)/shard_map/ppermute | solution.py:38
  124.9 10.8 %collective-permute-start.25 = (bf16[2,3,256,128]{3,2,1,0:T(8,128)(2,1)}, bf16[2,3,256,128]{3,2,1,0:T(8,128)(2,1)S(1)}, u32[]{:S(2)}, u32[]{:S(2)}) collective-permute-start(bf16[2,3,256,128]{3,2,1,0:T(8,128)(2,1)} %pad_maximum_fusion.3), channel_id=1, source_target_pairs={{0,16},{1,17},{2,18},{3,19},{4,20},{5,21},{6,22},{7,23},{8,24},{9,... | collective-permute-start | bytes 1179656 | tf_op jit(solution)/shard_map/ppermute | solution.py:38
  129.9 28.4 %collective-permute-start.28 = (bf16[2,2,256,256]{3,2,1,0:T(8,128)(2,1)}, bf16[2,2,256,256]{3,2,1,0:T(8,128)(2,1)S(1)}, u32[]{:S(2)}, u32[]{:S(2)}) collective-permute-start(bf16[2,2,256,256]{3,2,1,0:T(8,128)(2,1)} %get-tuple-element.80), channel_id=1, source_target_pairs={{0,3},{1,0},{2,1},{3,2},{4,7},{5,4},{6,5},{7,6},{8,11},{9,8},{10,9... | collective-permute-start | bytes 1572872 | tf_op jit(solution)/shard_map/ppermute | solution.py:38
  130.3 28.0 %collective-permute-start.29 = (bf16[2,2,256,256]{3,2,1,0:T(8,128)(2,1)}, bf16[2,2,256,256]{3,2,1,0:T(8,128)(2,1)S(1)}, u32[]{:S(2)}, u32[]{:S(2)}) collective-permute-start(bf16[2,2,256,256]{3,2,1,0:T(8,128)(2,1)} %get-tuple-element.81), channel_id=1, source_target_pairs={{0,2},{1,3},{2,0},{3,1},{4,6},{5,7},{6,4},{7,5},{8,10},{9,11},{10,... | collective-permute-start | bytes 1572872 | tf_op jit(solution)/shard_map/ppermute | solution.py:38
  130.6 27.6 %collective-permute-start.30 = (bf16[2,2,256,256]{3,2,1,0:T(8,128)(2,1)}, bf16[2,2,256,256]{3,2,1,0:T(8,128)(2,1)S(1)}, u32[]{:S(2)}, u32[]{:S(2)}) collective-permute-start(bf16[2,2,256,256]{3,2,1,0:T(8,128)(2,1)} %get-tuple-element.82), channel_id=1, source_target_pairs={{0,1},{1,2},{2,3},{3,0},{4,5},{5,6},{6,7},{7,4},{8,9},{9,10},{10,1... | collective-permute-start | bytes 1572872 | tf_op jit(solution)/shard_map/ppermute | solution.py:38
  135.8 26.1 %collective-permute-start.26 = (bf16[2,3,256,128]{3,2,1,0:T(8,128)(2,1)S(1)}, bf16[2,3,256,128]{3,2,1,0:T(8,128)(2,1)S(1)}, u32[]{:S(2)}, u32[]{:S(2)}) collective-permute-start(bf16[2,3,256,128]{3,2,1,0:T(8,128)(2,1)S(1)} %pad_maximum_fusion.4), channel_id=1, source_target_pairs={{0,8},{1,9},{2,10},{3,11},{4,12},{5,13},{6,14},{7,15},{8,0},{9,1},... | collective-permute-start | bytes 1179656 | tf_op jit(solution)/shard_map/ppermute | solution.py:38
  150.8 11.3 %collective-permute-start.36 = (bf16[128,256]{1,0:T(8,128)(2,1)S(1)}, bf16[128,256]{1,0:T(8,128)(2,1)S(1)}, u32[]{:S(2)}, u32[]{:S(2)}) collective-permute-start(bf16[128,256]{1,0:T(8,128)(2,1)S(1)} %get-tuple-element.101), channel_id=1, source_target_pairs={{0,12},{1,13},{2,14},{3,15},{4,8},{5,9},{6,10},{7,11},{8,4},{9,5},... | collective-permute-start | bytes 196616 | tf_op jit(solution)/shard_map/ppermute | solution.py:38
  158.6 11.7 %collective-permute-start.33 = (bf16[256,256]{1,0:T(8,128)(2,1)S(1)}, bf16[256,256]{1,0:T(8,128)(2,1)S(1)}, u32[]{:S(2)}, u32[]{:S(2)}) collective-permute-start(bf16[256,256]{1,0:T(8,128)(2,1)S(1)} %get-tuple-element.95), channel_id=1, source_target_pairs={{0,20},{1,21},{2,22},{3,23},{4,16},{5,17},{6,18},{7,19},{8,28},{9,... | collective-permute-start | bytes 393224 | tf_op jit(solution)/shard_map/ppermute | solution.py:38
  159.5 10.8 %collective-permute-start.32 = (bf16[256,256]{1,0:T(8,128)(2,1)S(1)}, bf16[256,256]{1,0:T(8,128)(2,1)S(1)}, u32[]{:S(2)}, u32[]{:S(2)}) collective-permute-start(bf16[256,256]{1,0:T(8,128)(2,1)S(1)} %get-tuple-element.96), channel_id=1, source_target_pairs={{0,4},{1,5},{2,6},{3,7},{4,0},{5,1},{6,2},{7,3},{8,12},{9,13},{10,... | collective-permute-start | bytes 393224 | tf_op jit(solution)/shard_map/ppermute | solution.py:38
  160.7 9.6 %collective-permute-start.31 = (bf16[256,256]{1,0:T(8,128)(2,1)S(1)}, bf16[256,256]{1,0:T(8,128)(2,1)S(1)}, u32[]{:S(2)}, u32[]{:S(2)}) collective-permute-start(bf16[256,256]{1,0:T(8,128)(2,1)S(1)} %get-tuple-element.97), channel_id=1, source_target_pairs={{0,16},{1,17},{2,18},{3,19},{4,20},{5,21},{6,22},{7,23},{8,24},{9,... | collective-permute-start | bytes 393224 | tf_op jit(solution)/shard_map/ppermute | solution.py:38
  162.0 3.0 %collective-permute-start.34 = (bf16[128,256]{1,0:T(8,128)(2,1)S(1)}, bf16[128,256]{1,0:T(8,128)(2,1)S(1)}, u32[]{:S(2)}, u32[]{:S(2)}) collective-permute-start(bf16[128,256]{1,0:T(8,128)(2,1)S(1)} %get-tuple-element.102), channel_id=1, source_target_pairs={{0,8},{1,9},{2,10},{3,11},{4,12},{5,13},{6,14},{7,15},{8,0},{9,1},... | collective-permute-start | bytes 196616 | tf_op jit(solution)/shard_map/ppermute | solution.py:38
  162.1 8.2 %collective-permute-start.35 = (bf16[128,256]{1,0:T(8,128)(2,1)S(1)}, bf16[128,256]{1,0:T(8,128)(2,1)S(1)}, u32[]{:S(2)}, u32[]{:S(2)}) collective-permute-start(bf16[128,256]{1,0:T(8,128)(2,1)S(1)} %get-tuple-element.104), channel_id=1, source_target_pairs={{0,4},{1,5},{2,6},{3,7},{4,0},{5,1},{6,2},{7,3},{8,12},{9,13},{10,... | collective-permute-start | bytes 196616 | tf_op jit(solution)/shard_map/ppermute | solution.py:38
  (31 other events, 214.3 us)
Sparse Core Ops, SparseCore 0:
  18.8 39.3 all-gather.2
  113.7 36.0 reduce-scatter.1

commit v2 on v1

--- a/solution.py
+++ b/solution.py
@@ -82,7 +82,7 @@
 def query_part(place, own, other, weights):
     work = cost(2 * 1024 * 2048 * 512, 7 << 20)
     outs = [((4 * T, DH), BF)] * 4
-    return in_vmem(query_kernel, "query_part", work, outs, place, *own, *other, weights, room=56)
+    return in_vmem(query_kernel, "query_part", work, outs, place, *own, *other, weights, room=20)
 
 
 def d_hidden_block(place_ref, refs, dl, i):
@@ -107,7 +107,7 @@
 def d_hidden_away(place, dq, weights):
     work = cost(1024 * 2048 * 512, 5 << 20)
     outs = [((8, 2, T, T), BF)]
-    return in_vmem(d_hidden_away_kernel, "d_hidden_away", work, outs, place, *dq, weights, room=56)[0]
+    return in_vmem(d_hidden_away_kernel, "d_hidden_away", work, outs, place, *dq, weights, room=20)[0]
 
 
 def d_hidden_near(place, dq, weights, away):
@@ -264,7 +264,7 @@
             pltpu.VMEM((W + n, DH), F32),
             pltpu.VMEM((W + n, DH), F32),
         ],
-        compiler_params=params(56),
+        compiler_params=params(20),
         cost_estimate=cost(12 * n * 768 * DH, 5 << 20, n * W),
         name="attend",
     )(place, *parts, *pieces, *prev)

time: 179 us -> 173 us (0.966)
  Pallas kernels: 30.2 us -> 23.3 us
  waiting for transfers between devices: 48.6 us -> 44.1 us
  starting transfers between devices: 66.1 us -> 69.3 us
    pallas_call x6, Pallas kernels: 22.9 us -> 18.1 us  [in_vmem(): pl.pallas_call(kernel, in_specs=[pl.BlockSpec(memory_space=pltpu.SMEM)] +...]
    ppermute x37, starting transfers between devices: 66.1 us -> 69.2 us  [move(): return lax.ppermute(block, AXES, pairs)]
    ppermute x37, waiting for transfers between devices: 35.5 us -> 32.4 us  [move(): return lax.ppermute(block, AXES, pairs)]
    unnamed x83 -> x51, local copies, waits for them, and re-layouts: 5.36 us -> 7.59 us
    pallas_call x1, Pallas kernels: 7.31 us -> 5.15 us  [attend(): pl.pallas_call(attend_kernel, in_specs=[pl.BlockSpec(memory_space=pltpu.S...]
  transfers between devices with their start and end apart: 39 -> 39, of which waited for: 14 -> 14; matrix products, arithmetic and copies ran while one was open for 7% -> 6% of each run, Pallas kernels for 9% -> 7%
where the time goes in v2:
time: 173 us; the launch traced here: 172 us
  starting transfers between devices  69.3 us (40%)
  waiting for transfers between devices  44.1 us (25%)
  Pallas kernels  23.3 us (13%)
  between operations  14.6 us (8%)
  local copies, waits for them, and re-layouts  12.9 us (7%)
  other arithmetic  7.55 us (4%)
    ppermute x37, starting transfers between devices, move(): return lax.ppermute(block, AXES, pairs)  69.2 us
    ppermute x37, waiting for transfers between devices, move(): return lax.ppermute(block, AXES, pairs)  32.4 us
    pallas_call x6, Pallas kernels, in_vmem(): pl.pallas_call(kernel, in_specs=[pl.BlockSpec(memory_space=pltpu.SMEM)] +...  18.1 us
    reduce_scatter x1, waiting for transfers between devices, per_device(): lax.psum_scatter(sums.reshape(NZ * T, 4 * DH), 'z', scatter_dimension=0,...  11.6 us
    unnamed x51, local copies, waits for them, and re-layouts  7.59 us
    pallas_call x1, Pallas kernels, attend(): pl.pallas_call(attend_kernel, in_specs=[pl.BlockSpec(memory_space=pltpu.S...  5.15 us
  transfers between devices with their start and end apart: 39, of which 14 were waited for; matrix products, arithmetic and copies ran while one was open for 6% of the time, Pallas kernels for 7%

profile of v2, /device:TPU:1, one launch (start us, length us, event | category | flops | bytes accessed | tf_op | source)
XLA Modules:
  0.0 171.7 jit_solution(4824536237638171790)
XLA Ops:
  7.3 1.3 fusion.16
  8.6 4.5 %collective-permute-start.12 = (bf16[128,256]{1,0:T(8,128)(2,1)S(1)}, bf16[128,256]{1,0:T(8,128)(2,1)S(1)}, u32[]{:S(2)}, u32[]{:S(2)}) collective-permute-start(bf16[128,256]{1,0:T(8,128)(2,1)S(1)} %pad_maximum_fusion.14), channel_id=1, source_target_pairs={{0,12},{1,13},{2,14},{3,15},{4,8},{5,9},{6,10},{7,11},{8,4},{9,5},... | collective-permute-start | bytes 196616 | tf_op jit(solution)/shard_map/ppermute | solution.py:38
  13.2 1.8 %collective-permute-start.10 = (bf16[128,256]{1,0:T(8,128)(2,1)S(1)}, bf16[128,256]{1,0:T(8,128)(2,1)S(1)}, u32[]{:S(2)}, u32[]{:S(2)}) collective-permute-start(bf16[128,256]{1,0:T(8,128)(2,1)S(1)} %pad_maximum_fusion.12), channel_id=1, source_target_pairs={{0,4},{1,5},{2,6},{3,7},{4,0},{5,1},{6,2},{7,3},{8,12},{9,13},{10,... | collective-permute-start | bytes 196616 | tf_op jit(solution)/shard_map/ppermute | solution.py:38
  15.0 2.8 %collective-permute-done.10 = bf16[128,256]{1,0:T(8,128)(2,1)S(1)} collective-permute-done((bf16[128,256]{1,0:T(8,128)(2,1)S(1)}, bf16[128,256]{1,0:T(8,128)(2,1)S(1)}, u32[]{:S(2)}, u32[]{:S(2)}) %collective-permute-start.10) | collective-permute-done | bytes 65568 | tf_op jit(solution)/shard_map/ppermute | solution.py:38
  19.2 1.1 collective-permute-start.2
  20.7 2.4 %collective-permute-start.1 = (bf16[256,256]{0,1:T(8,128)(2,1)S(1)}, bf16[256,256]{0,1:T(8,128)(2,1)S(1)}, u32[]{:S(2)}, u32[]{:S(2)}) collective-permute-start(bf16[256,256]{0,1:T(8,128)(2,1)S(1)} %bitcast.110), channel_id=1, source_target_pairs={{0,4},{1,5},{2,6},{3,7},{4,0},{5,1},{6,2},{7,3},{8,12},{9,13},{10,... | collective-permute-start | bytes 393224 | tf_op jit(solution)/shard_map/ppermute | solution.py:38
  24.3 3.0 %collective-permute-done.1 = bf16[256,256]{0,1:T(8,128)(2,1)S(1)} collective-permute-done((bf16[256,256]{0,1:T(8,128)(2,1)S(1)}, bf16[256,256]{0,1:T(8,128)(2,1)S(1)}, u32[]{:S(2)}, u32[]{:S(2)}) %collective-permute-start.1) | collective-permute-done | bytes 131104 | tf_op jit(solution)/shard_map/ppermute | solution.py:38
  27.6 2.6 %collective-permute-start.5 = (bf16[2,2,256,256]{3,2,1,0:T(8,128)(2,1)S(1)}, bf16[2,2,256,256]{3,2,1,0:T(8,128)(2,1)S(1)}, u32[]{:S(2)}, u32[]{:S(2)}) collective-permute-start(bf16[2,2,256,256]{3,2,1,0:T(8,128)(2,1)S(1)} %bitcast.96), channel_id=1, source_target_pairs={{0,3},{1,0},{2,1},{3,2},{4,7},{5,4},{6,5},{7,6},{8,11},{9,8},{10,9... | collective-permute-start | bytes 1572872 | tf_op jit(solution)/shard_map/ppermute | solution.py:38
  32.2 4.1 %collective-permute-start.16 = (bf16[2,3,256,128]{3,2,1,0:T(8,128)(2,1)S(1)}, bf16[2,3,256,128]{3,2,1,0:T(8,128)(2,1)S(1)}, u32[]{:S(2)}, u32[]{:S(2)}) collective-permute-start(bf16[2,3,256,128]{3,2,1,0:T(8,128)(2,1)S(1)} %pad_maximum_fusion.1), channel_id=1, source_target_pairs={{0,8},{1,9},{2,10},{3,11},{4,12},{5,13},{6,14},{7,15},{8,0},{9,1},... | collective-permute-start | bytes 1179656 | tf_op jit(solution)/shard_map/ppermute | solution.py:38
  36.4 2.7 %collective-permute-done.5.refs_3_ = bf16[2,2,256,256]{3,2,1,0:T(8,128)(2,1)S(1)} collective-permute-done((bf16[2,2,256,256]{3,2,1,0:T(8,128)(2,1)S(1)}, bf16[2,2,256,256]{3,2,1,0:T(8,128)(2,1)S(1)}, u32[]{:S(2)}, u32[]{:S(2)}) %collective-permute-start.5) | collective-permute-done | bytes 524320 | tf_op jit(solution)/shard_map/ppermute | solution.py:38
  39.0 14.5 %collective-permute-start.9 = (bf16[2,2,256,256]{3,2,1,0:T(8,128)(2,1)S(1)}, bf16[2,2,256,256]{3,2,1,0:T(8,128)(2,1)}, u32[]{:S(2)}, u32[]{:S(2)}) collective-permute-start(bf16[2,2,256,256]{3,2,1,0:T(8,128)(2,1)S(1)} %collective-permute-done.5.refs_3_), channel_id=1, source_target_pairs={{0,8},{1,9},{2,10},{3,11},{4,12},{5,13},{6,14},{7,15},{8,0},{9,1},... | collective-permute-start | bytes 1572872 | tf_op jit(solution)/shard_map/ppermute | solution.py:38
  53.6 3.2 %collective-permute-done.3.refs_1_ = bf16[2,2,256,256]{3,2,1,0:T(8,128)(2,1)S(1)} collective-permute-done((bf16[2,2,256,256]{3,2,1,0:T(8,128)(2,1)S(1)}, bf16[2,2,256,256]{3,2,1,0:T(8,128)(2,1)S(1)}, u32[]{:S(2)}, u32[]{:S(2)}) %collective-permute-start.3) | collective-permute-done | bytes 524320 | tf_op jit(solution)/shard_map/ppermute | solution.py:38
  58.0 1.5 collective-permute-start.17
  59.6 1.6 copy-done
  61.2 3.9 %query_part.1 = (bf16[1024,128]{1,0:T(8,128)(2,1)S(1)}, bf16[1024,128]{1,0:T(8,128)(2,1)S(1)}, bf16[1024,128]{1,0:T(8,128)(2,1)S(1)}, bf16[1024,128]{1,0:T(8,128)(2,1)S(1)}) custom-call(s32[23]{0:T(128)S(1)} %stack.218.place_ref, bf16[2,2,256,256]{3,2,1,0:T(8,128)(2,1)S(1)} %bitcast.100, bf16[2,2,256,256]{3,2,1,0:T(8,128)(2,1)S(1)} %collective-permute-done.3.refs_1_, ...), custom_call_target="tpu_custom_call" | custom-call | flops 2147483648 | bytes 7340032 | tf_op jit(solution)/shard_map/query_part/pallas_call | solution.py:71
  65.1 1.3 collective-permute-start.13
  66.4 1.4 collective-permute-start.14
  68.9 1.7 %collective-permute-start.19 = (bf16[2,256,128]{2,1,0:T(8,128)(2,1)S(1)}, bf16[2,256,128]{2,1,0:T(8,128)(2,1)S(1)}, u32[]{:S(2)}, u32[]{:S(2)}) collective-permute-start(bf16[2,256,128]{2,1,0:T(8,128)(2,1)S(1)} %get-tuple-element.111), channel_id=1, source_target_pairs={{0,32},{1,33},{2,34},{3,35},{4,36},{5,37},{6,38},{7,39},{8,40},{9,... | collective-permute-start | bytes 393224 | tf_op jit(solution)/shard_map/ppermute | solution.py:38
  70.6 1.6 collective-permute-start.18
  72.3 5.1 %collective-permute-done.19.prev1_ref = bf16[2,256,128]{2,1,0:T(8,128)(2,1)S(1)} collective-permute-done((bf16[2,256,128]{2,1,0:T(8,128)(2,1)S(1)}, bf16[2,256,128]{2,1,0:T(8,128)(2,1)S(1)}, u32[]{:S(2)}, u32[]{:S(2)}) %collective-permute-start.19) | collective-permute-done | bytes 131104 | tf_op jit(solution)/shard_map/ppermute | solution.py:38
  77.3 2.8 %collective-permute-done.18.prev0_ref = bf16[2,256,128]{2,1,0:T(8,128)(2,1)S(1)} collective-permute-done((bf16[2,256,128]{2,1,0:T(8,128)(2,1)S(1)}, bf16[2,256,128]{2,1,0:T(8,128)(2,1)S(1)}, u32[]{:S(2)}, u32[]{:S(2)}) %collective-permute-start.18) | collective-permute-done | bytes 131104 | tf_op jit(solution)/shard_map/ppermute | solution.py:38
  80.2 5.2 %attend.1 = (bf16[4,256,128]{2,1,0:T(8,128)(2,1)S(1)}, bf16[1024,128]{1,0:T(8,128)(2,1)S(1)}, f32[4,2,256,128]{3,2,1,0:T(8,128)S(1)}, bf16[2,2,256,128]{3,2,1,0:T(8,128)(2,1)S(1)}) custom-call(s32[23]{0:T(128)S(1)} %stack.218.place_ref, bf16[1024,128]{1,0:T(8,128)(2,1)S(1)} %get-tuple-element.57.q0_ref, ...), custom_call_target="tpu_custom_call" | custom-call | flops 1207959552 | bytes 5242880 | tf_op jit(solution)/shard_map/attend/pallas_call | solution.py:249
  85.4 3.2 %collective-permute-start.21 = (bf16[1024,128]{1,0:T(8,128)(2,1)S(1)}, bf16[1024,128]{1,0:T(8,128)(2,1)S(1)}, u32[]{:S(2)}, u32[]{:S(2)}) collective-permute-start(bf16[1024,128]{1,0:T(8,128)(2,1)S(1)} %get-tuple-element.75.refs_0_.refs_8_), channel_id=1, source_target_pairs={{0,4},{1,5},{2,6},{3,7},{4,0},{5,1},{6,2},{7,3},{8,12},{9,13},{10,... | collective-permute-start | bytes 786440 | tf_op jit(solution)/shard_map/ppermute | solution.py:38
  88.7 5.5 %collective-permute-start.24 = (bf16[2,256,128]{2,1,0:T(8,128)(2,1)S(1)}, bf16[2,256,128]{2,1,0:T(8,128)(2,1)S(1)}, u32[]{:S(2)}, u32[]{:S(2)}) collective-permute-start(bf16[2,256,128]{2,1,0:T(8,128)(2,1)S(1)} %get-tuple-element.109), channel_id=1, source_target_pairs={{0,224},{1,225},{2,226},{3,227},{4,228},{5,229},{6,230},{7,231},{8... | collective-permute-start | bytes 393224 | tf_op jit(solution)/shard_map/ppermute | solution.py:38
  94.9 1.2 collective-permute-done.24
  96.1 2.2 %collective-permute-done.23 = bf16[2,256,128]{2,1,0:T(8,128)(2,1)S(1)} collective-permute-done((bf16[2,256,128]{2,1,0:T(8,128)(2,1)S(1)}, bf16[2,256,128]{2,1,0:T(8,128)(2,1)S(1)}, u32[]{:S(2)}, u32[]{:S(2)}) %collective-permute-start.23) | collective-permute-done | bytes 131104 | tf_op jit(solution)/shard_map/ppermute | solution.py:38
  98.3 1.6 collective-permute-done.22.refs_3_.refs_11_
  100.0 4.1 %d_weight_part.1 = bf16[8,256,512]{2,1,0:T(8,128)(2,1)S(1)} custom-call(s32[23]{0:T(128)S(1)} %stack.218.place_ref, bf16[2,2,256,256]{3,2,1,0:T(8,128)(2,1)S(1)} %bitcast.101, bf16[2,2,256,256]{3,2,1,0:T(8,128)(2,1)S(1)} %copy-done.16, bf16[2,2,256,256]{3,2,1,0:T(8,128)(2,1)S(1)} %copy-done.14, bf16[2,2,256,256]{3,2,1,0:T(8,128)(2,1)S(1)} %collective-permute-done.5.refs_3_, ...), custom_call_target="tpu_custom_call" | custom-call | flops 2147483648 | bytes 7340032 | tf_op jit(solution)/shard_map/d_weight_part/pallas_call | solution.py:71
  104.2 1.3 copy-done.2
  105.6 1.5 copy-done.1
  108.1 0.9 copy-done.7
  110.0 3.2 %d_hidden_away.1 = bf16[8,2,256,256]{3,2,1,0:T(8,128)(2,1)} custom-call(s32[23]{0:T(128)S(1)} %stack.254.place_ref, bf16[1024,128]{1,0:T(8,128)(2,1)S(1)} %get-tuple-element.75.refs_0_.refs_8_, bf16[1024,128]{1,0:T(8,128)(2,1)S(1)} %copy-done.10, bf16[1024,128]{1,0:T(8,128)(2,1)S(1)} %copy-done.7, bf16[1024,128]{1,0:T(8,128)(2,1)S(1)} %copy-done.4, ...), custom_call_target="tpu_custom_call" | custom-call | flops 1073741824 | bytes 5242880 | tf_op jit(solution)/shard_map/d_hidden_away/pallas_call | solution.py:71
  113.1 1.9 %collective-permute-start.27 = (bf16[8,2,256,256]{3,2,1,0:T(8,128)(2,1)}, bf16[8,2,256,256]{3,2,1,0:T(8,128)(2,1)}, u32[]{:S(2)}, u32[]{:S(2)}) collective-permute-start(bf16[8,2,256,256]{3,2,1,0:T(8,128)(2,1)} %d_hidden_away.1), channel_id=1, source_target_pairs={{0,8},{1,9},{2,10},{3,11},{4,12},{5,13},{6,14},{7,15},{8,0},{9,1},... | collective-permute-start | bytes 6291464 | tf_op jit(solution)/shard_map/ppermute | solution.py:38
  115.1 1.7 fusion.15
  116.8 2.1 %fusion.9 = (bf16[2,256,128]{2,1,0:T(8,128)(2,1)}, bf16[2,256,128]{2,1,0:T(8,128)(2,1)S(1)}, bf16[2,256,128]{2,1,0:T(8,128)(2,1)S(1)}, bf16[2,256,128]{2,1,0:T(8,128)(2,1)S(1)}) fusion(f32[4,2,256,128]{3,2,1,0:T(8,128)S(1)} %get-tuple-element.69, pred[]{:T(512)S(6)} %eq.28, s32[]{:T(128)S(6)} %select_n.188, bf16[1,2,256,128]{3,2,1,0:T(8,128)(2,1)} %bitcast.108, ...), kind=kLoop, calls=%fused_computation.33 | loop fusion | flops 1310720 | bytes 1835018 | tf_op jit(solution)/shard_map/convert_element_type | solution.py:357
  119.7 1.0 collective-permute-start.25
  120.7 3.8 %d_hidden_near.1 = (bf16[2,2,256,256]{3,2,1,0:T(8,128)(2,1)S(1)}, bf16[2,2,256,256]{3,2,1,0:T(8,128)(2,1)}, bf16[2,2,256,256]{3,2,1,0:T(8,128)(2,1)}, bf16[2,2,256,256]{3,2,1,0:T(8,128)(2,1)}) custom-call(s32[23]{0:T(128)S(1)} %stack.218.place_ref, bf16[1024,128]{1,0:T(8,128)(2,1)S(1)} %get-tuple-element.75.refs_0_.refs_8_, ...), custom_call_target="tpu_custom_call" | custom-call | flops 1073741824 | bytes 7340032 | tf_op jit(solution)/shard_map/d_hidden_near/pallas_call | solution.py:71
  126.9 3.8 %collective-permute-done.25.y_ref = bf16[2,3,256,128]{3,2,1,0:T(8,128)(2,1)S(1)} collective-permute-done((bf16[2,3,256,128]{3,2,1,0:T(8,128)(2,1)}, bf16[2,3,256,128]{3,2,1,0:T(8,128)(2,1)S(1)}, u32[]{:S(2)}, u32[]{:S(2)}) %collective-permute-start.25) | collective-permute-done | bytes 393248 | tf_op jit(solution)/shard_map/ppermute | solution.py:38
  132.3 11.6 %reduce-scatter.2.cloned.1.call-done = bf16[256,512]{1,0:T(8,128)(2,1)} async-done(((bf16[2048,512]{1,0:T(8,128)(2,1)}), bf16[256,512]{1,0:T(8,128)(2,1)}) %reduce-scatter.2.cloned.1.call-update) | async-done | bytes 262160 | tf_op jit(solution)/shard_map/reduce_scatter | solution.py:348
  143.8 1.0 fusion.14
  144.8 7.4 %collective-permute-start.36 = (bf16[128,256]{1,0:T(8,128)(2,1)S(1)}, bf16[128,256]{1,0:T(8,128)(2,1)S(1)}, u32[]{:S(2)}, u32[]{:S(2)}) collective-permute-start(bf16[128,256]{1,0:T(8,128)(2,1)S(1)} %get-tuple-element.101), channel_id=1, source_target_pairs={{0,12},{1,13},{2,14},{3,15},{4,8},{5,9},{6,10},{7,11},{8,4},{9,5},... | collective-permute-start | bytes 196616 | tf_op jit(solution)/shard_map/ppermute | solution.py:38
  153.4 1.2 collective-permute-start.32
  154.6 1.2 collective-permute-start.31
  155.8 1.3 collective-permute-start.34
  157.2 1.0 collective-permute-start.35
  158.2 1.6 attended_last.1
  159.7 3.5 %collective-permute-done.35.refs_6_ = bf16[128,256]{1,0:T(8,128)(2,1)S(1)} collective-permute-done((bf16[128,256]{1,0:T(8,128)(2,1)S(1)}, bf16[128,256]{1,0:T(8,128)(2,1)S(1)}, u32[]{:S(2)}, u32[]{:S(2)}) %collective-permute-start.35) | collective-permute-done | bytes 65568 | tf_op jit(solution)/shard_map/ppermute | solution.py:38
  163.3 1.6 last.1
  (129 shorter events, 16.8 us)
Async XLA Ops:
  7.2 11.6 %copy-start.17 = (bf16[256,1024]{1,0:T(8,128)(2,1)S(1)}, bf16[256,1024]{1,0:T(8,128)(2,1)}, u32[]{:S(2)}) copy-start(bf16[256,1024]{1,0:T(8,128)(2,1)} %param.5) | copy-start | bytes 1572868
  7.2 52.4 %all-gather.3.cloned.1.call-start = ((), (), s32[]{:S(2)}) async-start(), calls=%async_computation.2 | async-start | bytes 2359296 | tf_op jit(solution)/shard_map/all_gather | solution.py:332
  8.6 6.4 %collective-permute-start.12 = (bf16[128,256]{1,0:T(8,128)(2,1)S(1)}, bf16[128,256]{1,0:T(8,128)(2,1)S(1)}, u32[]{:S(2)}, u32[]{:S(2)}) collective-permute-start(bf16[128,256]{1,0:T(8,128)(2,1)S(1)} %pad_maximum_fusion.14), channel_id=1, source_target_pairs={{0,12},{1,13},{2,14},{3,15},{4,8},{5,9},{6,10},{7,11},{8,4},{9,5},... | collective-permute-start | bytes 196616 | tf_op jit(solution)/shard_map/ppermute | solution.py:38
  13.1 1.9 %collective-permute-start.11 = (bf16[128,256]{1,0:T(8,128)(2,1)S(1)}, bf16[128,256]{1,0:T(8,128)(2,1)S(1)}, u32[]{:S(2)}, u32[]{:S(2)}) collective-permute-start(bf16[128,256]{1,0:T(8,128)(2,1)S(1)} %pad_maximum_fusion.13), channel_id=1, source_target_pairs={{0,8},{1,9},{2,10},{3,11},{4,12},{5,13},{6,14},{7,15},{8,0},{9,1},... | collective-permute-start | bytes 196616 | tf_op jit(solution)/shard_map/ppermute | solution.py:38
  13.2 4.7 %collective-permute-start.10 = (bf16[128,256]{1,0:T(8,128)(2,1)S(1)}, bf16[128,256]{1,0:T(8,128)(2,1)S(1)}, u32[]{:S(2)}, u32[]{:S(2)}) collective-permute-start(bf16[128,256]{1,0:T(8,128)(2,1)S(1)} %pad_maximum_fusion.12), channel_id=1, source_target_pairs={{0,4},{1,5},{2,6},{3,7},{4,0},{5,1},{6,2},{7,3},{8,12},{9,13},{10,... | collective-permute-start | bytes 196616 | tf_op jit(solution)/shard_map/ppermute | solution.py:38
  18.7 125.1 %reduce-scatter.2.cloned.1.call-start = ((), (), s32[]{:S(2)}) async-start(), calls=%async_computation.1 | async-start | bytes 2359296 | tf_op jit(solution)/shard_map/reduce_scatter | solution.py:348
  19.2 5.1 %collective-permute-start.2 = (bf16[256,256]{0,1:T(8,128)(2,1)S(1)}, bf16[256,256]{0,1:T(8,128)(2,1)S(1)}, u32[]{:S(2)}, u32[]{:S(2)}) collective-permute-start(bf16[256,256]{0,1:T(8,128)(2,1)S(1)} %bitcast.112), channel_id=1, source_target_pairs={{0,20},{1,21},{2,22},{3,23},{4,16},{5,17},{6,18},{7,19},{8,28},{9,... | collective-permute-start | bytes 393224 | tf_op jit(solution)/shard_map/ppermute | solution.py:38
  20.3 4.0 %collective-permute-start = (bf16[256,256]{0,1:T(8,128)(2,1)S(1)}, bf16[256,256]{0,1:T(8,128)(2,1)S(1)}, u32[]{:S(2)}, u32[]{:S(2)}) collective-permute-start(bf16[256,256]{0,1:T(8,128)(2,1)S(1)} %bitcast.111), channel_id=1, source_target_pairs={{0,16},{1,17},{2,18},{3,19},{4,20},{5,21},{6,22},{7,23},{8,24},{9,... | collective-permute-start | bytes 393224 | tf_op jit(solution)/shard_map/ppermute | solution.py:38
  20.7 6.6 %collective-permute-start.1 = (bf16[256,256]{0,1:T(8,128)(2,1)S(1)}, bf16[256,256]{0,1:T(8,128)(2,1)S(1)}, u32[]{:S(2)}, u32[]{:S(2)}) collective-permute-start(bf16[256,256]{0,1:T(8,128)(2,1)S(1)} %bitcast.110), channel_id=1, source_target_pairs={{0,4},{1,5},{2,6},{3,7},{4,0},{5,1},{6,2},{7,3},{8,12},{9,13},{10,... | collective-permute-start | bytes 393224 | tf_op jit(solution)/shard_map/ppermute | solution.py:38
  27.6 11.4 %collective-permute-start.5 = (bf16[2,2,256,256]{3,2,1,0:T(8,128)(2,1)S(1)}, bf16[2,2,256,256]{3,2,1,0:T(8,128)(2,1)S(1)}, u32[]{:S(2)}, u32[]{:S(2)}) collective-permute-start(bf16[2,2,256,256]{3,2,1,0:T(8,128)(2,1)S(1)} %bitcast.96), channel_id=1, source_target_pairs={{0,3},{1,0},{2,1},{3,2},{4,7},{5,4},{6,5},{7,6},{8,11},{9,8},{10,9... | collective-permute-start | bytes 1572872 | tf_op jit(solution)/shard_map/ppermute | solution.py:38
  30.1 23.4 %collective-permute-start.4 = (bf16[2,2,256,256]{3,2,1,0:T(8,128)(2,1)S(1)}, bf16[2,2,256,256]{3,2,1,0:T(8,128)(2,1)S(1)}, u32[]{:S(2)}, u32[]{:S(2)}) collective-permute-start(bf16[2,2,256,256]{3,2,1,0:T(8,128)(2,1)S(1)} %bitcast.97), channel_id=1, source_target_pairs={{0,2},{1,3},{2,0},{3,1},{4,6},{5,7},{6,4},{7,5},{8,10},{9,11},{10,... | collective-permute-start | bytes 1572872 | tf_op jit(solution)/shard_map/ppermute | solution.py:38
  30.6 26.2 %collective-permute-start.3 = (bf16[2,2,256,256]{3,2,1,0:T(8,128)(2,1)S(1)}, bf16[2,2,256,256]{3,2,1,0:T(8,128)(2,1)S(1)}, u32[]{:S(2)}, u32[]{:S(2)}) collective-permute-start(bf16[2,2,256,256]{3,2,1,0:T(8,128)(2,1)S(1)} %bitcast.98), channel_id=1, source_target_pairs={{0,1},{1,2},{2,3},{3,0},{4,5},{5,6},{6,7},{7,4},{8,9},{9,10},{10,1... | collective-permute-start | bytes 1572872 | tf_op jit(solution)/shard_map/ppermute | solution.py:38
  32.2 25.0 %collective-permute-start.16 = (bf16[2,3,256,128]{3,2,1,0:T(8,128)(2,1)S(1)}, bf16[2,3,256,128]{3,2,1,0:T(8,128)(2,1)S(1)}, u32[]{:S(2)}, u32[]{:S(2)}) collective-permute-start(bf16[2,3,256,128]{3,2,1,0:T(8,128)(2,1)S(1)} %pad_maximum_fusion.1), channel_id=1, source_target_pairs={{0,8},{1,9},{2,10},{3,11},{4,12},{5,13},{6,14},{7,15},{8,0},{9,1},... | collective-permute-start | bytes 1179656 | tf_op jit(solution)/shard_map/ppermute | solution.py:38
  36.3 23.3 %collective-permute-start.6 = (bf16[2,2,256,256]{3,2,1,0:T(8,128)(2,1)S(1)}, bf16[2,2,256,256]{3,2,1,0:T(8,128)(2,1)}, u32[]{:S(2)}, u32[]{:S(2)}) collective-permute-start(bf16[2,2,256,256]{3,2,1,0:T(8,128)(2,1)S(1)} %bitcast.99), channel_id=1, source_target_pairs={{0,8},{1,9},{2,10},{3,11},{4,12},{5,13},{6,14},{7,15},{8,0},{9,1},... | collective-permute-start | bytes 1572872 | tf_op jit(solution)/shard_map/ppermute | solution.py:38
  39.0 20.6 %collective-permute-start.9 = (bf16[2,2,256,256]{3,2,1,0:T(8,128)(2,1)S(1)}, bf16[2,2,256,256]{3,2,1,0:T(8,128)(2,1)}, u32[]{:S(2)}, u32[]{:S(2)}) collective-permute-start(bf16[2,2,256,256]{3,2,1,0:T(8,128)(2,1)S(1)} %collective-permute-done.5.refs_3_), channel_id=1, source_target_pairs={{0,8},{1,9},{2,10},{3,11},{4,12},{5,13},{6,14},{7,15},{8,0},{9,1},... | collective-permute-start | bytes 1572872 | tf_op jit(solution)/shard_map/ppermute | solution.py:38
  53.5 11.5 %copy-start.13 = (bf16[2,2,256,256]{3,2,1,0:T(8,128)(2,1)}, bf16[2,2,256,256]{3,2,1,0:T(8,128)(2,1)S(1)}, u32[]{:S(2)}) copy-start(bf16[2,2,256,256]{3,2,1,0:T(8,128)(2,1)S(1)} %collective-permute-done.4.refs_2_) | copy-start | bytes 1572868
  53.5 6.0 %collective-permute-start.8 = (bf16[2,2,256,256]{3,2,1,0:T(8,128)(2,1)S(1)}, bf16[2,2,256,256]{3,2,1,0:T(8,128)(2,1)}, u32[]{:S(2)}, u32[]{:S(2)}) collective-permute-start(bf16[2,2,256,256]{3,2,1,0:T(8,128)(2,1)S(1)} %collective-permute-done.4.refs_2_), channel_id=1, source_target_pairs={{0,8},{1,9},{2,10},{3,11},{4,12},{5,13},{6,14},{7,15},{8,0},{9,1},... | collective-permute-start | bytes 1572872 | tf_op jit(solution)/shard_map/ppermute | solution.py:38
  56.8 8.3 %copy-start.15 = (bf16[2,2,256,256]{3,2,1,0:T(8,128)(2,1)}, bf16[2,2,256,256]{3,2,1,0:T(8,128)(2,1)S(1)}, u32[]{:S(2)}) copy-start(bf16[2,2,256,256]{3,2,1,0:T(8,128)(2,1)S(1)} %collective-permute-done.3.refs_1_) | copy-start | bytes 1572868
  56.8 2.8 %collective-permute-start.7 = (bf16[2,2,256,256]{3,2,1,0:T(8,128)(2,1)S(1)}, bf16[2,2,256,256]{3,2,1,0:T(8,128)(2,1)}, u32[]{:S(2)}, u32[]{:S(2)}) collective-permute-start(bf16[2,2,256,256]{3,2,1,0:T(8,128)(2,1)S(1)} %collective-permute-done.3.refs_1_), channel_id=1, source_target_pairs={{0,8},{1,9},{2,10},{3,11},{4,12},{5,13},{6,14},{7,15},{8,0},{9,1},... | collective-permute-start | bytes 1572872 | tf_op jit(solution)/shard_map/ppermute | solution.py:38
  58.0 10.8 %collective-permute-start.17 = (bf16[2,3,256,128]{3,2,1,0:T(8,128)(2,1)}, bf16[2,3,256,128]{3,2,1,0:T(8,128)(2,1)S(1)}, u32[]{:S(2)}, u32[]{:S(2)}) collective-permute-start(bf16[2,3,256,128]{3,2,1,0:T(8,128)(2,1)} %pad_maximum_fusion.2), channel_id=1, source_target_pairs={{0,16},{1,17},{2,18},{3,19},{4,20},{5,21},{6,22},{7,23},{8,24},{9,... | collective-permute-start | bytes 1179656 | tf_op jit(solution)/shard_map/ppermute | solution.py:38
  65.1 15.1 %collective-permute-start.13 = (bf16[1024,128]{1,0:T(8,128)(2,1)S(1)}, bf16[1024,128]{1,0:T(8,128)(2,1)S(1)}, u32[]{:S(2)}, u32[]{:S(2)}) collective-permute-start(bf16[1024,128]{1,0:T(8,128)(2,1)S(1)} %get-tuple-element.58), channel_id=1, source_target_pairs={{0,20},{1,21},{2,22},{3,23},{4,16},{5,17},{6,18},{7,19},{8,28},{9,... | collective-permute-start | bytes 786440 | tf_op jit(solution)/shard_map/ppermute | solution.py:38
  66.4 13.7 %collective-permute-start.14 = (bf16[1024,128]{1,0:T(8,128)(2,1)S(1)}, bf16[1024,128]{1,0:T(8,128)(2,1)S(1)}, u32[]{:S(2)}, u32[]{:S(2)}) collective-permute-start(bf16[1024,128]{1,0:T(8,128)(2,1)S(1)} %get-tuple-element.59), channel_id=1, source_target_pairs={{0,4},{1,5},{2,6},{3,7},{4,0},{5,1},{6,2},{7,3},{8,12},{9,13},{10,... | collective-permute-start | bytes 786440 | tf_op jit(solution)/shard_map/ppermute | solution.py:38
  67.9 12.3 %collective-permute-start.15 = (bf16[1024,128]{1,0:T(8,128)(2,1)S(1)}, bf16[1024,128]{1,0:T(8,128)(2,1)S(1)}, u32[]{:S(2)}, u32[]{:S(2)}) collective-permute-start(bf16[1024,128]{1,0:T(8,128)(2,1)S(1)} %get-tuple-element.60), channel_id=1, source_target_pairs={{0,16},{1,17},{2,18},{3,19},{4,20},{5,21},{6,22},{7,23},{8,24},{9,... | collective-permute-start | bytes 786440 | tf_op jit(solution)/shard_map/ppermute | solution.py:38
  68.9 8.5 %collective-permute-start.19 = (bf16[2,256,128]{2,1,0:T(8,128)(2,1)S(1)}, bf16[2,256,128]{2,1,0:T(8,128)(2,1)S(1)}, u32[]{:S(2)}, u32[]{:S(2)}) collective-permute-start(bf16[2,256,128]{2,1,0:T(8,128)(2,1)S(1)} %get-tuple-element.111), channel_id=1, source_target_pairs={{0,32},{1,33},{2,34},{3,35},{4,36},{5,37},{6,38},{7,39},{8,40},{9,... | collective-permute-start | bytes 393224 | tf_op jit(solution)/shard_map/ppermute | solution.py:38
  70.6 29.3 %copy-start.14 = (bf16[2,2,256,256]{3,2,1,0:T(8,128)(2,1)S(1)}, bf16[2,2,256,256]{3,2,1,0:T(8,128)(2,1)}, u32[]{:S(2)}) copy-start(bf16[2,2,256,256]{3,2,1,0:T(8,128)(2,1)} %copy-done.13) | copy-start | bytes 1572868
  70.6 29.3 %copy-start.16 = (bf16[2,2,256,256]{3,2,1,0:T(8,128)(2,1)S(1)}, bf16[2,2,256,256]{3,2,1,0:T(8,128)(2,1)}, u32[]{:S(2)}) copy-start(bf16[2,2,256,256]{3,2,1,0:T(8,128)(2,1)} %copy-done.15) | copy-start | bytes 1572868
  70.6 9.5 %collective-permute-start.18 = (bf16[2,256,128]{2,1,0:T(8,128)(2,1)S(1)}, bf16[2,256,128]{2,1,0:T(8,128)(2,1)S(1)}, u32[]{:S(2)}, u32[]{:S(2)}) collective-permute-start(bf16[2,256,128]{2,1,0:T(8,128)(2,1)S(1)} %get-tuple-element.112), channel_id=1, source_target_pairs={{0,32},{1,33},{2,34},{3,35},{4,36},{5,37},{6,38},{7,39},{8,40},{9,... | collective-permute-start | bytes 393224 | tf_op jit(solution)/shard_map/ppermute | solution.py:38
  85.3 14.6 %copy-start.12 = (bf16[4,256,128]{2,1,0:T(8,128)(2,1)}, bf16[4,256,128]{2,1,0:T(8,128)(2,1)S(1)}, u32[]{:S(2)}) copy-start(bf16[4,256,128]{2,1,0:T(8,128)(2,1)S(1)} %get-tuple-element.68) | copy-start | bytes 786436
  85.3 14.6 %collective-permute-start.22 = (bf16[1024,128]{1,0:T(8,128)(2,1)S(1)}, bf16[1024,128]{1,0:T(8,128)(2,1)S(1)}, u32[]{:S(2)}, u32[]{:S(2)}) collective-permute-start(bf16[1024,128]{1,0:T(8,128)(2,1)S(1)} %get-tuple-element.75.refs_0_.refs_8_), channel_id=1, source_target_pairs={{0,20},{1,21},{2,22},{3,23},{4,16},{5,17},{6,18},{7,19},{8,28},{9,... | collective-permute-start | bytes 786440 | tf_op jit(solution)/shard_map/ppermute | solution.py:38
  85.4 14.5 %collective-permute-start.21 = (bf16[1024,128]{1,0:T(8,128)(2,1)S(1)}, bf16[1024,128]{1,0:T(8,128)(2,1)S(1)}, u32[]{:S(2)}, u32[]{:S(2)}) collective-permute-start(bf16[1024,128]{1,0:T(8,128)(2,1)S(1)} %get-tuple-element.75.refs_0_.refs_8_), channel_id=1, source_target_pairs={{0,4},{1,5},{2,6},{3,7},{4,0},{5,1},{6,2},{7,3},{8,12},{9,13},{10,... | collective-permute-start | bytes 786440 | tf_op jit(solution)/shard_map/ppermute | solution.py:38
  88.6 11.3 %collective-permute-start.20 = (bf16[1024,128]{1,0:T(8,128)(2,1)S(1)}, bf16[1024,128]{1,0:T(8,128)(2,1)S(1)}, u32[]{:S(2)}, u32[]{:S(2)}) collective-permute-start(bf16[1024,128]{1,0:T(8,128)(2,1)S(1)} %get-tuple-element.75.refs_0_.refs_8_), channel_id=1, source_target_pairs={{0,16},{1,17},{2,18},{3,19},{4,20},{5,21},{6,22},{7,23},{8,24},{9,... | collective-permute-start | bytes 786440 | tf_op jit(solution)/shard_map/ppermute | solution.py:38
  88.7 7.4 %collective-permute-start.24 = (bf16[2,256,128]{2,1,0:T(8,128)(2,1)S(1)}, bf16[2,256,128]{2,1,0:T(8,128)(2,1)S(1)}, u32[]{:S(2)}, u32[]{:S(2)}) collective-permute-start(bf16[2,256,128]{2,1,0:T(8,128)(2,1)S(1)} %get-tuple-element.109), channel_id=1, source_target_pairs={{0,224},{1,225},{2,226},{3,227},{4,228},{5,229},{6,230},{7,231},{8... | collective-permute-start | bytes 393224 | tf_op jit(solution)/shard_map/ppermute | solution.py:38
  94.2 4.1 %collective-permute-start.23 = (bf16[2,256,128]{2,1,0:T(8,128)(2,1)S(1)}, bf16[2,256,128]{2,1,0:T(8,128)(2,1)S(1)}, u32[]{:S(2)}, u32[]{:S(2)}) collective-permute-start(bf16[2,256,128]{2,1,0:T(8,128)(2,1)S(1)} %get-tuple-element.110), channel_id=1, source_target_pairs={{0,224},{1,225},{2,226},{3,227},{4,228},{5,229},{6,230},{7,231},{8... | collective-permute-start | bytes 393224 | tf_op jit(solution)/shard_map/ppermute | solution.py:38
  96.1 8.0 %copy-start.22 = (bf16[2,256,128]{2,1,0:T(8,128)(2,1)}, bf16[2,256,128]{2,1,0:T(8,128)(2,1)S(1)}, u32[]{:S(2)}) copy-start(bf16[2,256,128]{2,1,0:T(8,128)(2,1)S(1)} %collective-permute-done.24) | copy-start | bytes 393220
  98.3 5.8 %copy-start.23 = (bf16[2,256,128]{2,1,0:T(8,128)(2,1)}, bf16[2,256,128]{2,1,0:T(8,128)(2,1)S(1)}, u32[]{:S(2)}) copy-start(bf16[2,256,128]{2,1,0:T(8,128)(2,1)S(1)} %collective-permute-done.23) | copy-start | bytes 393220
  113.1 7.5 %collective-permute-start.27 = (bf16[8,2,256,256]{3,2,1,0:T(8,128)(2,1)}, bf16[8,2,256,256]{3,2,1,0:T(8,128)(2,1)}, u32[]{:S(2)}, u32[]{:S(2)}) collective-permute-start(bf16[8,2,256,256]{3,2,1,0:T(8,128)(2,1)} %d_hidden_away.1), channel_id=1, source_target_pairs={{0,8},{1,9},{2,10},{3,11},{4,12},{5,13},{6,14},{7,15},{8,0},{9,1},... | collective-permute-start | bytes 6291464 | tf_op jit(solution)/shard_map/ppermute | solution.py:38
  119.7 11.0 %collective-permute-start.25 = (bf16[2,3,256,128]{3,2,1,0:T(8,128)(2,1)}, bf16[2,3,256,128]{3,2,1,0:T(8,128)(2,1)S(1)}, u32[]{:S(2)}, u32[]{:S(2)}) collective-permute-start(bf16[2,3,256,128]{3,2,1,0:T(8,128)(2,1)} %pad_maximum_fusion.3), channel_id=1, source_target_pairs={{0,16},{1,17},{2,18},{3,19},{4,20},{5,21},{6,22},{7,23},{8,24},{9,... | collective-permute-start | bytes 1179656 | tf_op jit(solution)/shard_map/ppermute | solution.py:38
  124.5 27.7 %collective-permute-start.28 = (bf16[2,2,256,256]{3,2,1,0:T(8,128)(2,1)}, bf16[2,2,256,256]{3,2,1,0:T(8,128)(2,1)S(1)}, u32[]{:S(2)}, u32[]{:S(2)}) collective-permute-start(bf16[2,2,256,256]{3,2,1,0:T(8,128)(2,1)} %get-tuple-element.80), channel_id=1, source_target_pairs={{0,3},{1,0},{2,1},{3,2},{4,7},{5,4},{6,5},{7,6},{8,11},{9,8},{10,9... | collective-permute-start | bytes 1572872 | tf_op jit(solution)/shard_map/ppermute | solution.py:38
  125.4 26.8 %collective-permute-start.29 = (bf16[2,2,256,256]{3,2,1,0:T(8,128)(2,1)}, bf16[2,2,256,256]{3,2,1,0:T(8,128)(2,1)S(1)}, u32[]{:S(2)}, u32[]{:S(2)}) collective-permute-start(bf16[2,2,256,256]{3,2,1,0:T(8,128)(2,1)} %get-tuple-element.81), channel_id=1, source_target_pairs={{0,2},{1,3},{2,0},{3,1},{4,6},{5,7},{6,4},{7,5},{8,10},{9,11},{10,... | collective-permute-start | bytes 1572872 | tf_op jit(solution)/shard_map/ppermute | solution.py:38
  125.4 26.8 %collective-permute-start.30 = (bf16[2,2,256,256]{3,2,1,0:T(8,128)(2,1)}, bf16[2,2,256,256]{3,2,1,0:T(8,128)(2,1)S(1)}, u32[]{:S(2)}, u32[]{:S(2)}) collective-permute-start(bf16[2,2,256,256]{3,2,1,0:T(8,128)(2,1)} %get-tuple-element.82), channel_id=1, source_target_pairs={{0,1},{1,2},{2,3},{3,0},{4,5},{5,6},{6,7},{7,4},{8,9},{9,10},{10,1... | collective-permute-start | bytes 1572872 | tf_op jit(solution)/shard_map/ppermute | solution.py:38
  131.5 26.6 %copy-start.21 = (bf16[1,256,128]{2,1,0:T(8,128)(2,1)S(1)}, bf16[1,256,128]{2,1,0:T(8,128)(2,1)}, u32[]{:S(2)}) copy-start(bf16[1,256,128]{2,1,0:T(8,128)(2,1)} %get-tuple-element.108) | copy-start | bytes 196612
  131.5 24.3 %collective-permute-start.26 = (bf16[2,3,256,128]{3,2,1,0:T(8,128)(2,1)}, bf16[2,3,256,128]{3,2,1,0:T(8,128)(2,1)S(1)}, u32[]{:S(2)}, u32[]{:S(2)}) collective-permute-start(bf16[2,3,256,128]{3,2,1,0:T(8,128)(2,1)} %pad_maximum_fusion.4), channel_id=1, source_target_pairs={{0,8},{1,9},{2,10},{3,11},{4,12},{5,13},{6,14},{7,15},{8,0},{9,1},... | collective-permute-start | bytes 1179656 | tf_op jit(solution)/shard_map/ppermute | solution.py:38
  144.8 12.4 %collective-permute-start.36 = (bf16[128,256]{1,0:T(8,128)(2,1)S(1)}, bf16[128,256]{1,0:T(8,128)(2,1)S(1)}, u32[]{:S(2)}, u32[]{:S(2)}) collective-permute-start(bf16[128,256]{1,0:T(8,128)(2,1)S(1)} %get-tuple-element.101), channel_id=1, source_target_pairs={{0,12},{1,13},{2,14},{3,15},{4,8},{5,9},{6,10},{7,11},{8,4},{9,5},... | collective-permute-start | bytes 196616 | tf_op jit(solution)/shard_map/ppermute | solution.py:38
  152.5 10.8 %collective-permute-start.33 = (bf16[256,256]{1,0:T(8,128)(2,1)S(1)}, bf16[256,256]{1,0:T(8,128)(2,1)S(1)}, u32[]{:S(2)}, u32[]{:S(2)}) collective-permute-start(bf16[256,256]{1,0:T(8,128)(2,1)S(1)} %get-tuple-element.95), channel_id=1, source_target_pairs={{0,20},{1,21},{2,22},{3,23},{4,16},{5,17},{6,18},{7,19},{8,28},{9,... | collective-permute-start | bytes 393224 | tf_op jit(solution)/shard_map/ppermute | solution.py:38
  153.4 9.9 %collective-permute-start.32 = (bf16[256,256]{1,0:T(8,128)(2,1)S(1)}, bf16[256,256]{1,0:T(8,128)(2,1)S(1)}, u32[]{:S(2)}, u32[]{:S(2)}) collective-permute-start(bf16[256,256]{1,0:T(8,128)(2,1)S(1)} %get-tuple-element.96), channel_id=1, source_target_pairs={{0,4},{1,5},{2,6},{3,7},{4,0},{5,1},{6,2},{7,3},{8,12},{9,13},{10,... | collective-permute-start | bytes 393224 | tf_op jit(solution)/shard_map/ppermute | solution.py:38
  154.6 8.6 %collective-permute-start.31 = (bf16[256,256]{1,0:T(8,128)(2,1)S(1)}, bf16[256,256]{1,0:T(8,128)(2,1)S(1)}, u32[]{:S(2)}, u32[]{:S(2)}) collective-permute-start(bf16[256,256]{1,0:T(8,128)(2,1)S(1)} %get-tuple-element.97), channel_id=1, source_target_pairs={{0,16},{1,17},{2,18},{3,19},{4,20},{5,21},{6,22},{7,23},{8,24},{9,... | collective-permute-start | bytes 393224 | tf_op jit(solution)/shard_map/ppermute | solution.py:38
  155.8 3.9 %collective-permute-start.34 = (bf16[128,256]{1,0:T(8,128)(2,1)S(1)}, bf16[128,256]{1,0:T(8,128)(2,1)S(1)}, u32[]{:S(2)}, u32[]{:S(2)}) collective-permute-start(bf16[128,256]{1,0:T(8,128)(2,1)S(1)} %get-tuple-element.102), channel_id=1, source_target_pairs={{0,8},{1,9},{2,10},{3,11},{4,12},{5,13},{6,14},{7,15},{8,0},{9,1},... | collective-permute-start | bytes 196616 | tf_op jit(solution)/shard_map/ppermute | solution.py:38
  157.2 6.1 %collective-permute-start.35 = (bf16[128,256]{1,0:T(8,128)(2,1)S(1)}, bf16[128,256]{1,0:T(8,128)(2,1)S(1)}, u32[]{:S(2)}, u32[]{:S(2)}) collective-permute-start(bf16[128,256]{1,0:T(8,128)(2,1)S(1)} %get-tuple-element.104), channel_id=1, source_target_pairs={{0,4},{1,5},{2,6},{3,7},{4,0},{5,1},{6,2},{7,3},{8,12},{9,13},{10,... | collective-permute-start | bytes 196616 | tf_op jit(solution)/shard_map/ppermute | solution.py:38
  (15 other events, 52.1 us)
Sparse Core Ops, SparseCore 0:
  18.8 39.3 all-gather.2
  105.7 38.1 reduce-scatter.1

commit v3 on v2

--- a/solution.py
+++ b/solution.py
@@ -91,12 +91,6 @@
     return mm(dq, refs[4][place_ref[i]], ((1,), (1,)))
 
 
-def d_hidden_away_kernel(place_ref, *refs):
-    for dl in range(2):
-        for i in range(8):
-            refs[5][i, dl] = d_hidden_block(place_ref, refs, dl, i).astype(BF)
-
-
 def d_hidden_near_kernel(place_ref, *refs):
     for dl in range(2):
         for i in range(8):
@@ -104,12 +98,6 @@
             refs[6 + i // 2][i % 2, dl] = (part + refs[5][i, dl].astype(F32)).astype(BF)
 
 
-def d_hidden_away(place, dq, weights):
-    work = cost(1024 * 2048 * 512, 5 << 20)
-    outs = [((8, 2, T, T), BF)]
-    return in_vmem(d_hidden_away_kernel, "d_hidden_away", work, outs, place, *dq, weights, room=20)[0]
-
-
 def d_hidden_near(place, dq, weights, away):
     work = cost(1024 * 2048 * 512, 7 << 20)
     outs = [((2, 2, T, T), BF)] * 4
@@ -117,7 +105,7 @@
 
 
 def d_weight_kernel(place_ref, *refs):
-    own, other, dqs, out_ref = refs[:4], refs[4:8], refs[8:12], refs[12]
+    own, other, dqs, out_ref, away_ref = refs[:4], refs[4:8], refs[8:12], refs[13], refs[14]
     dq = jnp.concatenate(
         [
             jnp.concatenate(
@@ -136,12 +124,17 @@
             [feature_block(tokens, i, dl) for tokens in (own, other) for dl in range(2)], axis=0
         )
         out_ref[place_ref[i]] = mm(h, dq, ((0,), (0,))).astype(BF)
-
-
-def d_weight_part(place, own, other, dq):
-    work = cost(2 * 1024 * 2048 * 512, 7 << 20)
-    outs = [((NZ, T, 4 * DH), BF)]
-    return in_vmem(d_weight_kernel, "d_weight_part", work, outs, place, *own, *other, *dq)[0]
+    for dl in range(2):
+        for i in range(8):
+            away_ref[i, dl] = d_hidden_block(place_ref, refs[8:13], dl + 2, i).astype(BF)
+
+
+def d_weight_part(place, own, other, dq, weights):
+    work = cost(3 * 1024 * 2048 * 512, 11 << 20)
+    outs = [((NZ, T, 4 * DH), BF), ((8, 2, T, T), BF)]
+    return in_vmem(
+        d_weight_kernel, "d_weight_part", work, outs, place, *own, *other, *dq, weights
+    )
 
 
 def attended_kernel(place_ref, own_ref, core_ref, y_ref, *outs):
@@ -288,7 +281,6 @@
     lanes = [(yl ^ dl) * 4 + (yh ^ dy) for dy, dl in quad]
     tail = heads + lanes + [yh, 1 - yh, (z % SEQ_Z == 0).astype(jnp.int32)]
     place = jnp.stack(blocks + rows + tail).astype(jnp.int32)
-    place_other = jnp.stack(blocks + rows[2:] + rows[:2] + tail).astype(jnp.int32)
 
     def weight_piece(dc, dy):
         half = lax.dynamic_slice_in_dim(weight, (yh ^ dy) * DH, DH, 0)
@@ -344,9 +336,9 @@
     dq, late = tie(dq, late)
     late = jnp.stack(late)
 
-    sums = d_weight_part(place, own, other, dq)
+    sums, away = d_weight_part(place, own, other, dq, weights)
     shard = lax.psum_scatter(sums.reshape(NZ * T, 4 * DH), "z", scatter_dimension=0, tiled=True)
-    away = move(d_hidden_away(place_other, dq, weights), co=1)
+    away = move(away, co=1)
     near = d_hidden_near(place, dq, weights, away)
     line = [near[0]] + [move(near[dx], dx=-dx) for dx in range(1, NX)]
 
@@ -367,7 +359,6 @@
         return block[:, dy * T : (dy + 1) * T]
 
     ends = [weight_back(dc, dy) for dy, dc in quad]
-    line = after(line, *ends)
     ends = [move(ends[k], yh=quad[k][0], co=quad[k][1]) if k else ends[0] for k in range(4)]
     line = sum(block.astype(F32) for block in line).astype(BF)
     back = [line[dy, dl] for dy, dl in quad]

time: 173 us -> 169 us (0.977)
  waiting for transfers between devices: 44.1 us -> 52.9 us
  local copies, waits for them, and re-layouts: 12.9 us -> 6.25 us
  other arithmetic: 7.55 us -> 4.51 us
    ppermute x37, waiting for transfers between devices: 32.4 us -> 52 us  [move(): return lax.ppermute(block, AXES, pairs)]
    reduce_scatter x1, waiting for transfers between devices: 11.6 us -> 0.01 us  [per_device(): lax.psum_scatter(sums.reshape(NZ * T, 4 * DH), 'z', scatter_dimension=0,...]
    unnamed x51 -> x49, local copies, waits for them, and re-layouts: 7.59 us -> 3.3 us
    pallas_call x6 -> x5, Pallas kernels: 18.1 us -> 16.4 us  [in_vmem(): pl.pallas_call(kernel, in_specs=[pl.BlockSpec(memory_space=pltpu.SMEM)] +...]
  transfers between devices with their start and end apart: 39 -> 39, of which waited for: 14 -> 19; matrix products, arithmetic and copies ran while one was open for 6% -> 3% of each run, Pallas kernels for 7% -> 5%
where the time goes in v3:
time: 169 us
  starting transfers between devices  68.6 us (41%)
  waiting for transfers between devices  52.9 us (31%)
  Pallas kernels  21.6 us (13%)
  between operations  14.6 us (9%)
  local copies, waits for them, and re-layouts  6.25 us (4%)
  other arithmetic  4.51 us (3%)
    ppermute x37, starting transfers between devices, move(): return lax.ppermute(block, AXES, pairs)  68.5 us
    ppermute x37, waiting for transfers between devices, move(): return lax.ppermute(block, AXES, pairs)  52 us
    pallas_call x5, Pallas kernels, in_vmem(): pl.pallas_call(kernel, in_specs=[pl.BlockSpec(memory_space=pltpu.SMEM)] +...  16.4 us
    pallas_call x1, Pallas kernels, attend(): pl.pallas_call(attend_kernel, in_specs=[pl.BlockSpec(memory_space=pltpu.S...  5.16 us
  transfers between devices with their start and end apart: 39, of which 19 were waited for; matrix products, arithmetic and copies ran while one was open for 3% of the time, Pallas kernels for 5%

profile of v3, /device:TPU:1, one launch (start us, length us, event | category | flops | bytes accessed | tf_op | source)
XLA Modules:
  0.0 168.5 jit_solution(9270606770744522770)
XLA Ops:
  7.3 1.3 fusion.16
  8.6 3.3 %collective-permute-start.11 = (bf16[128,256]{1,0:T(8,128)(2,1)S(1)}, bf16[128,256]{1,0:T(8,128)(2,1)S(1)}, u32[]{:S(2)}, u32[]{:S(2)}) collective-permute-start(bf16[128,256]{1,0:T(8,128)(2,1)S(1)} %pad_maximum_fusion.13), channel_id=1, source_target_pairs={{0,8},{1,9},{2,10},{3,11},{4,12},{5,13},{6,14},{7,15},{8,0},{9,1},... | collective-permute-start | bytes 196616 | tf_op jit(solution)/shard_map/ppermute | solution.py:38
  12.0 1.2 collective-permute-start.12
  13.2 1.8 %collective-permute-start.10 = (bf16[128,256]{1,0:T(8,128)(2,1)S(1)}, bf16[128,256]{1,0:T(8,128)(2,1)S(1)}, u32[]{:S(2)}, u32[]{:S(2)}) collective-permute-start(bf16[128,256]{1,0:T(8,128)(2,1)S(1)} %pad_maximum_fusion.12), channel_id=1, source_target_pairs={{0,4},{1,5},{2,6},{3,7},{4,0},{5,1},{6,2},{7,3},{8,12},{9,13},{10,... | collective-permute-start | bytes 196616 | tf_op jit(solution)/shard_map/ppermute | solution.py:38
  15.0 2.4 %collective-permute-done.12 = bf16[128,256]{1,0:T(8,128)(2,1)S(1)} collective-permute-done((bf16[128,256]{1,0:T(8,128)(2,1)S(1)}, bf16[128,256]{1,0:T(8,128)(2,1)S(1)}, u32[]{:S(2)}, u32[]{:S(2)}) %collective-permute-start.12) | collective-permute-done | bytes 65568 | tf_op jit(solution)/shard_map/ppermute | solution.py:38
  19.2 1.6 collective-permute-start.2
  21.4 1.1 collective-permute-start
  22.8 1.5 collective-permute-done.2
  24.4 1.9 %collective-permute-done.1 = bf16[256,256]{0,1:T(8,128)(2,1)S(1)} collective-permute-done((bf16[256,256]{0,1:T(8,128)(2,1)S(1)}, bf16[256,256]{0,1:T(8,128)(2,1)S(1)}, u32[]{:S(2)}, u32[]{:S(2)}) %collective-permute-start.1) | collective-permute-done | bytes 131104 | tf_op jit(solution)/shard_map/ppermute | solution.py:38
  26.3 0.9 collective-permute-done
  27.4 1.0 collective-permute-start.3
  28.5 2.5 %collective-permute-start.4 = (bf16[2,2,256,256]{3,2,1,0:T(8,128)(2,1)S(1)}, bf16[2,2,256,256]{3,2,1,0:T(8,128)(2,1)S(1)}, u32[]{:S(2)}, u32[]{:S(2)}) collective-permute-start(bf16[2,2,256,256]{3,2,1,0:T(8,128)(2,1)S(1)} %bitcast.96), channel_id=1, source_target_pairs={{0,2},{1,3},{2,0},{3,1},{4,6},{5,7},{6,4},{7,5},{8,10},{9,11},{10,... | collective-permute-start | bytes 1572872 | tf_op jit(solution)/shard_map/ppermute | solution.py:38
  30.9 1.2 collective-permute-start.5
  32.2 3.8 %collective-permute-start.16 = (bf16[2,3,256,128]{3,2,1,0:T(8,128)(2,1)S(1)}, bf16[2,3,256,128]{3,2,1,0:T(8,128)(2,1)S(1)}, u32[]{:S(2)}, u32[]{:S(2)}) collective-permute-start(bf16[2,3,256,128]{3,2,1,0:T(8,128)(2,1)S(1)} %pad_maximum_fusion.1), channel_id=1, source_target_pairs={{0,8},{1,9},{2,10},{3,11},{4,12},{5,13},{6,14},{7,15},{8,0},{9,1},... | collective-permute-start | bytes 1179656 | tf_op jit(solution)/shard_map/ppermute | solution.py:38
  36.1 3.4 %collective-permute-done.3.refs_1_ = bf16[2,2,256,256]{3,2,1,0:T(8,128)(2,1)S(1)} collective-permute-done((bf16[2,2,256,256]{3,2,1,0:T(8,128)(2,1)S(1)}, bf16[2,2,256,256]{3,2,1,0:T(8,128)(2,1)S(1)}, u32[]{:S(2)}, u32[]{:S(2)}) %collective-permute-start.3) | collective-permute-done | bytes 524320 | tf_op jit(solution)/shard_map/ppermute | solution.py:38
  39.4 6.3 %collective-permute-start.7 = (bf16[2,2,256,256]{3,2,1,0:T(8,128)(2,1)S(1)}, bf16[2,2,256,256]{3,2,1,0:T(8,128)(2,1)}, u32[]{:S(2)}, u32[]{:S(2)}) collective-permute-start(bf16[2,2,256,256]{3,2,1,0:T(8,128)(2,1)S(1)} %collective-permute-done.3.refs_1_), channel_id=1, source_target_pairs={{0,8},{1,9},{2,10},{3,11},{4,12},{5,13},{6,14},{7,15},{8,0},{9,1},... | collective-permute-start | bytes 1572872 | tf_op jit(solution)/shard_map/ppermute | solution.py:38
  45.7 5.6 %collective-permute-done.4.refs_2_ = bf16[2,2,256,256]{3,2,1,0:T(8,128)(2,1)S(1)} collective-permute-done((bf16[2,2,256,256]{3,2,1,0:T(8,128)(2,1)S(1)}, bf16[2,2,256,256]{3,2,1,0:T(8,128)(2,1)S(1)}, u32[]{:S(2)}, u32[]{:S(2)}) %collective-permute-start.4) | collective-permute-done | bytes 524320 | tf_op jit(solution)/shard_map/ppermute | solution.py:38
  51.3 3.8 %collective-permute-start.8 = (bf16[2,2,256,256]{3,2,1,0:T(8,128)(2,1)S(1)}, bf16[2,2,256,256]{3,2,1,0:T(8,128)(2,1)}, u32[]{:S(2)}, u32[]{:S(2)}) collective-permute-start(bf16[2,2,256,256]{3,2,1,0:T(8,128)(2,1)S(1)} %collective-permute-done.4.refs_2_), channel_id=1, source_target_pairs={{0,8},{1,9},{2,10},{3,11},{4,12},{5,13},{6,14},{7,15},{8,0},{9,1},... | collective-permute-start | bytes 1572872 | tf_op jit(solution)/shard_map/ppermute | solution.py:38
  58.4 1.6 copy-done
  59.9 3.9 %query_part.1 = (bf16[1024,128]{1,0:T(8,128)(2,1)S(1)}, bf16[1024,128]{1,0:T(8,128)(2,1)S(1)}, bf16[1024,128]{1,0:T(8,128)(2,1)S(1)}, bf16[1024,128]{1,0:T(8,128)(2,1)S(1)}) custom-call(s32[23]{0:T(128)S(1)} %stack.192.place_ref, bf16[2,2,256,256]{3,2,1,0:T(8,128)(2,1)S(1)} %bitcast.99, bf16[2,2,256,256]{3,2,1,0:T(8,128)(2,1)S(1)} %collective-permute-done.3.refs_1_, ...), custom_call_target="tpu_custom_call" | custom-call | flops 2147483648 | bytes 7340032 | tf_op jit(solution)/shard_map/query_part/pallas_call | solution.py:71
  63.8 2.7 %collective-permute-start.13 = (bf16[1024,128]{1,0:T(8,128)(2,1)S(1)}, bf16[1024,128]{1,0:T(8,128)(2,1)S(1)}, u32[]{:S(2)}, u32[]{:S(2)}) collective-permute-start(bf16[1024,128]{1,0:T(8,128)(2,1)S(1)} %get-tuple-element.56), channel_id=1, source_target_pairs={{0,20},{1,21},{2,22},{3,23},{4,16},{5,17},{6,18},{7,19},{8,28},{9,... | collective-permute-start | bytes 786440 | tf_op jit(solution)/shard_map/ppermute | solution.py:38
  68.4 1.6 collective-permute-start.19
  70.0 4.9 %collective-permute-done.18.prev0_ref = bf16[2,256,128]{2,1,0:T(8,128)(2,1)S(1)} collective-permute-done((bf16[2,256,128]{2,1,0:T(8,128)(2,1)S(1)}, bf16[2,256,128]{2,1,0:T(8,128)(2,1)S(1)}, u32[]{:S(2)}, u32[]{:S(2)}) %collective-permute-start.18) | collective-permute-done | bytes 131104 | tf_op jit(solution)/shard_map/ppermute | solution.py:38
  75.0 1.4 collective-permute-done.19.prev1_ref
  76.4 5.2 %attend.1 = (bf16[4,256,128]{2,1,0:T(8,128)(2,1)S(1)}, bf16[1024,128]{1,0:T(8,128)(2,1)S(1)}, f32[4,2,256,128]{3,2,1,0:T(8,128)S(1)}, bf16[2,2,256,128]{3,2,1,0:T(8,128)(2,1)S(1)}) custom-call(s32[23]{0:T(128)S(1)} %stack.192.place_ref, bf16[1024,128]{1,0:T(8,128)(2,1)S(1)} %get-tuple-element.55.q0_ref, ...), custom_call_target="tpu_custom_call" | custom-call | flops 1207959552 | bytes 5242880 | tf_op jit(solution)/shard_map/attend/pallas_call | solution.py:242
  82.1 3.0 %collective-permute-start.21 = (bf16[1024,128]{1,0:T(8,128)(2,1)S(1)}, bf16[1024,128]{1,0:T(8,128)(2,1)S(1)}, u32[]{:S(2)}, u32[]{:S(2)}) collective-permute-start(bf16[1024,128]{1,0:T(8,128)(2,1)S(1)} %get-tuple-element.73.refs_8_.refs_0_), channel_id=1, source_target_pairs={{0,4},{1,5},{2,6},{3,7},{4,0},{5,1},{6,2},{7,3},{8,12},{9,13},{10,... | collective-permute-start | bytes 786440 | tf_op jit(solution)/shard_map/ppermute | solution.py:38
  85.5 6.4 %collective-permute-start.23 = (bf16[2,256,128]{2,1,0:T(8,128)(2,1)S(1)}, bf16[2,256,128]{2,1,0:T(8,128)(2,1)S(1)}, u32[]{:S(2)}, u32[]{:S(2)}) collective-permute-start(bf16[2,256,128]{2,1,0:T(8,128)(2,1)S(1)} %get-tuple-element.106), channel_id=1, source_target_pairs={{0,224},{1,225},{2,226},{3,227},{4,228},{5,229},{6,230},{7,231},{8... | collective-permute-start | bytes 393224 | tf_op jit(solution)/shard_map/ppermute | solution.py:38
  92.9 1.0 collective-permute-done.23
  93.9 2.7 %collective-permute-done.24 = bf16[2,256,128]{2,1,0:T(8,128)(2,1)S(1)} collective-permute-done((bf16[2,256,128]{2,1,0:T(8,128)(2,1)S(1)}, bf16[2,256,128]{2,1,0:T(8,128)(2,1)S(1)}, u32[]{:S(2)}, u32[]{:S(2)}) %collective-permute-start.24) | collective-permute-done | bytes 131104 | tf_op jit(solution)/shard_map/ppermute | solution.py:38
  96.7 6.3 %d_weight_part.1 = (bf16[8,256,512]{2,1,0:T(8,128)(2,1)}, bf16[8,2,256,256]{3,2,1,0:T(8,128)(2,1)S(1)}) custom-call(s32[23]{0:T(128)S(1)} %stack.192.place_ref, bf16[2,2,256,256]{3,2,1,0:T(8,128)(2,1)S(1)} %bitcast.100, bf16[2,2,256,256]{3,2,1,0:T(8,128)(2,1)S(1)} %copy-done.12, bf16[2,2,256,256]{3,2,1,0:T(8,128)(2,1)S(1)} %copy-done.14, ...), custom_call_target="tpu_custom_call" | custom-call | flops 3221225472 | bytes 11534336 | tf_op jit(solution)/shard_map/d_weight_part/pallas_call | solution.py:71
  103.1 1.4 copy-done.10
  104.5 3.9 %collective-permute-start.27 = (bf16[8,2,256,256]{3,2,1,0:T(8,128)(2,1)}, bf16[8,2,256,256]{3,2,1,0:T(8,128)(2,1)}, u32[]{:S(2)}, u32[]{:S(2)}) collective-permute-start(bf16[8,2,256,256]{3,2,1,0:T(8,128)(2,1)} %copy-done.10), channel_id=1, source_target_pairs={{0,8},{1,9},{2,10},{3,11},{4,12},{5,13},{6,14},{7,15},{8,0},{9,1},... | collective-permute-start | bytes 6291464 | tf_op jit(solution)/shard_map/ppermute | solution.py:38
  108.4 1.5 fusion.9
  110.0 2.6 %collective-permute-done.27.refs_5_ = bf16[8,2,256,256]{3,2,1,0:T(8,128)(2,1)} collective-permute-done((bf16[8,2,256,256]{3,2,1,0:T(8,128)(2,1)}, bf16[8,2,256,256]{3,2,1,0:T(8,128)(2,1)}, u32[]{:S(2)}, u32[]{:S(2)}) %collective-permute-start.27) | collective-permute-done | bytes 2097184 | tf_op jit(solution)/shard_map/ppermute | solution.py:38
  112.5 3.0 %d_hidden_near.1 = (bf16[2,2,256,256]{3,2,1,0:T(8,128)(2,1)S(1)}, bf16[2,2,256,256]{3,2,1,0:T(8,128)(2,1)S(1)}, bf16[2,2,256,256]{3,2,1,0:T(8,128)(2,1)S(1)}, bf16[2,2,256,256]{3,2,1,0:T(8,128)(2,1)S(1)}) custom-call(s32[23]{0:T(128)S(1)} %stack.192.place_ref, bf16[1024,128]{1,0:T(8,128)(2,1)S(1)} %copy-done.3, bf16[1024,128]{1,0:T(8,128)(2,1)S(1)} %copy-done.5, ...), custom_call_target="tpu_custom_call" | custom-call | flops 1073741824 | bytes 7340032 | tf_op jit(solution)/shard_map/d_hidden_near/pallas_call | solution.py:71
  115.6 1.4 collective-permute-start.30
  117.0 2.1 %collective-permute-start.29 = (bf16[2,2,256,256]{3,2,1,0:T(8,128)(2,1)S(1)}, bf16[2,2,256,256]{3,2,1,0:T(8,128)(2,1)S(1)}, u32[]{:S(2)}, u32[]{:S(2)}) collective-permute-start(bf16[2,2,256,256]{3,2,1,0:T(8,128)(2,1)S(1)} %get-tuple-element.80), channel_id=1, source_target_pairs={{0,2},{1,3},{2,0},{3,1},{4,6},{5,7},{6,4},{7,5},{8,10},{9,11},{10,... | collective-permute-start | bytes 1572872 | tf_op jit(solution)/shard_map/ppermute | solution.py:38
  119.1 1.3 collective-permute-start.28
  120.5 9.5 %collective-permute-done.25.y_ref = bf16[2,3,256,128]{3,2,1,0:T(8,128)(2,1)S(1)} collective-permute-done((bf16[2,3,256,128]{3,2,1,0:T(8,128)(2,1)S(1)}, bf16[2,3,256,128]{3,2,1,0:T(8,128)(2,1)S(1)}, u32[]{:S(2)}, u32[]{:S(2)}) %collective-permute-start.25) | collective-permute-done | bytes 393248 | tf_op jit(solution)/shard_map/ppermute | solution.py:38
  130.8 2.0 %collective-permute-start.26 = (bf16[2,3,256,128]{3,2,1,0:T(8,128)(2,1)}, bf16[2,3,256,128]{3,2,1,0:T(8,128)(2,1)S(1)}, u32[]{:S(2)}, u32[]{:S(2)}) collective-permute-start(bf16[2,3,256,128]{3,2,1,0:T(8,128)(2,1)} %pad_maximum_fusion.4), channel_id=1, source_target_pairs={{0,8},{1,9},{2,10},{3,11},{4,12},{5,13},{6,14},{7,15},{8,0},{9,1},... | collective-permute-start | bytes 1179656 | tf_op jit(solution)/shard_map/ppermute | solution.py:38
  132.8 9.2 %collective-permute-done.29 = bf16[2,2,256,256]{3,2,1,0:T(8,128)(2,1)S(1)} collective-permute-done((bf16[2,2,256,256]{3,2,1,0:T(8,128)(2,1)S(1)}, bf16[2,2,256,256]{3,2,1,0:T(8,128)(2,1)S(1)}, u32[]{:S(2)}, u32[]{:S(2)}) %collective-permute-start.29) | collective-permute-done | bytes 524320 | tf_op jit(solution)/shard_map/ppermute | solution.py:38
  142.4 3.0 %collective-permute-start.32 = (bf16[256,256]{1,0:T(8,128)(2,1)S(1)}, bf16[256,256]{1,0:T(8,128)(2,1)S(1)}, u32[]{:S(2)}, u32[]{:S(2)}) collective-permute-start(bf16[256,256]{1,0:T(8,128)(2,1)S(1)} %get-tuple-element.92), channel_id=1, source_target_pairs={{0,4},{1,5},{2,6},{3,7},{4,0},{5,1},{6,2},{7,3},{8,12},{9,13},{10,... | collective-permute-start | bytes 393224 | tf_op jit(solution)/shard_map/ppermute | solution.py:38
  146.2 1.0 fusion.14
  147.2 4.4 %collective-permute-start.34 = (bf16[128,256]{1,0:T(8,128)(2,1)S(1)}, bf16[128,256]{1,0:T(8,128)(2,1)S(1)}, u32[]{:S(2)}, u32[]{:S(2)}) collective-permute-start(bf16[128,256]{1,0:T(8,128)(2,1)S(1)} %get-tuple-element.98), channel_id=1, source_target_pairs={{0,8},{1,9},{2,10},{3,11},{4,12},{5,13},{6,14},{7,15},{8,0},{9,1},... | collective-permute-start | bytes 196616 | tf_op jit(solution)/shard_map/ppermute | solution.py:38
  151.6 2.9 %collective-permute-start.35 = (bf16[128,256]{1,0:T(8,128)(2,1)S(1)}, bf16[128,256]{1,0:T(8,128)(2,1)S(1)}, u32[]{:S(2)}, u32[]{:S(2)}) collective-permute-start(bf16[128,256]{1,0:T(8,128)(2,1)S(1)} %get-tuple-element.100), channel_id=1, source_target_pairs={{0,4},{1,5},{2,6},{3,7},{4,0},{5,1},{6,2},{7,3},{8,12},{9,13},{10,... | collective-permute-start | bytes 196616 | tf_op jit(solution)/shard_map/ppermute | solution.py:38
  154.9 1.6 attended_last.1
  156.8 3.3 %collective-permute-done.36.refs_7_ = bf16[128,256]{1,0:T(8,128)(2,1)S(1)} collective-permute-done((bf16[128,256]{1,0:T(8,128)(2,1)S(1)}, bf16[128,256]{1,0:T(8,128)(2,1)S(1)}, u32[]{:S(2)}, u32[]{:S(2)}) %collective-permute-start.36) | collective-permute-done | bytes 65568 | tf_op jit(solution)/shard_map/ppermute | solution.py:38
  160.1 1.6 last.1
  (125 shorter events, 13.2 us)
Async XLA Ops:
  7.2 11.7 %copy-start.17 = (bf16[256,1024]{1,0:T(8,128)(2,1)S(1)}, bf16[256,1024]{1,0:T(8,128)(2,1)}, u32[]{:S(2)}) copy-start(bf16[256,1024]{1,0:T(8,128)(2,1)} %param.5) | copy-start | bytes 1572868
  7.2 51.2 %all-gather.3.cloned.1.call-start = ((), (), s32[]{:S(2)}) async-start(), calls=%async_computation.2 | async-start | bytes 2359296 | tf_op jit(solution)/shard_map/all_gather | solution.py:324
  8.6 6.4 %collective-permute-start.11 = (bf16[128,256]{1,0:T(8,128)(2,1)S(1)}, bf16[128,256]{1,0:T(8,128)(2,1)S(1)}, u32[]{:S(2)}, u32[]{:S(2)}) collective-permute-start(bf16[128,256]{1,0:T(8,128)(2,1)S(1)} %pad_maximum_fusion.13), channel_id=1, source_target_pairs={{0,8},{1,9},{2,10},{3,11},{4,12},{5,13},{6,14},{7,15},{8,0},{9,1},... | collective-permute-start | bytes 196616 | tf_op jit(solution)/shard_map/ppermute | solution.py:38
  12.0 5.4 %collective-permute-start.12 = (bf16[128,256]{1,0:T(8,128)(2,1)S(1)}, bf16[128,256]{1,0:T(8,128)(2,1)S(1)}, u32[]{:S(2)}, u32[]{:S(2)}) collective-permute-start(bf16[128,256]{1,0:T(8,128)(2,1)S(1)} %pad_maximum_fusion.14), channel_id=1, source_target_pairs={{0,12},{1,13},{2,14},{3,15},{4,8},{5,9},{6,10},{7,11},{8,4},{9,5},... | collective-permute-start | bytes 196616 | tf_op jit(solution)/shard_map/ppermute | solution.py:38
  13.2 4.8 %collective-permute-start.10 = (bf16[128,256]{1,0:T(8,128)(2,1)S(1)}, bf16[128,256]{1,0:T(8,128)(2,1)S(1)}, u32[]{:S(2)}, u32[]{:S(2)}) collective-permute-start(bf16[128,256]{1,0:T(8,128)(2,1)S(1)} %pad_maximum_fusion.12), channel_id=1, source_target_pairs={{0,4},{1,5},{2,6},{3,7},{4,0},{5,1},{6,2},{7,3},{8,12},{9,13},{10,... | collective-permute-start | bytes 196616 | tf_op jit(solution)/shard_map/ppermute | solution.py:38
  18.8 127.5 %reduce-scatter.2.cloned.1.call-start = ((), (), s32[]{:S(2)}) async-start(), calls=%async_computation.1 | async-start | bytes 2359296 | tf_op jit(solution)/shard_map/reduce_scatter | solution.py:340
  19.2 5.1 %collective-permute-start.2 = (bf16[256,256]{0,1:T(8,128)(2,1)S(1)}, bf16[256,256]{0,1:T(8,128)(2,1)S(1)}, u32[]{:S(2)}, u32[]{:S(2)}) collective-permute-start(bf16[256,256]{0,1:T(8,128)(2,1)S(1)} %bitcast.111), channel_id=1, source_target_pairs={{0,20},{1,21},{2,22},{3,23},{4,16},{5,17},{6,18},{7,19},{8,28},{9,... | collective-permute-start | bytes 393224 | tf_op jit(solution)/shard_map/ppermute | solution.py:38
  20.8 5.4 %collective-permute-start.1 = (bf16[256,256]{0,1:T(8,128)(2,1)S(1)}, bf16[256,256]{0,1:T(8,128)(2,1)S(1)}, u32[]{:S(2)}, u32[]{:S(2)}) collective-permute-start(bf16[256,256]{0,1:T(8,128)(2,1)S(1)} %bitcast.110), channel_id=1, source_target_pairs={{0,4},{1,5},{2,6},{3,7},{4,0},{5,1},{6,2},{7,3},{8,12},{9,13},{10,... | collective-permute-start | bytes 393224 | tf_op jit(solution)/shard_map/ppermute | solution.py:38
  21.4 5.7 %collective-permute-start = (bf16[256,256]{0,1:T(8,128)(2,1)S(1)}, bf16[256,256]{0,1:T(8,128)(2,1)S(1)}, u32[]{:S(2)}, u32[]{:S(2)}) collective-permute-start(bf16[256,256]{0,1:T(8,128)(2,1)S(1)} %bitcast.109), channel_id=1, source_target_pairs={{0,16},{1,17},{2,18},{3,19},{4,20},{5,21},{6,22},{7,23},{8,24},{9,... | collective-permute-start | bytes 393224 | tf_op jit(solution)/shard_map/ppermute | solution.py:38
  27.4 12.0 %collective-permute-start.3 = (bf16[2,2,256,256]{3,2,1,0:T(8,128)(2,1)S(1)}, bf16[2,2,256,256]{3,2,1,0:T(8,128)(2,1)S(1)}, u32[]{:S(2)}, u32[]{:S(2)}) collective-permute-start(bf16[2,2,256,256]{3,2,1,0:T(8,128)(2,1)S(1)} %bitcast.95), channel_id=1, source_target_pairs={{0,1},{1,2},{2,3},{3,0},{4,5},{5,6},{6,7},{7,4},{8,9},{9,10},{10,1... | collective-permute-start | bytes 1572872 | tf_op jit(solution)/shard_map/ppermute | solution.py:38
  28.5 22.8 %collective-permute-start.4 = (bf16[2,2,256,256]{3,2,1,0:T(8,128)(2,1)S(1)}, bf16[2,2,256,256]{3,2,1,0:T(8,128)(2,1)S(1)}, u32[]{:S(2)}, u32[]{:S(2)}) collective-permute-start(bf16[2,2,256,256]{3,2,1,0:T(8,128)(2,1)S(1)} %bitcast.96), channel_id=1, source_target_pairs={{0,2},{1,3},{2,0},{3,1},{4,6},{5,7},{6,4},{7,5},{8,10},{9,11},{10,... | collective-permute-start | bytes 1572872 | tf_op jit(solution)/shard_map/ppermute | solution.py:38
  30.9 24.1 %collective-permute-start.5 = (bf16[2,2,256,256]{3,2,1,0:T(8,128)(2,1)S(1)}, bf16[2,2,256,256]{3,2,1,0:T(8,128)(2,1)S(1)}, u32[]{:S(2)}, u32[]{:S(2)}) collective-permute-start(bf16[2,2,256,256]{3,2,1,0:T(8,128)(2,1)S(1)} %bitcast.97), channel_id=1, source_target_pairs={{0,3},{1,0},{2,1},{3,2},{4,7},{5,4},{6,5},{7,6},{8,11},{9,8},{10,9... | collective-permute-start | bytes 1572872 | tf_op jit(solution)/shard_map/ppermute | solution.py:38
  32.2 23.0 %collective-permute-start.16 = (bf16[2,3,256,128]{3,2,1,0:T(8,128)(2,1)S(1)}, bf16[2,3,256,128]{3,2,1,0:T(8,128)(2,1)S(1)}, u32[]{:S(2)}, u32[]{:S(2)}) collective-permute-start(bf16[2,3,256,128]{3,2,1,0:T(8,128)(2,1)S(1)} %pad_maximum_fusion.1), channel_id=1, source_target_pairs={{0,8},{1,9},{2,10},{3,11},{4,12},{5,13},{6,14},{7,15},{8,0},{9,1},... | collective-permute-start | bytes 1179656 | tf_op jit(solution)/shard_map/ppermute | solution.py:38
  36.0 20.6 %collective-permute-start.6 = (bf16[2,2,256,256]{3,2,1,0:T(8,128)(2,1)S(1)}, bf16[2,2,256,256]{3,2,1,0:T(8,128)(2,1)}, u32[]{:S(2)}, u32[]{:S(2)}) collective-permute-start(bf16[2,2,256,256]{3,2,1,0:T(8,128)(2,1)S(1)} %bitcast.98), channel_id=1, source_target_pairs={{0,8},{1,9},{2,10},{3,11},{4,12},{5,13},{6,14},{7,15},{8,0},{9,1},... | collective-permute-start | bytes 1572872 | tf_op jit(solution)/shard_map/ppermute | solution.py:38
  39.4 24.4 %copy-start.11 = (bf16[2,2,256,256]{3,2,1,0:T(8,128)(2,1)}, bf16[2,2,256,256]{3,2,1,0:T(8,128)(2,1)S(1)}, u32[]{:S(2)}) copy-start(bf16[2,2,256,256]{3,2,1,0:T(8,128)(2,1)S(1)} %collective-permute-done.3.refs_1_) | copy-start | bytes 1572868
  39.4 17.2 %collective-permute-start.7 = (bf16[2,2,256,256]{3,2,1,0:T(8,128)(2,1)S(1)}, bf16[2,2,256,256]{3,2,1,0:T(8,128)(2,1)}, u32[]{:S(2)}, u32[]{:S(2)}) collective-permute-start(bf16[2,2,256,256]{3,2,1,0:T(8,128)(2,1)S(1)} %collective-permute-done.3.refs_1_), channel_id=1, source_target_pairs={{0,8},{1,9},{2,10},{3,11},{4,12},{5,13},{6,14},{7,15},{8,0},{9,1},... | collective-permute-start | bytes 1572872 | tf_op jit(solution)/shard_map/ppermute | solution.py:38
  51.3 12.5 %copy-start.13 = (bf16[2,2,256,256]{3,2,1,0:T(8,128)(2,1)}, bf16[2,2,256,256]{3,2,1,0:T(8,128)(2,1)S(1)}, u32[]{:S(2)}) copy-start(bf16[2,2,256,256]{3,2,1,0:T(8,128)(2,1)S(1)} %collective-permute-done.4.refs_2_) | copy-start | bytes 1572868
  51.3 5.4 %collective-permute-start.8 = (bf16[2,2,256,256]{3,2,1,0:T(8,128)(2,1)S(1)}, bf16[2,2,256,256]{3,2,1,0:T(8,128)(2,1)}, u32[]{:S(2)}, u32[]{:S(2)}) collective-permute-start(bf16[2,2,256,256]{3,2,1,0:T(8,128)(2,1)S(1)} %collective-permute-done.4.refs_2_), channel_id=1, source_target_pairs={{0,8},{1,9},{2,10},{3,11},{4,12},{5,13},{6,14},{7,15},{8,0},{9,1},... | collective-permute-start | bytes 1572872 | tf_op jit(solution)/shard_map/ppermute | solution.py:38
  55.1 8.8 %copy-start.15 = (bf16[2,2,256,256]{3,2,1,0:T(8,128)(2,1)}, bf16[2,2,256,256]{3,2,1,0:T(8,128)(2,1)S(1)}, u32[]{:S(2)}) copy-start(bf16[2,2,256,256]{3,2,1,0:T(8,128)(2,1)S(1)} %collective-permute-done.5.refs_3_) | copy-start | bytes 1572868
  55.1 2.4 %collective-permute-start.9 = (bf16[2,2,256,256]{3,2,1,0:T(8,128)(2,1)S(1)}, bf16[2,2,256,256]{3,2,1,0:T(8,128)(2,1)}, u32[]{:S(2)}, u32[]{:S(2)}) collective-permute-start(bf16[2,2,256,256]{3,2,1,0:T(8,128)(2,1)S(1)} %collective-permute-done.5.refs_3_), channel_id=1, source_target_pairs={{0,8},{1,9},{2,10},{3,11},{4,12},{5,13},{6,14},{7,15},{8,0},{9,1},... | collective-permute-start | bytes 1572872 | tf_op jit(solution)/shard_map/ppermute | solution.py:38
  56.0 11.3 %collective-permute-start.17 = (bf16[2,3,256,128]{3,2,1,0:T(8,128)(2,1)}, bf16[2,3,256,128]{3,2,1,0:T(8,128)(2,1)S(1)}, u32[]{:S(2)}, u32[]{:S(2)}) collective-permute-start(bf16[2,3,256,128]{3,2,1,0:T(8,128)(2,1)} %pad_maximum_fusion.2), channel_id=1, source_target_pairs={{0,16},{1,17},{2,18},{3,19},{4,20},{5,21},{6,22},{7,23},{8,24},{9,... | collective-permute-start | bytes 1179656 | tf_op jit(solution)/shard_map/ppermute | solution.py:38
  63.8 12.5 %collective-permute-start.13 = (bf16[1024,128]{1,0:T(8,128)(2,1)S(1)}, bf16[1024,128]{1,0:T(8,128)(2,1)S(1)}, u32[]{:S(2)}, u32[]{:S(2)}) collective-permute-start(bf16[1024,128]{1,0:T(8,128)(2,1)S(1)} %get-tuple-element.56), channel_id=1, source_target_pairs={{0,20},{1,21},{2,22},{3,23},{4,16},{5,17},{6,18},{7,19},{8,28},{9,... | collective-permute-start | bytes 786440 | tf_op jit(solution)/shard_map/ppermute | solution.py:38
  66.6 9.8 %collective-permute-start.14 = (bf16[1024,128]{1,0:T(8,128)(2,1)S(1)}, bf16[1024,128]{1,0:T(8,128)(2,1)S(1)}, u32[]{:S(2)}, u32[]{:S(2)}) collective-permute-start(bf16[1024,128]{1,0:T(8,128)(2,1)S(1)} %get-tuple-element.57), channel_id=1, source_target_pairs={{0,4},{1,5},{2,6},{3,7},{4,0},{5,1},{6,2},{7,3},{8,12},{9,13},{10,... | collective-permute-start | bytes 786440 | tf_op jit(solution)/shard_map/ppermute | solution.py:38
  67.1 9.3 %collective-permute-start.15 = (bf16[1024,128]{1,0:T(8,128)(2,1)S(1)}, bf16[1024,128]{1,0:T(8,128)(2,1)S(1)}, u32[]{:S(2)}, u32[]{:S(2)}) collective-permute-start(bf16[1024,128]{1,0:T(8,128)(2,1)S(1)} %get-tuple-element.58), channel_id=1, source_target_pairs={{0,16},{1,17},{2,18},{3,19},{4,20},{5,21},{6,22},{7,23},{8,24},{9,... | collective-permute-start | bytes 786440 | tf_op jit(solution)/shard_map/ppermute | solution.py:38
  67.5 7.5 %collective-permute-start.18 = (bf16[2,256,128]{2,1,0:T(8,128)(2,1)S(1)}, bf16[2,256,128]{2,1,0:T(8,128)(2,1)S(1)}, u32[]{:S(2)}, u32[]{:S(2)}) collective-permute-start(bf16[2,256,128]{2,1,0:T(8,128)(2,1)S(1)} %get-tuple-element.108), channel_id=1, source_target_pairs={{0,32},{1,33},{2,34},{3,35},{4,36},{5,37},{6,38},{7,39},{8,40},{9,... | collective-permute-start | bytes 393224 | tf_op jit(solution)/shard_map/ppermute | solution.py:38
  68.4 28.3 %copy-start.12 = (bf16[2,2,256,256]{3,2,1,0:T(8,128)(2,1)S(1)}, bf16[2,2,256,256]{3,2,1,0:T(8,128)(2,1)}, u32[]{:S(2)}) copy-start(bf16[2,2,256,256]{3,2,1,0:T(8,128)(2,1)} %copy-done.11) | copy-start | bytes 1572868
  68.4 28.3 %copy-start.14 = (bf16[2,2,256,256]{3,2,1,0:T(8,128)(2,1)S(1)}, bf16[2,2,256,256]{3,2,1,0:T(8,128)(2,1)}, u32[]{:S(2)}) copy-start(bf16[2,2,256,256]{3,2,1,0:T(8,128)(2,1)} %copy-done.13) | copy-start | bytes 1572868
  68.4 28.3 %copy-start.16 = (bf16[2,2,256,256]{3,2,1,0:T(8,128)(2,1)S(1)}, bf16[2,2,256,256]{3,2,1,0:T(8,128)(2,1)}, u32[]{:S(2)}) copy-start(bf16[2,2,256,256]{3,2,1,0:T(8,128)(2,1)} %copy-done.15) | copy-start | bytes 1572868
  68.4 8.0 %collective-permute-start.19 = (bf16[2,256,128]{2,1,0:T(8,128)(2,1)S(1)}, bf16[2,256,128]{2,1,0:T(8,128)(2,1)S(1)}, u32[]{:S(2)}, u32[]{:S(2)}) collective-permute-start(bf16[2,256,128]{2,1,0:T(8,128)(2,1)S(1)} %get-tuple-element.107), channel_id=1, source_target_pairs={{0,32},{1,33},{2,34},{3,35},{4,36},{5,37},{6,38},{7,39},{8,40},{9,... | collective-permute-start | bytes 393224 | tf_op jit(solution)/shard_map/ppermute | solution.py:38
  81.5 21.5 %copy-start.2 = (bf16[1024,128]{1,0:T(8,128)(2,1)}, bf16[1024,128]{1,0:T(8,128)(2,1)S(1)}, u32[]{:S(2)}) copy-start(bf16[1024,128]{1,0:T(8,128)(2,1)S(1)} %get-tuple-element.73.refs_8_.refs_0_) | copy-start | bytes 786436
  81.6 15.1 %collective-permute-start.20 = (bf16[1024,128]{1,0:T(8,128)(2,1)S(1)}, bf16[1024,128]{1,0:T(8,128)(2,1)S(1)}, u32[]{:S(2)}, u32[]{:S(2)}) collective-permute-start(bf16[1024,128]{1,0:T(8,128)(2,1)S(1)} %get-tuple-element.73.refs_8_.refs_0_), channel_id=1, source_target_pairs={{0,16},{1,17},{2,18},{3,19},{4,20},{5,21},{6,22},{7,23},{8,24},{9,... | collective-permute-start | bytes 786440 | tf_op jit(solution)/shard_map/ppermute | solution.py:38
  82.1 14.5 %collective-permute-start.21 = (bf16[1024,128]{1,0:T(8,128)(2,1)S(1)}, bf16[1024,128]{1,0:T(8,128)(2,1)S(1)}, u32[]{:S(2)}, u32[]{:S(2)}) collective-permute-start(bf16[1024,128]{1,0:T(8,128)(2,1)S(1)} %get-tuple-element.73.refs_8_.refs_0_), channel_id=1, source_target_pairs={{0,4},{1,5},{2,6},{3,7},{4,0},{5,1},{6,2},{7,3},{8,12},{9,13},{10,... | collective-permute-start | bytes 786440 | tf_op jit(solution)/shard_map/ppermute | solution.py:38
  85.1 11.6 %collective-permute-start.22 = (bf16[1024,128]{1,0:T(8,128)(2,1)S(1)}, bf16[1024,128]{1,0:T(8,128)(2,1)S(1)}, u32[]{:S(2)}, u32[]{:S(2)}) collective-permute-start(bf16[1024,128]{1,0:T(8,128)(2,1)S(1)} %get-tuple-element.73.refs_8_.refs_0_), channel_id=1, source_target_pairs={{0,20},{1,21},{2,22},{3,23},{4,16},{5,17},{6,18},{7,19},{8,28},{9,... | collective-permute-start | bytes 786440 | tf_op jit(solution)/shard_map/ppermute | solution.py:38
  85.5 8.4 %collective-permute-start.23 = (bf16[2,256,128]{2,1,0:T(8,128)(2,1)S(1)}, bf16[2,256,128]{2,1,0:T(8,128)(2,1)S(1)}, u32[]{:S(2)}, u32[]{:S(2)}) collective-permute-start(bf16[2,256,128]{2,1,0:T(8,128)(2,1)S(1)} %get-tuple-element.106), channel_id=1, source_target_pairs={{0,224},{1,225},{2,226},{3,227},{4,228},{5,229},{6,230},{7,231},{8... | collective-permute-start | bytes 393224 | tf_op jit(solution)/shard_map/ppermute | solution.py:38
  92.0 4.7 %collective-permute-start.24 = (bf16[2,256,128]{2,1,0:T(8,128)(2,1)S(1)}, bf16[2,256,128]{2,1,0:T(8,128)(2,1)S(1)}, u32[]{:S(2)}, u32[]{:S(2)}) collective-permute-start(bf16[2,256,128]{2,1,0:T(8,128)(2,1)S(1)} %get-tuple-element.105), channel_id=1, source_target_pairs={{0,224},{1,225},{2,226},{3,227},{4,228},{5,229},{6,230},{7,231},{8... | collective-permute-start | bytes 393224 | tf_op jit(solution)/shard_map/ppermute | solution.py:38
  93.9 10.6 %copy-start.21 = (bf16[2,256,128]{2,1,0:T(8,128)(2,1)}, bf16[2,256,128]{2,1,0:T(8,128)(2,1)S(1)}, u32[]{:S(2)}) copy-start(bf16[2,256,128]{2,1,0:T(8,128)(2,1)S(1)} %collective-permute-done.23) | copy-start | bytes 393220
  104.5 8.0 %collective-permute-start.27 = (bf16[8,2,256,256]{3,2,1,0:T(8,128)(2,1)}, bf16[8,2,256,256]{3,2,1,0:T(8,128)(2,1)}, u32[]{:S(2)}, u32[]{:S(2)}) collective-permute-start(bf16[8,2,256,256]{3,2,1,0:T(8,128)(2,1)} %copy-done.10), channel_id=1, source_target_pairs={{0,8},{1,9},{2,10},{3,11},{4,12},{5,13},{6,14},{7,15},{8,0},{9,1},... | collective-permute-start | bytes 6291464 | tf_op jit(solution)/shard_map/ppermute | solution.py:38
  115.6 17.2 %collective-permute-start.30 = (bf16[2,2,256,256]{3,2,1,0:T(8,128)(2,1)S(1)}, bf16[2,2,256,256]{3,2,1,0:T(8,128)(2,1)S(1)}, u32[]{:S(2)}, u32[]{:S(2)}) collective-permute-start(bf16[2,2,256,256]{3,2,1,0:T(8,128)(2,1)S(1)} %get-tuple-element.81), channel_id=1, source_target_pairs={{0,1},{1,2},{2,3},{3,0},{4,5},{5,6},{6,7},{7,4},{8,9},{9,10},{10,1... | collective-permute-start | bytes 1572872 | tf_op jit(solution)/shard_map/ppermute | solution.py:38
  117.0 25.0 %collective-permute-start.29 = (bf16[2,2,256,256]{3,2,1,0:T(8,128)(2,1)S(1)}, bf16[2,2,256,256]{3,2,1,0:T(8,128)(2,1)S(1)}, u32[]{:S(2)}, u32[]{:S(2)}) collective-permute-start(bf16[2,2,256,256]{3,2,1,0:T(8,128)(2,1)S(1)} %get-tuple-element.80), channel_id=1, source_target_pairs={{0,2},{1,3},{2,0},{3,1},{4,6},{5,7},{6,4},{7,5},{8,10},{9,11},{10,... | collective-permute-start | bytes 1572872 | tf_op jit(solution)/shard_map/ppermute | solution.py:38
  119.1 22.9 %collective-permute-start.28 = (bf16[2,2,256,256]{3,2,1,0:T(8,128)(2,1)S(1)}, bf16[2,2,256,256]{3,2,1,0:T(8,128)(2,1)S(1)}, u32[]{:S(2)}, u32[]{:S(2)}) collective-permute-start(bf16[2,2,256,256]{3,2,1,0:T(8,128)(2,1)S(1)} %get-tuple-element.79), channel_id=1, source_target_pairs={{0,3},{1,0},{2,1},{3,2},{4,7},{5,4},{6,5},{7,6},{8,11},{9,8},{10,9... | collective-permute-start | bytes 1572872 | tf_op jit(solution)/shard_map/ppermute | solution.py:38
  120.4 9.6 %collective-permute-start.25 = (bf16[2,3,256,128]{3,2,1,0:T(8,128)(2,1)S(1)}, bf16[2,3,256,128]{3,2,1,0:T(8,128)(2,1)S(1)}, u32[]{:S(2)}, u32[]{:S(2)}) collective-permute-start(bf16[2,3,256,128]{3,2,1,0:T(8,128)(2,1)S(1)} %pad_maximum_fusion.3), channel_id=1, source_target_pairs={{0,16},{1,17},{2,18},{3,19},{4,20},{5,21},{6,22},{7,23},{8,24},{9,... | collective-permute-start | bytes 1179656 | tf_op jit(solution)/shard_map/ppermute | solution.py:38
  130.8 20.8 %collective-permute-start.26 = (bf16[2,3,256,128]{3,2,1,0:T(8,128)(2,1)}, bf16[2,3,256,128]{3,2,1,0:T(8,128)(2,1)S(1)}, u32[]{:S(2)}, u32[]{:S(2)}) collective-permute-start(bf16[2,3,256,128]{3,2,1,0:T(8,128)(2,1)} %pad_maximum_fusion.4), channel_id=1, source_target_pairs={{0,8},{1,9},{2,10},{3,11},{4,12},{5,13},{6,14},{7,15},{8,0},{9,1},... | collective-permute-start | bytes 1179656 | tf_op jit(solution)/shard_map/ppermute | solution.py:38
  142.3 12.2 %collective-permute-start.31 = (bf16[256,256]{1,0:T(8,128)(2,1)S(1)}, bf16[256,256]{1,0:T(8,128)(2,1)S(1)}, u32[]{:S(2)}, u32[]{:S(2)}) collective-permute-start(bf16[256,256]{1,0:T(8,128)(2,1)S(1)} %get-tuple-element.93), channel_id=1, source_target_pairs={{0,16},{1,17},{2,18},{3,19},{4,20},{5,21},{6,22},{7,23},{8,24},{9,... | collective-permute-start | bytes 393224 | tf_op jit(solution)/shard_map/ppermute | solution.py:38
  142.4 14.0 %collective-permute-start.32 = (bf16[256,256]{1,0:T(8,128)(2,1)S(1)}, bf16[256,256]{1,0:T(8,128)(2,1)S(1)}, u32[]{:S(2)}, u32[]{:S(2)}) collective-permute-start(bf16[256,256]{1,0:T(8,128)(2,1)S(1)} %get-tuple-element.92), channel_id=1, source_target_pairs={{0,4},{1,5},{2,6},{3,7},{4,0},{5,1},{6,2},{7,3},{8,12},{9,13},{10,... | collective-permute-start | bytes 393224 | tf_op jit(solution)/shard_map/ppermute | solution.py:38
  145.4 11.1 %collective-permute-start.33 = (bf16[256,256]{1,0:T(8,128)(2,1)S(1)}, bf16[256,256]{1,0:T(8,128)(2,1)S(1)}, u32[]{:S(2)}, u32[]{:S(2)}) collective-permute-start(bf16[256,256]{1,0:T(8,128)(2,1)S(1)} %get-tuple-element.91), channel_id=1, source_target_pairs={{0,20},{1,21},{2,22},{3,23},{4,16},{5,17},{6,18},{7,19},{8,28},{9,... | collective-permute-start | bytes 393224 | tf_op jit(solution)/shard_map/ppermute | solution.py:38
  147.2 9.2 %collective-permute-start.34 = (bf16[128,256]{1,0:T(8,128)(2,1)S(1)}, bf16[128,256]{1,0:T(8,128)(2,1)S(1)}, u32[]{:S(2)}, u32[]{:S(2)}) collective-permute-start(bf16[128,256]{1,0:T(8,128)(2,1)S(1)} %get-tuple-element.98), channel_id=1, source_target_pairs={{0,8},{1,9},{2,10},{3,11},{4,12},{5,13},{6,14},{7,15},{8,0},{9,1},... | collective-permute-start | bytes 196616 | tf_op jit(solution)/shard_map/ppermute | solution.py:38
  151.6 5.2 %collective-permute-start.35 = (bf16[128,256]{1,0:T(8,128)(2,1)S(1)}, bf16[128,256]{1,0:T(8,128)(2,1)S(1)}, u32[]{:S(2)}, u32[]{:S(2)}) collective-permute-start(bf16[128,256]{1,0:T(8,128)(2,1)S(1)} %get-tuple-element.100), channel_id=1, source_target_pairs={{0,4},{1,5},{2,6},{3,7},{4,0},{5,1},{6,2},{7,3},{8,12},{9,13},{10,... | collective-permute-start | bytes 196616 | tf_op jit(solution)/shard_map/ppermute | solution.py:38
  154.5 5.6 %collective-permute-start.36 = (bf16[128,256]{1,0:T(8,128)(2,1)S(1)}, bf16[128,256]{1,0:T(8,128)(2,1)S(1)}, u32[]{:S(2)}, u32[]{:S(2)}) collective-permute-start(bf16[128,256]{1,0:T(8,128)(2,1)S(1)} %get-tuple-element.97), channel_id=1, source_target_pairs={{0,12},{1,13},{2,14},{3,15},{4,8},{5,9},{6,10},{7,11},{8,4},{9,5},... | collective-permute-start | bytes 196616 | tf_op jit(solution)/shard_map/ppermute | solution.py:38
  (14 other events, 66.9 us)
Sparse Core Ops, SparseCore 0:
  18.9 39.3 all-gather.2
  104.6 41.1 reduce-scatter.1

commit v4 on v3

--- a/solution.py
+++ b/solution.py
@@ -101,7 +101,7 @@
 def d_hidden_near(place, dq, weights, away):
     work = cost(1024 * 2048 * 512, 7 << 20)
     outs = [((2, 2, T, T), BF)] * 4
-    return in_vmem(d_hidden_near_kernel, "d_hidden_near", work, outs, place, *dq, weights, away)
+    return in_vmem(d_hidden_near_kernel, "d_hidden_near", work, outs, place, *dq, weights, away, room=40)
 
 
 def d_weight_kernel(place_ref, *refs):

time: 169 us -> 169 us (level)
  no operation moved by 1% of the time
where the time goes in v4:
time: 169 us
  starting transfers between devices  68.6 us (41%)
  waiting for transfers between devices  52.9 us (31%)
  Pallas kernels  21.6 us (13%)
  between operations  14.6 us (9%)
  local copies, waits for them, and re-layouts  6.25 us (4%)
  other arithmetic  4.52 us (3%)
    ppermute x37, starting transfers between devices, move(): return lax.ppermute(block, AXES, pairs)  68.5 us
    ppermute x37, waiting for transfers between devices, move(): return lax.ppermute(block, AXES, pairs)  52 us
    pallas_call x5, Pallas kernels, in_vmem(): pl.pallas_call(kernel, in_specs=[pl.BlockSpec(memory_space=pltpu.SMEM)] +...  16.4 us
    pallas_call x1, Pallas kernels, attend(): pl.pallas_call(attend_kernel, in_specs=[pl.BlockSpec(memory_space=pltpu.S...  5.16 us
  transfers between devices with their start and end apart: 39, of which 19 were waited for; matrix products, arithmetic and copies ran while one was open for 3% of the time, Pallas kernels for 5%

profile of v4, /device:TPU:1, one launch (start us, length us, event | category | flops | bytes accessed | tf_op | source)
XLA Modules:
  0.0 168.5 jit_solution(13115012220332002681)
XLA Ops:
  7.3 1.3 fusion.16
  8.6 3.3 %collective-permute-start.11 = (bf16[128,256]{1,0:T(8,128)(2,1)S(1)}, bf16[128,256]{1,0:T(8,128)(2,1)S(1)}, u32[]{:S(2)}, u32[]{:S(2)}) collective-permute-start(bf16[128,256]{1,0:T(8,128)(2,1)S(1)} %pad_maximum_fusion.13), channel_id=1, source_target_pairs={{0,8},{1,9},{2,10},{3,11},{4,12},{5,13},{6,14},{7,15},{8,0},{9,1},... | collective-permute-start | bytes 196616 | tf_op jit(solution)/shard_map/ppermute | solution.py:38
  12.0 1.2 collective-permute-start.12
  13.2 1.8 %collective-permute-start.10 = (bf16[128,256]{1,0:T(8,128)(2,1)S(1)}, bf16[128,256]{1,0:T(8,128)(2,1)S(1)}, u32[]{:S(2)}, u32[]{:S(2)}) collective-permute-start(bf16[128,256]{1,0:T(8,128)(2,1)S(1)} %pad_maximum_fusion.12), channel_id=1, source_target_pairs={{0,4},{1,5},{2,6},{3,7},{4,0},{5,1},{6,2},{7,3},{8,12},{9,13},{10,... | collective-permute-start | bytes 196616 | tf_op jit(solution)/shard_map/ppermute | solution.py:38
  15.0 2.4 %collective-permute-done.12 = bf16[128,256]{1,0:T(8,128)(2,1)S(1)} collective-permute-done((bf16[128,256]{1,0:T(8,128)(2,1)S(1)}, bf16[128,256]{1,0:T(8,128)(2,1)S(1)}, u32[]{:S(2)}, u32[]{:S(2)}) %collective-permute-start.12) | collective-permute-done | bytes 65568 | tf_op jit(solution)/shard_map/ppermute | solution.py:38
  19.2 1.6 collective-permute-start.2
  21.4 1.1 collective-permute-start
  22.8 1.5 collective-permute-done.2
  24.4 1.9 %collective-permute-done.1 = bf16[256,256]{0,1:T(8,128)(2,1)S(1)} collective-permute-done((bf16[256,256]{0,1:T(8,128)(2,1)S(1)}, bf16[256,256]{0,1:T(8,128)(2,1)S(1)}, u32[]{:S(2)}, u32[]{:S(2)}) %collective-permute-start.1) | collective-permute-done | bytes 131104 | tf_op jit(solution)/shard_map/ppermute | solution.py:38
  26.3 0.9 collective-permute-done
  27.4 1.0 collective-permute-start.3
  28.5 2.5 %collective-permute-start.4 = (bf16[2,2,256,256]{3,2,1,0:T(8,128)(2,1)S(1)}, bf16[2,2,256,256]{3,2,1,0:T(8,128)(2,1)S(1)}, u32[]{:S(2)}, u32[]{:S(2)}) collective-permute-start(bf16[2,2,256,256]{3,2,1,0:T(8,128)(2,1)S(1)} %bitcast.96), channel_id=1, source_target_pairs={{0,2},{1,3},{2,0},{3,1},{4,6},{5,7},{6,4},{7,5},{8,10},{9,11},{10,... | collective-permute-start | bytes 1572872 | tf_op jit(solution)/shard_map/ppermute | solution.py:38
  30.9 1.2 collective-permute-start.5
  32.2 3.8 %collective-permute-start.16 = (bf16[2,3,256,128]{3,2,1,0:T(8,128)(2,1)S(1)}, bf16[2,3,256,128]{3,2,1,0:T(8,128)(2,1)S(1)}, u32[]{:S(2)}, u32[]{:S(2)}) collective-permute-start(bf16[2,3,256,128]{3,2,1,0:T(8,128)(2,1)S(1)} %pad_maximum_fusion.1), channel_id=1, source_target_pairs={{0,8},{1,9},{2,10},{3,11},{4,12},{5,13},{6,14},{7,15},{8,0},{9,1},... | collective-permute-start | bytes 1179656 | tf_op jit(solution)/shard_map/ppermute | solution.py:38
  36.1 3.4 %collective-permute-done.3.refs_1_ = bf16[2,2,256,256]{3,2,1,0:T(8,128)(2,1)S(1)} collective-permute-done((bf16[2,2,256,256]{3,2,1,0:T(8,128)(2,1)S(1)}, bf16[2,2,256,256]{3,2,1,0:T(8,128)(2,1)S(1)}, u32[]{:S(2)}, u32[]{:S(2)}) %collective-permute-start.3) | collective-permute-done | bytes 524320 | tf_op jit(solution)/shard_map/ppermute | solution.py:38
  39.4 6.3 %collective-permute-start.7 = (bf16[2,2,256,256]{3,2,1,0:T(8,128)(2,1)S(1)}, bf16[2,2,256,256]{3,2,1,0:T(8,128)(2,1)}, u32[]{:S(2)}, u32[]{:S(2)}) collective-permute-start(bf16[2,2,256,256]{3,2,1,0:T(8,128)(2,1)S(1)} %collective-permute-done.3.refs_1_), channel_id=1, source_target_pairs={{0,8},{1,9},{2,10},{3,11},{4,12},{5,13},{6,14},{7,15},{8,0},{9,1},... | collective-permute-start | bytes 1572872 | tf_op jit(solution)/shard_map/ppermute | solution.py:38
  45.7 5.6 %collective-permute-done.4.refs_2_ = bf16[2,2,256,256]{3,2,1,0:T(8,128)(2,1)S(1)} collective-permute-done((bf16[2,2,256,256]{3,2,1,0:T(8,128)(2,1)S(1)}, bf16[2,2,256,256]{3,2,1,0:T(8,128)(2,1)S(1)}, u32[]{:S(2)}, u32[]{:S(2)}) %collective-permute-start.4) | collective-permute-done | bytes 524320 | tf_op jit(solution)/shard_map/ppermute | solution.py:38
  51.3 3.8 %collective-permute-start.8 = (bf16[2,2,256,256]{3,2,1,0:T(8,128)(2,1)S(1)}, bf16[2,2,256,256]{3,2,1,0:T(8,128)(2,1)}, u32[]{:S(2)}, u32[]{:S(2)}) collective-permute-start(bf16[2,2,256,256]{3,2,1,0:T(8,128)(2,1)S(1)} %collective-permute-done.4.refs_2_), channel_id=1, source_target_pairs={{0,8},{1,9},{2,10},{3,11},{4,12},{5,13},{6,14},{7,15},{8,0},{9,1},... | collective-permute-start | bytes 1572872 | tf_op jit(solution)/shard_map/ppermute | solution.py:38
  58.4 1.6 copy-done
  59.9 3.9 %query_part.1 = (bf16[1024,128]{1,0:T(8,128)(2,1)S(1)}, bf16[1024,128]{1,0:T(8,128)(2,1)S(1)}, bf16[1024,128]{1,0:T(8,128)(2,1)S(1)}, bf16[1024,128]{1,0:T(8,128)(2,1)S(1)}) custom-call(s32[23]{0:T(128)S(1)} %stack.192.place_ref, bf16[2,2,256,256]{3,2,1,0:T(8,128)(2,1)S(1)} %bitcast.99, bf16[2,2,256,256]{3,2,1,0:T(8,128)(2,1)S(1)} %collective-permute-done.3.refs_1_, ...), custom_call_target="tpu_custom_call" | custom-call | flops 2147483648 | bytes 7340032 | tf_op jit(solution)/shard_map/query_part/pallas_call | solution.py:71
  63.8 2.7 %collective-permute-start.13 = (bf16[1024,128]{1,0:T(8,128)(2,1)S(1)}, bf16[1024,128]{1,0:T(8,128)(2,1)S(1)}, u32[]{:S(2)}, u32[]{:S(2)}) collective-permute-start(bf16[1024,128]{1,0:T(8,128)(2,1)S(1)} %get-tuple-element.56), channel_id=1, source_target_pairs={{0,20},{1,21},{2,22},{3,23},{4,16},{5,17},{6,18},{7,19},{8,28},{9,... | collective-permute-start | bytes 786440 | tf_op jit(solution)/shard_map/ppermute | solution.py:38
  68.4 1.6 collective-permute-start.19
  70.0 4.9 %collective-permute-done.18.prev0_ref = bf16[2,256,128]{2,1,0:T(8,128)(2,1)S(1)} collective-permute-done((bf16[2,256,128]{2,1,0:T(8,128)(2,1)S(1)}, bf16[2,256,128]{2,1,0:T(8,128)(2,1)S(1)}, u32[]{:S(2)}, u32[]{:S(2)}) %collective-permute-start.18) | collective-permute-done | bytes 131104 | tf_op jit(solution)/shard_map/ppermute | solution.py:38
  75.0 1.4 collective-permute-done.19.prev1_ref
  76.4 5.2 %attend.1 = (bf16[4,256,128]{2,1,0:T(8,128)(2,1)S(1)}, bf16[1024,128]{1,0:T(8,128)(2,1)S(1)}, f32[4,2,256,128]{3,2,1,0:T(8,128)S(1)}, bf16[2,2,256,128]{3,2,1,0:T(8,128)(2,1)S(1)}) custom-call(s32[23]{0:T(128)S(1)} %stack.192.place_ref, bf16[1024,128]{1,0:T(8,128)(2,1)S(1)} %get-tuple-element.55.q0_ref, ...), custom_call_target="tpu_custom_call" | custom-call | flops 1207959552 | bytes 5242880 | tf_op jit(solution)/shard_map/attend/pallas_call | solution.py:242
  82.1 3.0 %collective-permute-start.21 = (bf16[1024,128]{1,0:T(8,128)(2,1)S(1)}, bf16[1024,128]{1,0:T(8,128)(2,1)S(1)}, u32[]{:S(2)}, u32[]{:S(2)}) collective-permute-start(bf16[1024,128]{1,0:T(8,128)(2,1)S(1)} %get-tuple-element.73.refs_8_.refs_0_), channel_id=1, source_target_pairs={{0,4},{1,5},{2,6},{3,7},{4,0},{5,1},{6,2},{7,3},{8,12},{9,13},{10,... | collective-permute-start | bytes 786440 | tf_op jit(solution)/shard_map/ppermute | solution.py:38
  85.5 6.4 %collective-permute-start.23 = (bf16[2,256,128]{2,1,0:T(8,128)(2,1)S(1)}, bf16[2,256,128]{2,1,0:T(8,128)(2,1)S(1)}, u32[]{:S(2)}, u32[]{:S(2)}) collective-permute-start(bf16[2,256,128]{2,1,0:T(8,128)(2,1)S(1)} %get-tuple-element.106), channel_id=1, source_target_pairs={{0,224},{1,225},{2,226},{3,227},{4,228},{5,229},{6,230},{7,231},{8... | collective-permute-start | bytes 393224 | tf_op jit(solution)/shard_map/ppermute | solution.py:38
  92.9 1.0 collective-permute-done.23
  93.9 2.7 %collective-permute-done.24 = bf16[2,256,128]{2,1,0:T(8,128)(2,1)S(1)} collective-permute-done((bf16[2,256,128]{2,1,0:T(8,128)(2,1)S(1)}, bf16[2,256,128]{2,1,0:T(8,128)(2,1)S(1)}, u32[]{:S(2)}, u32[]{:S(2)}) %collective-permute-start.24) | collective-permute-done | bytes 131104 | tf_op jit(solution)/shard_map/ppermute | solution.py:38
  96.7 6.3 %d_weight_part.1 = (bf16[8,256,512]{2,1,0:T(8,128)(2,1)}, bf16[8,2,256,256]{3,2,1,0:T(8,128)(2,1)S(1)}) custom-call(s32[23]{0:T(128)S(1)} %stack.192.place_ref, bf16[2,2,256,256]{3,2,1,0:T(8,128)(2,1)S(1)} %bitcast.100, bf16[2,2,256,256]{3,2,1,0:T(8,128)(2,1)S(1)} %copy-done.12, bf16[2,2,256,256]{3,2,1,0:T(8,128)(2,1)S(1)} %copy-done.14, ...), custom_call_target="tpu_custom_call" | custom-call | flops 3221225472 | bytes 11534336 | tf_op jit(solution)/shard_map/d_weight_part/pallas_call | solution.py:71
  103.1 1.4 copy-done.10
  104.5 3.9 %collective-permute-start.27 = (bf16[8,2,256,256]{3,2,1,0:T(8,128)(2,1)}, bf16[8,2,256,256]{3,2,1,0:T(8,128)(2,1)}, u32[]{:S(2)}, u32[]{:S(2)}) collective-permute-start(bf16[8,2,256,256]{3,2,1,0:T(8,128)(2,1)} %copy-done.10), channel_id=1, source_target_pairs={{0,8},{1,9},{2,10},{3,11},{4,12},{5,13},{6,14},{7,15},{8,0},{9,1},... | collective-permute-start | bytes 6291464 | tf_op jit(solution)/shard_map/ppermute | solution.py:38
  108.4 1.5 fusion.9
  110.0 2.6 %collective-permute-done.27.refs_5_ = bf16[8,2,256,256]{3,2,1,0:T(8,128)(2,1)} collective-permute-done((bf16[8,2,256,256]{3,2,1,0:T(8,128)(2,1)}, bf16[8,2,256,256]{3,2,1,0:T(8,128)(2,1)}, u32[]{:S(2)}, u32[]{:S(2)}) %collective-permute-start.27) | collective-permute-done | bytes 2097184 | tf_op jit(solution)/shard_map/ppermute | solution.py:38
  112.5 3.0 %d_hidden_near.1 = (bf16[2,2,256,256]{3,2,1,0:T(8,128)(2,1)S(1)}, bf16[2,2,256,256]{3,2,1,0:T(8,128)(2,1)S(1)}, bf16[2,2,256,256]{3,2,1,0:T(8,128)(2,1)S(1)}, bf16[2,2,256,256]{3,2,1,0:T(8,128)(2,1)S(1)}) custom-call(s32[23]{0:T(128)S(1)} %stack.192.place_ref, bf16[1024,128]{1,0:T(8,128)(2,1)S(1)} %copy-done.3, bf16[1024,128]{1,0:T(8,128)(2,1)S(1)} %copy-done.5, ...), custom_call_target="tpu_custom_call" | custom-call | flops 1073741824 | bytes 7340032 | tf_op jit(solution)/shard_map/d_hidden_near/pallas_call | solution.py:71
  115.6 1.4 collective-permute-start.30
  117.0 2.1 %collective-permute-start.29 = (bf16[2,2,256,256]{3,2,1,0:T(8,128)(2,1)S(1)}, bf16[2,2,256,256]{3,2,1,0:T(8,128)(2,1)S(1)}, u32[]{:S(2)}, u32[]{:S(2)}) collective-permute-start(bf16[2,2,256,256]{3,2,1,0:T(8,128)(2,1)S(1)} %get-tuple-element.80), channel_id=1, source_target_pairs={{0,2},{1,3},{2,0},{3,1},{4,6},{5,7},{6,4},{7,5},{8,10},{9,11},{10,... | collective-permute-start | bytes 1572872 | tf_op jit(solution)/shard_map/ppermute | solution.py:38
  119.1 1.3 collective-permute-start.28
  120.5 9.5 %collective-permute-done.25.y_ref = bf16[2,3,256,128]{3,2,1,0:T(8,128)(2,1)S(1)} collective-permute-done((bf16[2,3,256,128]{3,2,1,0:T(8,128)(2,1)S(1)}, bf16[2,3,256,128]{3,2,1,0:T(8,128)(2,1)S(1)}, u32[]{:S(2)}, u32[]{:S(2)}) %collective-permute-start.25) | collective-permute-done | bytes 393248 | tf_op jit(solution)/shard_map/ppermute | solution.py:38
  130.8 2.0 %collective-permute-start.26 = (bf16[2,3,256,128]{3,2,1,0:T(8,128)(2,1)}, bf16[2,3,256,128]{3,2,1,0:T(8,128)(2,1)S(1)}, u32[]{:S(2)}, u32[]{:S(2)}) collective-permute-start(bf16[2,3,256,128]{3,2,1,0:T(8,128)(2,1)} %pad_maximum_fusion.4), channel_id=1, source_target_pairs={{0,8},{1,9},{2,10},{3,11},{4,12},{5,13},{6,14},{7,15},{8,0},{9,1},... | collective-permute-start | bytes 1179656 | tf_op jit(solution)/shard_map/ppermute | solution.py:38
  132.8 9.2 %collective-permute-done.29 = bf16[2,2,256,256]{3,2,1,0:T(8,128)(2,1)S(1)} collective-permute-done((bf16[2,2,256,256]{3,2,1,0:T(8,128)(2,1)S(1)}, bf16[2,2,256,256]{3,2,1,0:T(8,128)(2,1)S(1)}, u32[]{:S(2)}, u32[]{:S(2)}) %collective-permute-start.29) | collective-permute-done | bytes 524320 | tf_op jit(solution)/shard_map/ppermute | solution.py:38
  142.4 3.0 %collective-permute-start.32 = (bf16[256,256]{1,0:T(8,128)(2,1)S(1)}, bf16[256,256]{1,0:T(8,128)(2,1)S(1)}, u32[]{:S(2)}, u32[]{:S(2)}) collective-permute-start(bf16[256,256]{1,0:T(8,128)(2,1)S(1)} %get-tuple-element.92), channel_id=1, source_target_pairs={{0,4},{1,5},{2,6},{3,7},{4,0},{5,1},{6,2},{7,3},{8,12},{9,13},{10,... | collective-permute-start | bytes 393224 | tf_op jit(solution)/shard_map/ppermute | solution.py:38
  146.3 1.0 fusion.14
  147.2 4.4 %collective-permute-start.34 = (bf16[128,256]{1,0:T(8,128)(2,1)S(1)}, bf16[128,256]{1,0:T(8,128)(2,1)S(1)}, u32[]{:S(2)}, u32[]{:S(2)}) collective-permute-start(bf16[128,256]{1,0:T(8,128)(2,1)S(1)} %get-tuple-element.98), channel_id=1, source_target_pairs={{0,8},{1,9},{2,10},{3,11},{4,12},{5,13},{6,14},{7,15},{8,0},{9,1},... | collective-permute-start | bytes 196616 | tf_op jit(solution)/shard_map/ppermute | solution.py:38
  151.6 2.9 %collective-permute-start.35 = (bf16[128,256]{1,0:T(8,128)(2,1)S(1)}, bf16[128,256]{1,0:T(8,128)(2,1)S(1)}, u32[]{:S(2)}, u32[]{:S(2)}) collective-permute-start(bf16[128,256]{1,0:T(8,128)(2,1)S(1)} %get-tuple-element.100), channel_id=1, source_target_pairs={{0,4},{1,5},{2,6},{3,7},{4,0},{5,1},{6,2},{7,3},{8,12},{9,13},{10,... | collective-permute-start | bytes 196616 | tf_op jit(solution)/shard_map/ppermute | solution.py:38
  154.9 1.6 attended_last.1
  156.8 3.3 %collective-permute-done.36.refs_7_ = bf16[128,256]{1,0:T(8,128)(2,1)S(1)} collective-permute-done((bf16[128,256]{1,0:T(8,128)(2,1)S(1)}, bf16[128,256]{1,0:T(8,128)(2,1)S(1)}, u32[]{:S(2)}, u32[]{:S(2)}) %collective-permute-start.36) | collective-permute-done | bytes 65568 | tf_op jit(solution)/shard_map/ppermute | solution.py:38
  160.1 1.6 last.1
  (125 shorter events, 13.2 us)
Async XLA Ops:
  7.2 11.7 %copy-start.17 = (bf16[256,1024]{1,0:T(8,128)(2,1)S(1)}, bf16[256,1024]{1,0:T(8,128)(2,1)}, u32[]{:S(2)}) copy-start(bf16[256,1024]{1,0:T(8,128)(2,1)} %param.5) | copy-start | bytes 1572868
  7.2 51.2 %all-gather.3.cloned.1.call-start = ((), (), s32[]{:S(2)}) async-start(), calls=%async_computation.2 | async-start | bytes 2359296 | tf_op jit(solution)/shard_map/all_gather | solution.py:324
  8.6 6.4 %collective-permute-start.11 = (bf16[128,256]{1,0:T(8,128)(2,1)S(1)}, bf16[128,256]{1,0:T(8,128)(2,1)S(1)}, u32[]{:S(2)}, u32[]{:S(2)}) collective-permute-start(bf16[128,256]{1,0:T(8,128)(2,1)S(1)} %pad_maximum_fusion.13), channel_id=1, source_target_pairs={{0,8},{1,9},{2,10},{3,11},{4,12},{5,13},{6,14},{7,15},{8,0},{9,1},... | collective-permute-start | bytes 196616 | tf_op jit(solution)/shard_map/ppermute | solution.py:38
  12.0 5.4 %collective-permute-start.12 = (bf16[128,256]{1,0:T(8,128)(2,1)S(1)}, bf16[128,256]{1,0:T(8,128)(2,1)S(1)}, u32[]{:S(2)}, u32[]{:S(2)}) collective-permute-start(bf16[128,256]{1,0:T(8,128)(2,1)S(1)} %pad_maximum_fusion.14), channel_id=1, source_target_pairs={{0,12},{1,13},{2,14},{3,15},{4,8},{5,9},{6,10},{7,11},{8,4},{9,5},... | collective-permute-start | bytes 196616 | tf_op jit(solution)/shard_map/ppermute | solution.py:38
  13.2 4.8 %collective-permute-start.10 = (bf16[128,256]{1,0:T(8,128)(2,1)S(1)}, bf16[128,256]{1,0:T(8,128)(2,1)S(1)}, u32[]{:S(2)}, u32[]{:S(2)}) collective-permute-start(bf16[128,256]{1,0:T(8,128)(2,1)S(1)} %pad_maximum_fusion.12), channel_id=1, source_target_pairs={{0,4},{1,5},{2,6},{3,7},{4,0},{5,1},{6,2},{7,3},{8,12},{9,13},{10,... | collective-permute-start | bytes 196616 | tf_op jit(solution)/shard_map/ppermute | solution.py:38
  18.8 127.5 %reduce-scatter.2.cloned.1.call-start = ((), (), s32[]{:S(2)}) async-start(), calls=%async_computation.1 | async-start | bytes 2359296 | tf_op jit(solution)/shard_map/reduce_scatter | solution.py:340
  19.2 5.1 %collective-permute-start.2 = (bf16[256,256]{0,1:T(8,128)(2,1)S(1)}, bf16[256,256]{0,1:T(8,128)(2,1)S(1)}, u32[]{:S(2)}, u32[]{:S(2)}) collective-permute-start(bf16[256,256]{0,1:T(8,128)(2,1)S(1)} %bitcast.111), channel_id=1, source_target_pairs={{0,20},{1,21},{2,22},{3,23},{4,16},{5,17},{6,18},{7,19},{8,28},{9,... | collective-permute-start | bytes 393224 | tf_op jit(solution)/shard_map/ppermute | solution.py:38
  20.8 5.4 %collective-permute-start.1 = (bf16[256,256]{0,1:T(8,128)(2,1)S(1)}, bf16[256,256]{0,1:T(8,128)(2,1)S(1)}, u32[]{:S(2)}, u32[]{:S(2)}) collective-permute-start(bf16[256,256]{0,1:T(8,128)(2,1)S(1)} %bitcast.110), channel_id=1, source_target_pairs={{0,4},{1,5},{2,6},{3,7},{4,0},{5,1},{6,2},{7,3},{8,12},{9,13},{10,... | collective-permute-start | bytes 393224 | tf_op jit(solution)/shard_map/ppermute | solution.py:38
  21.4 5.7 %collective-permute-start = (bf16[256,256]{0,1:T(8,128)(2,1)S(1)}, bf16[256,256]{0,1:T(8,128)(2,1)S(1)}, u32[]{:S(2)}, u32[]{:S(2)}) collective-permute-start(bf16[256,256]{0,1:T(8,128)(2,1)S(1)} %bitcast.109), channel_id=1, source_target_pairs={{0,16},{1,17},{2,18},{3,19},{4,20},{5,21},{6,22},{7,23},{8,24},{9,... | collective-permute-start | bytes 393224 | tf_op jit(solution)/shard_map/ppermute | solution.py:38
  27.4 12.0 %collective-permute-start.3 = (bf16[2,2,256,256]{3,2,1,0:T(8,128)(2,1)S(1)}, bf16[2,2,256,256]{3,2,1,0:T(8,128)(2,1)S(1)}, u32[]{:S(2)}, u32[]{:S(2)}) collective-permute-start(bf16[2,2,256,256]{3,2,1,0:T(8,128)(2,1)S(1)} %bitcast.95), channel_id=1, source_target_pairs={{0,1},{1,2},{2,3},{3,0},{4,5},{5,6},{6,7},{7,4},{8,9},{9,10},{10,1... | collective-permute-start | bytes 1572872 | tf_op jit(solution)/shard_map/ppermute | solution.py:38
  28.5 22.8 %collective-permute-start.4 = (bf16[2,2,256,256]{3,2,1,0:T(8,128)(2,1)S(1)}, bf16[2,2,256,256]{3,2,1,0:T(8,128)(2,1)S(1)}, u32[]{:S(2)}, u32[]{:S(2)}) collective-permute-start(bf16[2,2,256,256]{3,2,1,0:T(8,128)(2,1)S(1)} %bitcast.96), channel_id=1, source_target_pairs={{0,2},{1,3},{2,0},{3,1},{4,6},{5,7},{6,4},{7,5},{8,10},{9,11},{10,... | collective-permute-start | bytes 1572872 | tf_op jit(solution)/shard_map/ppermute | solution.py:38
  30.9 24.1 %collective-permute-start.5 = (bf16[2,2,256,256]{3,2,1,0:T(8,128)(2,1)S(1)}, bf16[2,2,256,256]{3,2,1,0:T(8,128)(2,1)S(1)}, u32[]{:S(2)}, u32[]{:S(2)}) collective-permute-start(bf16[2,2,256,256]{3,2,1,0:T(8,128)(2,1)S(1)} %bitcast.97), channel_id=1, source_target_pairs={{0,3},{1,0},{2,1},{3,2},{4,7},{5,4},{6,5},{7,6},{8,11},{9,8},{10,9... | collective-permute-start | bytes 1572872 | tf_op jit(solution)/shard_map/ppermute | solution.py:38
  32.2 23.0 %collective-permute-start.16 = (bf16[2,3,256,128]{3,2,1,0:T(8,128)(2,1)S(1)}, bf16[2,3,256,128]{3,2,1,0:T(8,128)(2,1)S(1)}, u32[]{:S(2)}, u32[]{:S(2)}) collective-permute-start(bf16[2,3,256,128]{3,2,1,0:T(8,128)(2,1)S(1)} %pad_maximum_fusion.1), channel_id=1, source_target_pairs={{0,8},{1,9},{2,10},{3,11},{4,12},{5,13},{6,14},{7,15},{8,0},{9,1},... | collective-permute-start | bytes 1179656 | tf_op jit(solution)/shard_map/ppermute | solution.py:38
  36.0 20.6 %collective-permute-start.6 = (bf16[2,2,256,256]{3,2,1,0:T(8,128)(2,1)S(1)}, bf16[2,2,256,256]{3,2,1,0:T(8,128)(2,1)}, u32[]{:S(2)}, u32[]{:S(2)}) collective-permute-start(bf16[2,2,256,256]{3,2,1,0:T(8,128)(2,1)S(1)} %bitcast.98), channel_id=1, source_target_pairs={{0,8},{1,9},{2,10},{3,11},{4,12},{5,13},{6,14},{7,15},{8,0},{9,1},... | collective-permute-start | bytes 1572872 | tf_op jit(solution)/shard_map/ppermute | solution.py:38
  39.4 24.4 %copy-start.11 = (bf16[2,2,256,256]{3,2,1,0:T(8,128)(2,1)}, bf16[2,2,256,256]{3,2,1,0:T(8,128)(2,1)S(1)}, u32[]{:S(2)}) copy-start(bf16[2,2,256,256]{3,2,1,0:T(8,128)(2,1)S(1)} %collective-permute-done.3.refs_1_) | copy-start | bytes 1572868
  39.4 17.2 %collective-permute-start.7 = (bf16[2,2,256,256]{3,2,1,0:T(8,128)(2,1)S(1)}, bf16[2,2,256,256]{3,2,1,0:T(8,128)(2,1)}, u32[]{:S(2)}, u32[]{:S(2)}) collective-permute-start(bf16[2,2,256,256]{3,2,1,0:T(8,128)(2,1)S(1)} %collective-permute-done.3.refs_1_), channel_id=1, source_target_pairs={{0,8},{1,9},{2,10},{3,11},{4,12},{5,13},{6,14},{7,15},{8,0},{9,1},... | collective-permute-start | bytes 1572872 | tf_op jit(solution)/shard_map/ppermute | solution.py:38
  51.3 12.5 %copy-start.13 = (bf16[2,2,256,256]{3,2,1,0:T(8,128)(2,1)}, bf16[2,2,256,256]{3,2,1,0:T(8,128)(2,1)S(1)}, u32[]{:S(2)}) copy-start(bf16[2,2,256,256]{3,2,1,0:T(8,128)(2,1)S(1)} %collective-permute-done.4.refs_2_) | copy-start | bytes 1572868
  51.3 5.4 %collective-permute-start.8 = (bf16[2,2,256,256]{3,2,1,0:T(8,128)(2,1)S(1)}, bf16[2,2,256,256]{3,2,1,0:T(8,128)(2,1)}, u32[]{:S(2)}, u32[]{:S(2)}) collective-permute-start(bf16[2,2,256,256]{3,2,1,0:T(8,128)(2,1)S(1)} %collective-permute-done.4.refs_2_), channel_id=1, source_target_pairs={{0,8},{1,9},{2,10},{3,11},{4,12},{5,13},{6,14},{7,15},{8,0},{9,1},... | collective-permute-start | bytes 1572872 | tf_op jit(solution)/shard_map/ppermute | solution.py:38
  55.1 8.8 %copy-start.15 = (bf16[2,2,256,256]{3,2,1,0:T(8,128)(2,1)}, bf16[2,2,256,256]{3,2,1,0:T(8,128)(2,1)S(1)}, u32[]{:S(2)}) copy-start(bf16[2,2,256,256]{3,2,1,0:T(8,128)(2,1)S(1)} %collective-permute-done.5.refs_3_) | copy-start | bytes 1572868
  55.1 2.4 %collective-permute-start.9 = (bf16[2,2,256,256]{3,2,1,0:T(8,128)(2,1)S(1)}, bf16[2,2,256,256]{3,2,1,0:T(8,128)(2,1)}, u32[]{:S(2)}, u32[]{:S(2)}) collective-permute-start(bf16[2,2,256,256]{3,2,1,0:T(8,128)(2,1)S(1)} %collective-permute-done.5.refs_3_), channel_id=1, source_target_pairs={{0,8},{1,9},{2,10},{3,11},{4,12},{5,13},{6,14},{7,15},{8,0},{9,1},... | collective-permute-start | bytes 1572872 | tf_op jit(solution)/shard_map/ppermute | solution.py:38
  56.0 11.3 %collective-permute-start.17 = (bf16[2,3,256,128]{3,2,1,0:T(8,128)(2,1)}, bf16[2,3,256,128]{3,2,1,0:T(8,128)(2,1)S(1)}, u32[]{:S(2)}, u32[]{:S(2)}) collective-permute-start(bf16[2,3,256,128]{3,2,1,0:T(8,128)(2,1)} %pad_maximum_fusion.2), channel_id=1, source_target_pairs={{0,16},{1,17},{2,18},{3,19},{4,20},{5,21},{6,22},{7,23},{8,24},{9,... | collective-permute-start | bytes 1179656 | tf_op jit(solution)/shard_map/ppermute | solution.py:38
  63.8 12.5 %collective-permute-start.13 = (bf16[1024,128]{1,0:T(8,128)(2,1)S(1)}, bf16[1024,128]{1,0:T(8,128)(2,1)S(1)}, u32[]{:S(2)}, u32[]{:S(2)}) collective-permute-start(bf16[1024,128]{1,0:T(8,128)(2,1)S(1)} %get-tuple-element.56), channel_id=1, source_target_pairs={{0,20},{1,21},{2,22},{3,23},{4,16},{5,17},{6,18},{7,19},{8,28},{9,... | collective-permute-start | bytes 786440 | tf_op jit(solution)/shard_map/ppermute | solution.py:38
  66.6 9.8 %collective-permute-start.14 = (bf16[1024,128]{1,0:T(8,128)(2,1)S(1)}, bf16[1024,128]{1,0:T(8,128)(2,1)S(1)}, u32[]{:S(2)}, u32[]{:S(2)}) collective-permute-start(bf16[1024,128]{1,0:T(8,128)(2,1)S(1)} %get-tuple-element.57), channel_id=1, source_target_pairs={{0,4},{1,5},{2,6},{3,7},{4,0},{5,1},{6,2},{7,3},{8,12},{9,13},{10,... | collective-permute-start | bytes 786440 | tf_op jit(solution)/shard_map/ppermute | solution.py:38
  67.1 9.3 %collective-permute-start.15 = (bf16[1024,128]{1,0:T(8,128)(2,1)S(1)}, bf16[1024,128]{1,0:T(8,128)(2,1)S(1)}, u32[]{:S(2)}, u32[]{:S(2)}) collective-permute-start(bf16[1024,128]{1,0:T(8,128)(2,1)S(1)} %get-tuple-element.58), channel_id=1, source_target_pairs={{0,16},{1,17},{2,18},{3,19},{4,20},{5,21},{6,22},{7,23},{8,24},{9,... | collective-permute-start | bytes 786440 | tf_op jit(solution)/shard_map/ppermute | solution.py:38
  67.5 7.5 %collective-permute-start.18 = (bf16[2,256,128]{2,1,0:T(8,128)(2,1)S(1)}, bf16[2,256,128]{2,1,0:T(8,128)(2,1)S(1)}, u32[]{:S(2)}, u32[]{:S(2)}) collective-permute-start(bf16[2,256,128]{2,1,0:T(8,128)(2,1)S(1)} %get-tuple-element.108), channel_id=1, source_target_pairs={{0,32},{1,33},{2,34},{3,35},{4,36},{5,37},{6,38},{7,39},{8,40},{9,... | collective-permute-start | bytes 393224 | tf_op jit(solution)/shard_map/ppermute | solution.py:38
  68.4 28.3 %copy-start.12 = (bf16[2,2,256,256]{3,2,1,0:T(8,128)(2,1)S(1)}, bf16[2,2,256,256]{3,2,1,0:T(8,128)(2,1)}, u32[]{:S(2)}) copy-start(bf16[2,2,256,256]{3,2,1,0:T(8,128)(2,1)} %copy-done.11) | copy-start | bytes 1572868
  68.4 28.3 %copy-start.14 = (bf16[2,2,256,256]{3,2,1,0:T(8,128)(2,1)S(1)}, bf16[2,2,256,256]{3,2,1,0:T(8,128)(2,1)}, u32[]{:S(2)}) copy-start(bf16[2,2,256,256]{3,2,1,0:T(8,128)(2,1)} %copy-done.13) | copy-start | bytes 1572868
  68.4 28.3 %copy-start.16 = (bf16[2,2,256,256]{3,2,1,0:T(8,128)(2,1)S(1)}, bf16[2,2,256,256]{3,2,1,0:T(8,128)(2,1)}, u32[]{:S(2)}) copy-start(bf16[2,2,256,256]{3,2,1,0:T(8,128)(2,1)} %copy-done.15) | copy-start | bytes 1572868
  68.4 8.0 %collective-permute-start.19 = (bf16[2,256,128]{2,1,0:T(8,128)(2,1)S(1)}, bf16[2,256,128]{2,1,0:T(8,128)(2,1)S(1)}, u32[]{:S(2)}, u32[]{:S(2)}) collective-permute-start(bf16[2,256,128]{2,1,0:T(8,128)(2,1)S(1)} %get-tuple-element.107), channel_id=1, source_target_pairs={{0,32},{1,33},{2,34},{3,35},{4,36},{5,37},{6,38},{7,39},{8,40},{9,... | collective-permute-start | bytes 393224 | tf_op jit(solution)/shard_map/ppermute | solution.py:38
  81.5 21.5 %copy-start.2 = (bf16[1024,128]{1,0:T(8,128)(2,1)}, bf16[1024,128]{1,0:T(8,128)(2,1)S(1)}, u32[]{:S(2)}) copy-start(bf16[1024,128]{1,0:T(8,128)(2,1)S(1)} %get-tuple-element.73.refs_8_.refs_0_) | copy-start | bytes 786436
  81.6 15.1 %collective-permute-start.20 = (bf16[1024,128]{1,0:T(8,128)(2,1)S(1)}, bf16[1024,128]{1,0:T(8,128)(2,1)S(1)}, u32[]{:S(2)}, u32[]{:S(2)}) collective-permute-start(bf16[1024,128]{1,0:T(8,128)(2,1)S(1)} %get-tuple-element.73.refs_8_.refs_0_), channel_id=1, source_target_pairs={{0,16},{1,17},{2,18},{3,19},{4,20},{5,21},{6,22},{7,23},{8,24},{9,... | collective-permute-start | bytes 786440 | tf_op jit(solution)/shard_map/ppermute | solution.py:38
  82.1 14.5 %collective-permute-start.21 = (bf16[1024,128]{1,0:T(8,128)(2,1)S(1)}, bf16[1024,128]{1,0:T(8,128)(2,1)S(1)}, u32[]{:S(2)}, u32[]{:S(2)}) collective-permute-start(bf16[1024,128]{1,0:T(8,128)(2,1)S(1)} %get-tuple-element.73.refs_8_.refs_0_), channel_id=1, source_target_pairs={{0,4},{1,5},{2,6},{3,7},{4,0},{5,1},{6,2},{7,3},{8,12},{9,13},{10,... | collective-permute-start | bytes 786440 | tf_op jit(solution)/shard_map/ppermute | solution.py:38
  85.1 11.6 %collective-permute-start.22 = (bf16[1024,128]{1,0:T(8,128)(2,1)S(1)}, bf16[1024,128]{1,0:T(8,128)(2,1)S(1)}, u32[]{:S(2)}, u32[]{:S(2)}) collective-permute-start(bf16[1024,128]{1,0:T(8,128)(2,1)S(1)} %get-tuple-element.73.refs_8_.refs_0_), channel_id=1, source_target_pairs={{0,20},{1,21},{2,22},{3,23},{4,16},{5,17},{6,18},{7,19},{8,28},{9,... | collective-permute-start | bytes 786440 | tf_op jit(solution)/shard_map/ppermute | solution.py:38
  85.5 8.4 %collective-permute-start.23 = (bf16[2,256,128]{2,1,0:T(8,128)(2,1)S(1)}, bf16[2,256,128]{2,1,0:T(8,128)(2,1)S(1)}, u32[]{:S(2)}, u32[]{:S(2)}) collective-permute-start(bf16[2,256,128]{2,1,0:T(8,128)(2,1)S(1)} %get-tuple-element.106), channel_id=1, source_target_pairs={{0,224},{1,225},{2,226},{3,227},{4,228},{5,229},{6,230},{7,231},{8... | collective-permute-start | bytes 393224 | tf_op jit(solution)/shard_map/ppermute | solution.py:38
  92.0 4.7 %collective-permute-start.24 = (bf16[2,256,128]{2,1,0:T(8,128)(2,1)S(1)}, bf16[2,256,128]{2,1,0:T(8,128)(2,1)S(1)}, u32[]{:S(2)}, u32[]{:S(2)}) collective-permute-start(bf16[2,256,128]{2,1,0:T(8,128)(2,1)S(1)} %get-tuple-element.105), channel_id=1, source_target_pairs={{0,224},{1,225},{2,226},{3,227},{4,228},{5,229},{6,230},{7,231},{8... | collective-permute-start | bytes 393224 | tf_op jit(solution)/shard_map/ppermute | solution.py:38
  93.9 10.6 %copy-start.21 = (bf16[2,256,128]{2,1,0:T(8,128)(2,1)}, bf16[2,256,128]{2,1,0:T(8,128)(2,1)S(1)}, u32[]{:S(2)}) copy-start(bf16[2,256,128]{2,1,0:T(8,128)(2,1)S(1)} %collective-permute-done.23) | copy-start | bytes 393220
  104.5 8.0 %collective-permute-start.27 = (bf16[8,2,256,256]{3,2,1,0:T(8,128)(2,1)}, bf16[8,2,256,256]{3,2,1,0:T(8,128)(2,1)}, u32[]{:S(2)}, u32[]{:S(2)}) collective-permute-start(bf16[8,2,256,256]{3,2,1,0:T(8,128)(2,1)} %copy-done.10), channel_id=1, source_target_pairs={{0,8},{1,9},{2,10},{3,11},{4,12},{5,13},{6,14},{7,15},{8,0},{9,1},... | collective-permute-start | bytes 6291464 | tf_op jit(solution)/shard_map/ppermute | solution.py:38
  115.6 17.2 %collective-permute-start.30 = (bf16[2,2,256,256]{3,2,1,0:T(8,128)(2,1)S(1)}, bf16[2,2,256,256]{3,2,1,0:T(8,128)(2,1)S(1)}, u32[]{:S(2)}, u32[]{:S(2)}) collective-permute-start(bf16[2,2,256,256]{3,2,1,0:T(8,128)(2,1)S(1)} %get-tuple-element.81), channel_id=1, source_target_pairs={{0,1},{1,2},{2,3},{3,0},{4,5},{5,6},{6,7},{7,4},{8,9},{9,10},{10,1... | collective-permute-start | bytes 1572872 | tf_op jit(solution)/shard_map/ppermute | solution.py:38
  117.0 25.0 %collective-permute-start.29 = (bf16[2,2,256,256]{3,2,1,0:T(8,128)(2,1)S(1)}, bf16[2,2,256,256]{3,2,1,0:T(8,128)(2,1)S(1)}, u32[]{:S(2)}, u32[]{:S(2)}) collective-permute-start(bf16[2,2,256,256]{3,2,1,0:T(8,128)(2,1)S(1)} %get-tuple-element.80), channel_id=1, source_target_pairs={{0,2},{1,3},{2,0},{3,1},{4,6},{5,7},{6,4},{7,5},{8,10},{9,11},{10,... | collective-permute-start | bytes 1572872 | tf_op jit(solution)/shard_map/ppermute | solution.py:38
  119.1 22.9 %collective-permute-start.28 = (bf16[2,2,256,256]{3,2,1,0:T(8,128)(2,1)S(1)}, bf16[2,2,256,256]{3,2,1,0:T(8,128)(2,1)S(1)}, u32[]{:S(2)}, u32[]{:S(2)}) collective-permute-start(bf16[2,2,256,256]{3,2,1,0:T(8,128)(2,1)S(1)} %get-tuple-element.79), channel_id=1, source_target_pairs={{0,3},{1,0},{2,1},{3,2},{4,7},{5,4},{6,5},{7,6},{8,11},{9,8},{10,9... | collective-permute-start | bytes 1572872 | tf_op jit(solution)/shard_map/ppermute | solution.py:38
  120.4 9.6 %collective-permute-start.25 = (bf16[2,3,256,128]{3,2,1,0:T(8,128)(2,1)S(1)}, bf16[2,3,256,128]{3,2,1,0:T(8,128)(2,1)S(1)}, u32[]{:S(2)}, u32[]{:S(2)}) collective-permute-start(bf16[2,3,256,128]{3,2,1,0:T(8,128)(2,1)S(1)} %pad_maximum_fusion.3), channel_id=1, source_target_pairs={{0,16},{1,17},{2,18},{3,19},{4,20},{5,21},{6,22},{7,23},{8,24},{9,... | collective-permute-start | bytes 1179656 | tf_op jit(solution)/shard_map/ppermute | solution.py:38
  130.8 20.8 %collective-permute-start.26 = (bf16[2,3,256,128]{3,2,1,0:T(8,128)(2,1)}, bf16[2,3,256,128]{3,2,1,0:T(8,128)(2,1)S(1)}, u32[]{:S(2)}, u32[]{:S(2)}) collective-permute-start(bf16[2,3,256,128]{3,2,1,0:T(8,128)(2,1)} %pad_maximum_fusion.4), channel_id=1, source_target_pairs={{0,8},{1,9},{2,10},{3,11},{4,12},{5,13},{6,14},{7,15},{8,0},{9,1},... | collective-permute-start | bytes 1179656 | tf_op jit(solution)/shard_map/ppermute | solution.py:38
  142.3 12.2 %collective-permute-start.31 = (bf16[256,256]{1,0:T(8,128)(2,1)S(1)}, bf16[256,256]{1,0:T(8,128)(2,1)S(1)}, u32[]{:S(2)}, u32[]{:S(2)}) collective-permute-start(bf16[256,256]{1,0:T(8,128)(2,1)S(1)} %get-tuple-element.93), channel_id=1, source_target_pairs={{0,16},{1,17},{2,18},{3,19},{4,20},{5,21},{6,22},{7,23},{8,24},{9,... | collective-permute-start | bytes 393224 | tf_op jit(solution)/shard_map/ppermute | solution.py:38
  142.4 14.0 %collective-permute-start.32 = (bf16[256,256]{1,0:T(8,128)(2,1)S(1)}, bf16[256,256]{1,0:T(8,128)(2,1)S(1)}, u32[]{:S(2)}, u32[]{:S(2)}) collective-permute-start(bf16[256,256]{1,0:T(8,128)(2,1)S(1)} %get-tuple-element.92), channel_id=1, source_target_pairs={{0,4},{1,5},{2,6},{3,7},{4,0},{5,1},{6,2},{7,3},{8,12},{9,13},{10,... | collective-permute-start | bytes 393224 | tf_op jit(solution)/shard_map/ppermute | solution.py:38
  145.4 11.1 %collective-permute-start.33 = (bf16[256,256]{1,0:T(8,128)(2,1)S(1)}, bf16[256,256]{1,0:T(8,128)(2,1)S(1)}, u32[]{:S(2)}, u32[]{:S(2)}) collective-permute-start(bf16[256,256]{1,0:T(8,128)(2,1)S(1)} %get-tuple-element.91), channel_id=1, source_target_pairs={{0,20},{1,21},{2,22},{3,23},{4,16},{5,17},{6,18},{7,19},{8,28},{9,... | collective-permute-start | bytes 393224 | tf_op jit(solution)/shard_map/ppermute | solution.py:38
  147.2 9.2 %collective-permute-start.34 = (bf16[128,256]{1,0:T(8,128)(2,1)S(1)}, bf16[128,256]{1,0:T(8,128)(2,1)S(1)}, u32[]{:S(2)}, u32[]{:S(2)}) collective-permute-start(bf16[128,256]{1,0:T(8,128)(2,1)S(1)} %get-tuple-element.98), channel_id=1, source_target_pairs={{0,8},{1,9},{2,10},{3,11},{4,12},{5,13},{6,14},{7,15},{8,0},{9,1},... | collective-permute-start | bytes 196616 | tf_op jit(solution)/shard_map/ppermute | solution.py:38
  151.6 5.2 %collective-permute-start.35 = (bf16[128,256]{1,0:T(8,128)(2,1)S(1)}, bf16[128,256]{1,0:T(8,128)(2,1)S(1)}, u32[]{:S(2)}, u32[]{:S(2)}) collective-permute-start(bf16[128,256]{1,0:T(8,128)(2,1)S(1)} %get-tuple-element.100), channel_id=1, source_target_pairs={{0,4},{1,5},{2,6},{3,7},{4,0},{5,1},{6,2},{7,3},{8,12},{9,13},{10,... | collective-permute-start | bytes 196616 | tf_op jit(solution)/shard_map/ppermute | solution.py:38
  154.5 5.6 %collective-permute-start.36 = (bf16[128,256]{1,0:T(8,128)(2,1)S(1)}, bf16[128,256]{1,0:T(8,128)(2,1)S(1)}, u32[]{:S(2)}, u32[]{:S(2)}) collective-permute-start(bf16[128,256]{1,0:T(8,128)(2,1)S(1)} %get-tuple-element.97), channel_id=1, source_target_pairs={{0,12},{1,13},{2,14},{3,15},{4,8},{5,9},{6,10},{7,11},{8,4},{9,5},... | collective-permute-start | bytes 196616 | tf_op jit(solution)/shard_map/ppermute | solution.py:38
  (14 other events, 66.9 us)
Sparse Core Ops, SparseCore 0:
  18.9 39.3 all-gather.2
  104.6 41.1 reduce-scatter.1
